TPU v7x, 32 devices: a whole 2x2x4 slice. The times are simulated.
32 devices in a mesh: pool: 8 (over z, x), blk: 4 (over y, core).
Axes of the slice: x: 2, y: 2, z: 4, core: 2. Of those that a mesh axis runs over, the one named last changes fastest.
Arguments:
- queries: bfloat16 [4096, 4096], P(('pool', 'blk')), may hold values from -26 to 26
- suffix_kv: bfloat16 [4096, 1024], P(('pool', 'blk')), may hold values from -5 to 5
- cache: bfloat16 [128, 128, 1024], P('pool'), may hold values from -6 to 6
- cache_scale: bfloat16 [128, 8], P('pool'), may hold values from 0.5 to 2
- prefix_len: int32 [8], replicated, may hold values from 1 to 2048, as said below
- suffix_len: int32 [8], replicated, may hold values from 256 to 512, as said below
- block_table: int32 [8, 16], replicated, may hold values from 0 to 127, as said below
- session_group: int32 [8], replicated, may hold values from 0 to 7, each once
Outputs:
- attention_out: bfloat16 [4096, 4096], P(('pool', 'blk'))
Inputs may be any that keep to these rules, and one draw needn't show every extreme that they name: `prefix_len`: one session's prefix is exactly 2048 tokens long. `suffix_len`: one session has exactly 512 live suffix tokens. `block_table`: entry [s, j] = h * 16 + r names slot r of holder h (the rows h * 16 to h * 16 + 15 of cache); every storage slot is named exactly once; within each aligned run of 8 blocks of a session (blocks c * 8 to c * 8 + 7) every holder appears once, so a holder holds exactly 2 of each session's table entries. Entries past a session's length are named but hold no live tokens.
All inputs are finite; a program needn't handle non-finite values.
Results may differ from a plain program's by a relative error of at most 0.0026.
Values may be sent and summed in bfloat16 or wider, within the bound.
No kernel may reach another device: no remote copies, remote signals or barrier semaphores. Data moves between devices by JAX's collectives and lax.ppermute only.
A program may use at most 128 MiB of HBM per device.

v0:
```python
import math

import jax
import jax.numpy as jnp
from jax import lax
from jax.sharding import PartitionSpec as P

QH = 32
KVH = 4
HD = 128


masked_score = -1e30


def fold_keys(running, query_heads, key_rows, value_rows, key_scale, value_scale, usable):
    highest, weight_sum, weighted = running
    scores = jnp.einsum("kgrd,nkd->kgrn", query_heads, key_rows, preferred_element_type=jnp.float32)
    scores = scores * jnp.transpose(key_scale)[:, None, None, :]
    scores = jnp.where(usable[None, None], scores, masked_score)
    new_highest = jnp.maximum(highest, jnp.max(scores, axis=3))
    weights = jnp.where(usable[None, None], jnp.exp(scores - new_highest[..., None]), 0.0)
    factor = jnp.exp(highest - new_highest)
    weight_sum = weight_sum * factor + jnp.sum(weights, axis=3)
    rounded = (weights * jnp.transpose(value_scale)[:, None, None, :]).astype(jnp.bfloat16)
    weighted = weighted * factor[..., None] + jnp.einsum(
        "kgrn,nkd->kgrd", rounded, value_rows, preferred_element_type=jnp.float32
    )
    return (new_highest, weight_sum, weighted)


def per_device(
    queries, suffix_kv, cache, cache_scale, prefix_len, suffix_len, block_table, session_group
):
    local_rows = queries.shape[0]
    kv_heads = KVH
    per_group = QH // KVH
    head_size = HD
    pool_count = lax.axis_size("pool")
    member_count = lax.axis_size("blk")
    pool_index = lax.axis_index("pool")
    member_index = lax.axis_index("blk")
    slot_count = cache.shape[0]
    block_size = cache.shape[1]
    session_count = block_table.shape[0]
    block_count = block_table.shape[1]
    run_count = block_count // pool_count
    inv_root = 1.0 / math.sqrt(head_size)
    chooser = (
        session_group[:, None] == jnp.arange(session_count, dtype=jnp.int32)[None, :]
    ).astype(jnp.int32)
    tables = jnp.sum(chooser[:, :, None] * block_table[None], axis=1)
    holders = (tables // slot_count).reshape(pool_count, run_count, pool_count)
    places = (tables % slot_count).reshape(pool_count, run_count, pool_count)
    send_slots = jnp.sum(jnp.where(holders == pool_index, places, 0), axis=2)
    own_choice = lax.dynamic_index_in_dim(chooser, pool_index, 0, keepdims=False)
    prefix_length = jnp.sum(own_choice * prefix_len)
    suffix_length = jnp.sum(own_choice * suffix_len)
    own_holders = lax.dynamic_index_in_dim(holders, pool_index, 0, keepdims=False)
    positions = jnp.arange(block_count, dtype=jnp.int32).reshape(run_count, pool_count)
    matches = own_holders[None, :, :] == jnp.arange(pool_count, dtype=jnp.int32)[:, None, None]
    block_place = jnp.sum(jnp.where(matches, positions[None], 0), axis=2)
    scale_rows = cache_scale[send_slots]
    split_cache = cache.reshape(slot_count, block_size, 2 * kv_heads, head_size)
    share_size = 2 * kv_heads // member_count
    outgoing = lax.dynamic_slice_in_dim(
        split_cache[send_slots], member_index * share_size, share_size, 3
    )
    arrived_part, arrived_scale = (
        lax.all_to_all(outgoing, "pool", split_axis=0, concat_axis=0, tiled=True),
        lax.all_to_all(scale_rows, "pool", split_axis=0, concat_axis=0, tiled=True),
    )
    arrived = lax.all_gather(arrived_part, "blk", axis=3, tiled=True)
    prefix_tokens = pool_count * run_count * block_size
    step_tokens = min(1024, prefix_tokens)
    step_count = prefix_tokens // step_tokens
    prefix_stack = arrived.reshape(step_count, step_tokens, 2, kv_heads, head_size)
    token_scale = jnp.broadcast_to(
        arrived_scale.astype(jnp.float32).reshape(pool_count, run_count, 1, 2, kv_heads),
        (pool_count, run_count, block_size, 2, kv_heads),
    ).reshape(step_count, step_tokens, 2, kv_heads)
    token_place = (
        block_place[:, :, None] * block_size
        + jnp.arange(block_size, dtype=jnp.int32)[None, None, :]
    ).reshape(step_count, step_tokens)
    query_heads = jnp.transpose(
        queries.reshape(local_rows, kv_heads, per_group, head_size), (1, 2, 0, 3)
    )
    row_place = member_index * local_rows + jnp.arange(local_rows, dtype=jnp.int32)
    initial = (
        jnp.full((kv_heads, per_group, local_rows), masked_score, jnp.float32),
        jnp.zeros((kv_heads, per_group, local_rows), jnp.float32),
        jnp.zeros((kv_heads, per_group, local_rows, head_size), jnp.float32),
    )
    shard_rows = lax.all_gather(suffix_kv, "blk", axis=0, tiled=True)
    piece_count = shard_rows.shape[0]
    split_rows = shard_rows.reshape(piece_count, 2, kv_heads, head_size)
    key_place = jnp.arange(piece_count, dtype=jnp.int32)
    usable = (key_place[None, :] <= row_place[:, None]) & (key_place[None, :] < suffix_length)
    flat_scale = jnp.full((piece_count, kv_heads), inv_root, jnp.float32)
    unit_scale = jnp.ones((piece_count, kv_heads), jnp.float32)
    running = fold_keys(
        initial, query_heads, split_rows[:, 0], split_rows[:, 1], flat_scale, unit_scale, usable
    )

    def prefix_step(running, step_inputs):
        token_rows, scale_step, place_rows = step_inputs
        usable = (place_rows < prefix_length)[None, :]
        updated = fold_keys(
            running,
            query_heads,
            token_rows[:, 0],
            token_rows[:, 1],
            scale_step[:, 0] * inv_root,
            scale_step[:, 1],
            usable,
        )
        return (updated, None)

    running, unused = lax.scan(prefix_step, running, (prefix_stack, token_scale, token_place))
    highest, weight_sum, weighted = running
    result = weighted / weight_sum[..., None]
    result = jnp.transpose(result, (2, 0, 1, 3)).reshape(local_rows, QH * head_size)
    result = jnp.where((row_place < suffix_length)[:, None], result, 0.0)
    return result.astype(jnp.bfloat16)


def solution(mesh):
    return jax.shard_map(
        per_device,
        mesh=mesh,
        in_specs=(
            P(("pool", "blk"), None),
            P(("pool", "blk"), None),
            P("pool", None, None),
            P("pool", None),
            P(),
            P(),
            P(),
            P(),
        ),
        out_specs=P(("pool", "blk"), None),
        check_vma=False,
    )
```

profile of v0, /device:TPU:9, one launch (start us, length us, event | category | flops | bytes accessed | tf_op | source)
XLA Modules:
  0.0 141.8 jit_solution(5961451731290356385)
XLA Ops:
  8.6 5.2 %copy.125 = bf16[256,8,8,128]{3,2,1,0:T(8,128)(2,1)} copy(bf16[256,8,8,128]{3,1,2,0:T(8,128)(2,1)} %bitcast.119) | data formatting | bytes 8388608
  13.8 5.3 %gather_fusion = bf16[16,128,8,128]{3,2,1,0:T(8,128)(2,1)} fusion(bf16[16,128,8,128]{3,2,1,0:T(8,128)(2,1)} %bitcast.114, s32[1024]{0:T(1024)S(1)} %pad_clamp_fusion), kind=kCustom, calls=%fused_computation | custom fusion | bytes 8388672 | tf_op jit(solution)/shard_map/gather | solution.py:67
  19.2 3.4 %constant_dynamic-slice_fusion.1 = bf16[8,2,128,2,128]{4,3,2,1,0:T(2,128)(2,1)S(1)} fusion(bf16[8,2,128,8,128]{4,3,2,1,0:T(8,128)(2,1)} %bitcast.117, s32[]{:T(128)S(6)} %select_n.71), kind=kLoop, calls=%fused_computation.67 | loop fusion | bytes 2097156 | tf_op jit(solution)/shard_map/dynamic_slice | solution.py:66
  22.6 1.2 copy.124
  23.8 5.7 %all-to-all-start = ((bf16[8,2,128,2,128]{4,2,1,3,0:T(8,128)(2,1)}), bf16[8,2,128,2,128]{4,2,1,3,0:T(8,128)(2,1)S(1)}, u32[]{:S(2)}, u32[]{:S(2)}) async-start(bf16[8,2,128,2,128]{4,2,1,3,0:T(8,128)(2,1)} %copy.124), calls=%async_computation | async-start | bytes 2097152 | tf_op jit(solution)/shard_map/all_to_all | solution.py:70
  30.5 22.0 %all-to-all-done = bf16[8,2,128,2,128]{4,2,1,3,0:T(8,128)(2,1)S(1)} async-done(((bf16[8,2,128,2,128]{4,2,1,3,0:T(8,128)(2,1)}), bf16[8,2,128,2,128]{4,2,1,3,0:T(8,128)(2,1)S(1)}, u32[]{:S(2)}, u32[]{:S(2)}) %all-to-all-start) | async-done | bytes 1048608 | tf_op jit(solution)/shard_map/all_to_all | solution.py:70
  53.6 1.2 gather_fusion.1
  54.8 6.6 %all-to-all-start.1 = ((bf16[8,2,8]{2,1,0:T(2,128)(2,1)}), bf16[8,2,8]{2,1,0:T(2,128)(2,1)S(1)}, u32[]{:S(2)}, u32[]{:S(2)}) async-start(bf16[8,2,8]{2,1,0:T(2,128)(2,1)} %bitcast.28), calls=%async_computation.1 | async-start | bytes 8192 | tf_op jit(solution)/shard_map/all_to_all | solution.py:71
  63.3 1.2 broadcast_compare_fusion.2
  66.3 2.9 %fusion.10 = (f32[4,8,128]{2,1,0:T(8,128)S(1)}, f32[4,8,128,512]{3,2,1,0:T(8,128)S(1)}) fusion(pred[128,512]{1,0:T(8,128)(4,1)S(1)} %fusion.21, bf16[4,8,128,128]{2,3,1,0:T(8,128)(2,1)S(1)} %bitcast.116, bf16[512,2,4,128]{0,3,2,1:T(8,128)(2,1)} %bitcast.121), kind=kOutput, calls=%fused_computation.29 | convolution fusion | flops 543158272 | bytes 10043392 | tf_op jit(solution)/shard_map/kgrd,nkd->kgrn/dot_general | solution.py:18
  69.2 2.6 %fusion.12 = f32[4,8,128]{2,1,0:T(8,128)S(1)} fusion(f32[4,8,128,512]{3,2,1,0:T(8,128)S(1)} %get-tuple-element.140, f32[4,8,128]{2,1,0:T(8,128)S(1)} %broadcast_maximum_fusion, pred[128,512]{1,0:T(8,128)(4,1)S(1)} %fusion.21), kind=kLoop, calls=%fused_computation.31 | loop fusion | flops 10481664 | bytes 8486912 | tf_op jit(solution)/shard_map/reduce_sum | solution.py:24
  71.8 3.9 %fusion.17 = f32[4,8,128,128]{3,2,1,0:T(8,128)} fusion(f32[4,8,128,512]{3,2,1,0:T(8,128)S(1)} %get-tuple-element.140, f32[4,8,128]{2,1,0:T(8,128)S(1)} %broadcast_maximum_fusion, pred[128,512]{1,0:T(8,128)(4,1)S(1)} %fusion.21, f32[4,8,128]{2,1,0:T(8,128)S(1)} %get-tuple-element.137, bf16[512,2,4,128]{0,3,2,1:T(8,128)(2,1)S(1)} %bitcast.122), kind=kOutput, calls=%fused_computation.37 | convolution fusion | flops 547880960 | bytes 11108352 | tf_op jit(solution)/shard_map/kgrn,nkd->kgrd/dot_general | solution.py:26
  75.7 14.8 %all-gather.5.cloned.1.call-done = bf16[8,2,128,8,128]{4,2,1,0,3:T(8,128)(2,1)} async-done(((bf16[8,2,128,2,128]{4,2,1,0,3:T(8,128)(2,1)}), bf16[8,2,128,8,128]{4,2,1,0,3:T(8,128)(2,1)}) %all-gather.5.cloned.1.call-update) | async-done | bytes 4194320 | tf_op jit(solution)/shard_map/all_gather | solution.py:73
  90.5 40.4 %while.14 = (s32[]{:T(128)}, f32[4,8,128]{2,1,0:T(8,128)S(1)}, f32[4,8,128]{2,1,0:T(8,128)S(1)}, f32[4,8,128,128]{3,2,1,0:T(8,128)}, s32[2,1024]{1,0:T(2,128)S(1...) while((s32[]{:T(128)}, f32[4,8,128]{2,1,0:T(8,128)S(1)}, ...), condition=%wide.region_10.11_spmd, body=%wide.region_7.10_spmd.sunk | while | flops 2207265792 | bytes 62399612 | solution.py:120
  91.2 1.7 %dynamic-slice_bitcast_fusion.3 = bf16[1024,2,4,128]{3,0,2,1:T(8,128)(2,1)S(1)} fusion(bf16[2,1024,2,4,128]{4,1,0,3,2:T(8,128)(2,1)} %get-tuple-element.234, s32[]{:T(128)S(6)} %copy.137), kind=kLoop, calls=%fused_computation.13.clone.1 | loop fusion | bytes 4194308 | tf_op jit(solution)/shard_map/while/body/jit(dynamic_index_in_dim)/squeeze | solution.py:120
  93.0 2.4 %bitcast_reduce_fusion.2 = (f32[4,8,128]{2,1,0:T(8,128)S(1)}, f32[4,1024,8,128]{3,1,2,0:T(8,128)S(1)}) fusion(f32[4,1024]{1,0:T(4,128)S(1)} %get-tuple-element.202, pred[1024]{0:T(1024)(128)(4,1)S(1)} %compare_reduce_fusion.2, bf16[4,8,128,128]{3,2,1,0:T(8,128)(2,1)S(1)} %get-tuple-element.235, ...), kind=kOutput, calls=%fused_computation.3.clone.1 | convolution fusion | flops 1086320640 | bytes 18908160 | tf_op jit(solution)/shard_map/while/body/eval_jaxpr/kgrd,nkd->kgrn/dot_general | solution.py:18
  95.4 5.2 %fusion.35 = f32[4,8,128]{2,1,0:T(8,128)S(1)} fusion(f32[4,1024,8,128]{3,1,2,0:T(8,128)S(1)} %get-tuple-element.204, f32[4,8,128]{2,1,0:T(8,128)S(1)} %max.4, f32[4,1024]{1,0:T(4,128)S(1)} %get-tuple-element.202, pred[1024]{0:T(1024)(128)(4,1)S(1)} %compare_reduce_fusion.2), kind=kLoop, calls=%fused_computation.8.clone.1 | loop fusion | flops 20967424 | bytes 16827392 | tf_op jit(solution)/shard_map/while/body/eval_jaxpr/reduce_sum | solution.py:24
  100.6 10.1 %multiply_add_fusion.6 = f32[4,8,128,128]{3,2,1,0:T(8,128)} fusion(f32[4,8,128,128]{3,2,1,0:T(8,128)} %get-tuple-element.221, f32[4,1024,8,128]{3,1,2,0:T(8,128)S(1)} %get-tuple-element.204, f32[4,1024]{1,0:T(4,128)S(1)} %get-tuple-element.206, f32[4,8,128]{2,1,0:T(8,128)S(1)} %max.4, f32[4,1024]{1,0:T(4,128)S(1)} %get-tuple-element.202, ...), kind=kOutput, calls=%fused_computation.12.clone.1 | convolution fusion | flops 1099956224 | bytes 22087680 | tf_op jit(solution)/shard_map/while/body/eval_jaxpr/kgrn,nkd->kgrd/dot_general | solution.py:26
  111.4 1.7 %dynamic-slice_bitcast_fusion.3 = bf16[1024,2,4,128]{3,0,2,1:T(8,128)(2,1)S(1)} fusion(bf16[2,1024,2,4,128]{4,1,0,3,2:T(8,128)(2,1)} %get-tuple-element.234, s32[]{:T(128)S(6)} %copy.137), kind=kLoop, calls=%fused_computation.13.clone.1 | loop fusion | bytes 4194308 | tf_op jit(solution)/shard_map/while/body/jit(dynamic_index_in_dim)/squeeze | solution.py:120
  113.2 2.4 %bitcast_reduce_fusion.2 = (f32[4,8,128]{2,1,0:T(8,128)S(1)}, f32[4,1024,8,128]{3,1,2,0:T(8,128)S(1)}) fusion(f32[4,1024]{1,0:T(4,128)S(1)} %get-tuple-element.202, pred[1024]{0:T(1024)(128)(4,1)S(1)} %compare_reduce_fusion.2, bf16[4,8,128,128]{3,2,1,0:T(8,128)(2,1)S(1)} %get-tuple-element.235, ...), kind=kOutput, calls=%fused_computation.3.clone.1 | convolution fusion | flops 1086320640 | bytes 18908160 | tf_op jit(solution)/shard_map/while/body/eval_jaxpr/kgrd,nkd->kgrn/dot_general | solution.py:18
  115.6 5.2 %fusion.35 = f32[4,8,128]{2,1,0:T(8,128)S(1)} fusion(f32[4,1024,8,128]{3,1,2,0:T(8,128)S(1)} %get-tuple-element.204, f32[4,8,128]{2,1,0:T(8,128)S(1)} %max.4, f32[4,1024]{1,0:T(4,128)S(1)} %get-tuple-element.202, pred[1024]{0:T(1024)(128)(4,1)S(1)} %compare_reduce_fusion.2), kind=kLoop, calls=%fused_computation.8.clone.1 | loop fusion | flops 20967424 | bytes 16827392 | tf_op jit(solution)/shard_map/while/body/eval_jaxpr/reduce_sum | solution.py:24
  120.8 10.1 %multiply_add_fusion.6 = f32[4,8,128,128]{3,2,1,0:T(8,128)} fusion(f32[4,8,128,128]{3,2,1,0:T(8,128)} %get-tuple-element.221, f32[4,1024,8,128]{3,1,2,0:T(8,128)S(1)} %get-tuple-element.204, f32[4,1024]{1,0:T(4,128)S(1)} %get-tuple-element.206, f32[4,8,128]{2,1,0:T(8,128)S(1)} %max.4, f32[4,1024]{1,0:T(4,128)S(1)} %get-tuple-element.202, ...), kind=kOutput, calls=%fused_computation.12.clone.1 | convolution fusion | flops 1099956224 | bytes 22087680 | tf_op jit(solution)/shard_map/while/body/eval_jaxpr/kgrn,nkd->kgrd/dot_general | solution.py:26
  130.8 1.9 %divide_bitcast_fusion = bf16[128,4,8,128]{3,0,2,1:T(8,128)(2,1)S(1)} fusion(f32[4,8,128,128]{3,2,1,0:T(8,128)} %get-tuple-element.53, f32[4,8,128]{2,1,0:T(8,128)S(1)} %get-tuple-element.54), kind=kLoop, calls=%fused_computation.36 | loop fusion | flops 1048576 | bytes 3162112 | tf_op jit(solution)/shard_map/transpose | solution.py:123
  133.5 1.5 %fusion.16 = bf16[128,4096]{1,0:T(8,128)(2,1)} fusion(bf16[16,8,32,128]{3,2,1,0:T(8,128)(2,1)S(1)} %bitcast.118, pred[128]{0:T(512)(128)(4,1)S(1)} %copy-done.4), kind=kLoop, calls=%fused_computation.35 | loop fusion | flops 524288 | bytes 2097280 | tf_op jit(solution)/shard_map/convert_element_type | solution.py:125
  (66 shorter events, 9.9 us)
Async XLA Ops:
  13.8 15.7 %copy-start.2 = (bf16[128,1024]{1,0:T(8,128)(2,1)S(1)}, bf16[128,1024]{1,0:T(8,128)(2,1)}, u32[]{:S(2)}) copy-start(bf16[128,1024]{1,0:T(8,128)(2,1)} %param.11) | copy-start | bytes 786436
  13.8 39.7 %copy-start.3 = (bf16[16,8]{0,1:T(8,128)(2,1)S(1)}, bf16[16,8]{0,1:T(8,128)(2,1)}, u32[]{:S(2)}) copy-start(bf16[16,8]{0,1:T(8,128)(2,1)} %param.13) | copy-start | bytes 772
  13.8 47.6 %copy-start.5 = (s32[8]{0:T(128)S(1)}, s32[8]{0:T(128)}, u32[]{:S(2)}) copy-start(s32[8]{0:T(128)} %param.14) | copy-start | bytes 100
  13.8 47.6 %copy-start.6 = (s32[8]{0:T(128)S(1)}, s32[8]{0:T(128)}, u32[]{:S(2)}) copy-start(s32[8]{0:T(128)} %param.15) | copy-start | bytes 100
  13.8 50.7 %copy-start = (bf16[128,4096]{1,0:T(8,128)(2,1)S(1)}, bf16[128,4096]{1,0:T(8,128)(2,1)}, u32[]{:S(2)}) copy-start(bf16[128,4096]{1,0:T(8,128)(2,1)} %param.10) | copy-start | bytes 3145732
  23.8 28.6 %all-to-all-start = ((bf16[8,2,128,2,128]{4,2,1,3,0:T(8,128)(2,1)}), bf16[8,2,128,2,128]{4,2,1,3,0:T(8,128)(2,1)S(1)}, u32[]{:S(2)}, u32[]{:S(2)}) async-start(bf16[8,2,128,2,128]{4,2,1,3,0:T(8,128)(2,1)} %copy.124), calls=%async_computation | async-start | bytes 2097152 | tf_op jit(solution)/shard_map/all_to_all | solution.py:70
  29.5 36.8 %all-gather.3.cloned.1.call-start = ((), (), s32[]{:S(2)}) async-start(), calls=%async_computation.2 | async-start | bytes 1310720 | tf_op jit(solution)/shard_map/all_gather | solution.py:95
  30.4 60.1 %all-gather.5.cloned.1.call-start = ((), (), s32[]{:S(2)}) async-start(), calls=%async_computation.3 | async-start | bytes 5242880 | tf_op jit(solution)/shard_map/all_gather | solution.py:73
  54.8 11.1 %all-to-all-start.1 = ((bf16[8,2,8]{2,1,0:T(2,128)(2,1)}), bf16[8,2,8]{2,1,0:T(2,128)(2,1)S(1)}, u32[]{:S(2)}, u32[]{:S(2)}) async-start(bf16[8,2,8]{2,1,0:T(2,128)(2,1)} %bitcast.28), calls=%async_computation.1 | async-start | bytes 8192 | tf_op jit(solution)/shard_map/all_to_all | solution.py:71
  66.3 5.5 %copy-start.1 = (bf16[512,1024]{0,1:T(8,128)(2,1)S(1)}, bf16[512,1024]{0,1:T(8,128)(2,1)}, u32[]{:S(2)}) copy-start(bf16[512,1024]{0,1:T(8,128)(2,1)} %all-gather.3.cloned.1.call-done) | copy-start | bytes 3145732
  90.5 43.0 %copy-start.4 = (pred[128]{0:T(512)(128)(4,1)S(1)}, pred[128]{0:T(512)(128)(4,1)}, u32[]{:S(2)}) copy-start(pred[128]{0:T(512)(128)(4,1)} %broadcast_compare_fusion.2) | copy-start | bytes 388
Sparse Core Ops, SparseCore 0:
  31.9 18.7 all-gather.2
  53.6 36.8 all-gather.4
where the time goes:
time: 143 us; the launch traced here: 142 us
  waiting for transfers between devices  36.8 us (26%)
  matrix products  31.7 us (22%)
  local copies, waits for them, and re-layouts  24.7 us (17%)
  other arithmetic  22.5 us (16%)
  between operations  13.6 us (10%)
  starting transfers between devices  12.4 us (9%)
    dot_general x3, matrix products, fold_keys(): jnp.einsum('kgrn,nkd->kgrd', rounded, value_rows, preferred_element_type=...  24 us
    all_to_all x1, waiting for transfers between devices, per_device(): lax.all_to_all(outgoing, 'pool', split_axis=0, concat_axis=0, tiled=True)  22 us
    all_gather x1, waiting for transfers between devices, per_device(): arrived = lax.all_gather(arrived_part, 'blk', axis=3, tiled=True)  14.8 us
    reduce_sum x3, other arithmetic, fold_keys(): weight_sum = weight_sum * factor + jnp.sum(weights, axis=3)  13 us
    unnamed x19, local copies, waits for them, and re-layouts  8.05 us
    dot_general x3, matrix products, fold_keys(): jnp.einsum('kgrd,nkd->kgrn', query_heads, key_rows, preferred_element_typ...  7.64 us
    all_to_all x1, starting transfers between devices, per_device(): lax.all_to_all(scale_rows, 'pool', split_axis=0, concat_axis=0, tiled=True)  6.63 us
    all_to_all x1, starting transfers between devices, per_device(): lax.all_to_all(outgoing, 'pool', split_axis=0, concat_axis=0, tiled=True)  5.69 us
  transfers between devices with their start and end apart: 4, of which 2 were waited for; matrix products, arithmetic and copies ran while one was open for 12% of the time, Pallas kernels for 0%

commit v1 on v0

--- a/solution.py
+++ b/solution.py
@@ -1,16 +1,617 @@
+import functools
 import math
 
 import jax
 import jax.numpy as jnp
 from jax import lax
+from jax.experimental import pallas as pl
+from jax.experimental.pallas import tpu as pltpu
 from jax.sharding import PartitionSpec as P
 
 QH = 32
 KVH = 4
 HD = 128
-
+PER = QH // KVH
+LOG2E = math.log2(math.e)
+INV_ROOT = 1.0 / math.sqrt(HD)
 
 masked_score = -1e30
+
+RUNS = 2
+BLK = 128
+PAIR = RUNS * BLK
+PIECE = 2 * PAIR + 16
+ROWS = 128
+WIDE = PER * ROWS
+BOTH = 2 * WIDE
+REF_ROW = HD
+SUM_ROW = HD + 8
+STATE = HD + 16
+POOL = 8
+META_J = 0
+META_LEN = 2 * POOL
+META_SUF = META_LEN + 1
+META_M = META_LEN + 2
+META_SEND = 24
+META_SIZE = META_SEND + 2 * POOL
+TILE = 512
+NT = (((1,), (1,)), ((), ()))
+VMEM_LIMIT = 24 << 20
+BF16 = jnp.bfloat16
+F32 = jnp.float32
+IN_VMEM = pl.BlockSpec(memory_space=pltpu.VMEM)
+IN_SMEM = pl.BlockSpec(memory_space=pltpu.SMEM)
+IN_HBM = pl.BlockSpec(memory_space=pltpu.HBM)
+
+
+COST = pl.CostEstimate(flops=1 << 10, bytes_accessed=1 << 10, transcendentals=0)
+
+
+def write_scales(scales, locals_, head, dst):
+    col_at = lax.broadcasted_iota(jnp.int32, scales.shape, 0)
+    slot_at = lax.broadcasted_iota(jnp.int32, scales.shape, 1)
+    row = lax.broadcasted_iota(jnp.int32, (16, HD), 0)
+    rows = jnp.zeros((16, HD), F32)
+    for half in range(2):
+        for run in range(RUNS):
+            chosen = (slot_at == locals_[run]) & (col_at == half * KVH + head)
+            one = jnp.sum(jnp.where(chosen, scales, 0.0), axis=(0, 1), keepdims=True)
+            rows = jnp.where(row == half * RUNS + run, one, rows)
+    dst[pl.ds(2 * PAIR, 16), :] = rows.astype(BF16)
+
+
+def piece_copies(cache, locals_, head, dst, sems, first):
+    made = []
+    for half in range(2):
+        column = pl.multiple_of((half * KVH + head) * HD, HD)
+        for run in range(RUNS):
+            made.append(
+                pltpu.make_async_copy(
+                    cache.at[locals_[run], :, pl.ds(column, HD)],
+                    dst.at[pl.ds(half * PAIR + run * BLK, BLK), :],
+                    sems.at[first + 2 * half + run],
+                )
+            )
+    return made
+
+
+def gather_pieces(meta, cache, cache_scale, jobs, sems):
+    m = meta[META_M]
+    pending = []
+    count = 0
+    for k, slots, refs in jobs:
+        locals_ = [meta[META_SEND + RUNS * k + run] for run in range(RUNS)]
+        made = []
+        for slot, ref in zip(slots, refs):
+            made += piece_copies(cache, locals_, m ^ (2 * slot), ref, sems, count)
+            count += 4
+        for c in made:
+            c.start()
+        pending.append((slots, refs, locals_, made))
+    scales = cache_scale[...].astype(F32)
+    for slots, refs, locals_, _ in pending:
+        for slot, ref in zip(slots, refs):
+            write_scales(scales, locals_, m ^ (2 * slot), ref)
+    return [made for _, _, _, made in pending]
+
+
+def leave(stages, outs, waits, sems):
+    made = []
+    for i, (stage, out) in enumerate(zip(stages, outs)):
+        for c in waits[i]:
+            c.wait()
+        c = pltpu.make_async_copy(stage, out, sems.at[i])
+        c.start()
+        made.append(c)
+    return made
+
+
+def far_kernel(ids, table_, groups_, lengths_, suffixes_, cache, cache_scale, *refs):
+    meta, out4, out5, stage, table, groups, lengths, suffixes, table_sems, sems, out_sems = refs
+    loads = [
+        pltpu.make_async_copy(a, b, table_sems.at[i])
+        for i, (a, b) in enumerate(
+            [(table_, table), (groups_, groups), (lengths_, lengths), (suffixes_, suffixes)]
+        )
+    ]
+    for c in loads:
+        c.start()
+    for c in loads:
+        c.wait()
+    p = ids[0]
+    meta[META_M] = ids[1]
+    slot_count = cache.shape[0]
+    low = p * slot_count
+
+    def send_slots(k):
+        session = groups[p ^ k]
+        for run in range(RUNS):
+            local = jnp.int32(0)
+            for jj in range(POOL):
+                at = table[session, run * POOL + jj] - low
+                local = jnp.where((at >= 0) & (at < slot_count), at, local)
+            meta[META_SEND + RUNS * k + run] = local
+
+    send_slots(4)
+    send_slots(5)
+    jobs = [(4, (0,), (stage.at[0],)), (5, (0,), (stage.at[1],))]
+    waits = gather_pieces(meta, cache, cache_scale, jobs, sems)
+    own = groups[p]
+    for run in range(RUNS):
+        for jj in range(POOL):
+            at = run * POOL + jj
+            meta[META_J + RUNS * ((table[own, at] // slot_count) ^ p) + run] = at
+    meta[META_LEN] = lengths[own]
+    meta[META_SUF] = suffixes[own]
+    leaving = leave([stage.at[0], stage.at[1]], [out4, out5], waits, out_sems)
+    for k in (0, 1, 2, 3, 6, 7):
+        send_slots(k)
+    for out in leaving:
+        out.wait()
+
+
+PIECE_1 = jax.ShapeDtypeStruct((PIECE, HD), BF16)
+PIECE_2 = jax.ShapeDtypeStruct((2, PIECE, HD), BF16)
+
+
+def far_call(ids, table, groups, lengths, suffixes, cache, cache_scale):
+    return pl.pallas_call(
+        far_kernel,
+        out_shape=[jax.ShapeDtypeStruct((META_SIZE,), jnp.int32), PIECE_1, PIECE_1],
+        in_specs=[IN_SMEM] + [IN_HBM] * 5 + [IN_VMEM],
+        out_specs=[IN_SMEM] + [IN_HBM] * 2,
+        scratch_shapes=[
+            pltpu.VMEM((2, PIECE, HD), BF16),
+            pltpu.SMEM(table.shape, jnp.int32),
+            pltpu.SMEM(groups.shape, jnp.int32),
+            pltpu.SMEM(lengths.shape, jnp.int32),
+            pltpu.SMEM(suffixes.shape, jnp.int32),
+            pltpu.SemaphoreType.DMA((4,)),
+            pltpu.SemaphoreType.DMA((8,)),
+            pltpu.SemaphoreType.DMA((2,)),
+        ],
+        compiler_params=pltpu.CompilerParams(vmem_limit_bytes=VMEM_LIMIT),
+        cost_estimate=COST,
+    )(ids, table, groups, lengths, suffixes, cache, cache_scale)
+
+
+SWAP = WIDE + 2 * HD
+
+
+def near_kernel(meta, cache, cache_scale, queries, suffix_kv, *refs):
+    out6, out1, swap, own, own_q, own_kv = refs[:6]
+    stage6, stage1, swap_stage, sems, swap_sems, own_sems, out_sems = refs[6:]
+    m = meta[META_M]
+    swaps = []
+    mine_copies = []
+    for slot in range(2):
+        mine = m ^ (2 * slot)
+        theirs = mine ^ 1
+        jobs = [
+            (queries, theirs * WIDE, WIDE, swap_stage.at[slot, :, pl.ds(0, WIDE)]),
+            (suffix_kv, theirs * HD, HD, swap_stage.at[slot, :, pl.ds(WIDE, HD)]),
+            (suffix_kv, (KVH + theirs) * HD, HD, swap_stage.at[slot, :, pl.ds(WIDE + HD, HD)]),
+            (queries, mine * WIDE, WIDE, own_q.at[slot]),
+            (suffix_kv, mine * HD, HD, own_kv.at[slot, pl.ds(0, ROWS), :]),
+            (suffix_kv, (KVH + mine) * HD, HD, own_kv.at[slot, pl.ds(ROWS, ROWS), :]),
+        ]
+        for i, (src, at, width, dst) in enumerate(jobs):
+            sem = (swap_sems if i < 3 else own_sems).at[3 * slot + i % 3]
+            c = pltpu.make_async_copy(src.at[:, pl.ds(pl.multiple_of(at, HD), width)], dst, sem)
+            c.start()
+            (swaps if i < 3 else mine_copies).append(c)
+    jobs = [
+        (6, (0,), (stage6,)),
+        (1, (0, 1), (stage1.at[0], stage1.at[1])),
+        (0, (0, 1), (own.at[0], own.at[1])),
+    ]
+    waits = gather_pieces(meta, cache, cache_scale, jobs, sems)
+    leaving = leave(
+        [swap_stage, stage6, stage1], [swap, out6, out1], [swaps, waits[0], waits[1]], out_sems
+    )
+    for c in mine_copies + waits[2] + leaving:
+        c.wait()
+
+
+def near_call(meta, cache, cache_scale, queries, suffix_kv):
+    return pl.pallas_call(
+        near_kernel,
+        out_shape=[
+            PIECE_1,
+            PIECE_2,
+            jax.ShapeDtypeStruct((2, ROWS, SWAP), BF16),
+            pltpu.VMEM((2, PIECE, HD), BF16),
+            pltpu.VMEM((2, ROWS, WIDE), BF16),
+            pltpu.VMEM((2, 2 * ROWS, HD), BF16),
+        ],
+        in_specs=[IN_SMEM, IN_HBM, IN_VMEM, IN_HBM, IN_HBM],
+        out_specs=[IN_HBM] * 3 + [IN_VMEM] * 3,
+        scratch_shapes=[
+            pltpu.VMEM((PIECE, HD), BF16),
+            pltpu.VMEM((2, PIECE, HD), BF16),
+            pltpu.VMEM((2, ROWS, SWAP), BF16),
+            pltpu.SemaphoreType.DMA((20,)),
+            pltpu.SemaphoreType.DMA((6,)),
+            pltpu.SemaphoreType.DMA((6,)),
+            pltpu.SemaphoreType.DMA((3,)),
+        ],
+        compiler_params=pltpu.CompilerParams(vmem_limit_bytes=VMEM_LIMIT),
+        cost_estimate=COST,
+    )(meta, cache, cache_scale, queries, suffix_kv)
+
+
+def wide(row):
+    return jnp.concatenate([row] * (TILE // HD), axis=1)
+
+
+def terms(tile, run):
+    key = tile[run : run + 1]
+    value = tile[RUNS + run : RUNS + run + 1]
+    return wide(key * (LOG2E * INV_ROOT)), wide(jnp.log2(value)), wide(1.0 / value)
+
+
+UNIT = None
+
+
+def fold(q, keys, values_t, before, after, blocks_of):
+    tiles = BOTH // TILE
+
+    def score(t):
+        return lax.dot_general(
+            keys, q[pl.ds(t * TILE, TILE), :], NT, preferred_element_type=F32
+        )
+
+    following = score(0)
+    for t in range(tiles):
+        scores = following
+        if t + 1 < tiles:
+            following = score(t + 1)
+        cols = pl.ds(t * TILE, TILE)
+        blocks = blocks_of(t)
+        old = before[REF_ROW : REF_ROW + 1, cols]
+        parts = []
+        reference = old
+        for b, (term, dead, mask) in enumerate(blocks):
+            part = scores[b * BLK : (b + 1) * BLK]
+            part = part if mask is None else jnp.where(mask, part, masked_score)
+            parts.append(part)
+            top = jnp.max(part, axis=0, keepdims=True)
+            top = top * (LOG2E * INV_ROOT) if term is UNIT else top * term[0]
+            if dead is not None:
+                top = jnp.where(dead, masked_score, top)
+            reference = jnp.maximum(reference, top)
+        factor = jnp.exp2(old - reference)
+        total = before[SUM_ROW : SUM_ROW + 1, cols] * factor
+        rounded = []
+        for part, (term, dead, mask) in zip(parts, blocks):
+            shift = reference if term is UNIT else reference - term[1]
+            if dead is not None:
+                shift = jnp.where(dead, -masked_score, shift)
+            scaled = part * (LOG2E * INV_ROOT) if term is UNIT else part * term[0]
+            weights = jnp.exp2(scaled - shift)
+            if mask is not None:
+                weights = jnp.where(mask, weights, 0.0)
+            summed = jnp.sum(weights, axis=0, keepdims=True)
+            total = total + (summed if term is UNIT else summed * term[2])
+            rounded.append(weights.astype(BF16))
+        rounded = jnp.concatenate(rounded, axis=0) if len(rounded) > 1 else rounded[0]
+        product = jnp.dot(values_t, rounded, preferred_element_type=F32)
+        after[:HD, cols] = before[:HD, cols] * factor + product
+        after[REF_ROW : REF_ROW + 1, cols] = reference
+        after[SUM_ROW : SUM_ROW + 1, cols] = total
+
+
+def add_pieces(q, before, after, pieces, ks, meta):
+    m = meta[META_M]
+    n = len(ks)
+    reach = jnp.where(((m // 2) * 2) * ROWS < meta[META_SUF], meta[META_LEN], 0)
+    counts = [
+        jnp.clip(reach - meta[META_J + RUNS * k + r] * BLK, 0, BLK) for k in ks for r in range(RUNS)
+    ]
+    most = functools.reduce(jnp.maximum, counts)
+
+    @pl.when(most < BLK)
+    def _():
+        after[...] = before[...]
+
+    @pl.when(most == BLK)
+    def _():
+        blocks = []
+        for i in range(n):
+            tile = pieces[i, 2 * PAIR :, :].astype(F32)
+            blocks += [(terms(tile, r), counts[RUNS * i + r] < BLK, None) for r in range(RUNS)]
+        keys = [pieces[i, :PAIR, :] for i in range(n)]
+        values = [pieces[i, PAIR : 2 * PAIR, :].T for i in range(n)]
+        fold(
+            q,
+            jnp.concatenate(keys, axis=0) if n > 1 else keys[0],
+            jnp.concatenate(values, axis=1) if n > 1 else values[0],
+            before,
+            after,
+            lambda t: blocks,
+        )
+
+    part = jnp.int32(-1)
+    count = jnp.int32(0)
+    for at, c in enumerate(counts):
+        hit = (c > 0) & (c < BLK)
+        part = jnp.where(hit, at, part)
+        count = jnp.where(hit, c, count)
+
+    @pl.when(part >= 0)
+    def _():
+        i = part // RUNS
+        run = part % RUNS
+        tile = pieces[i, 2 * PAIR :, :].astype(F32)
+        term = [jnp.where(run == 1, b, a) for a, b in zip(terms(tile, 0), terms(tile, 1))]
+        mask = lax.broadcasted_iota(jnp.int32, (BLK, TILE), 0) < count
+        at = pl.multiple_of(run * BLK, BLK)
+        fold(
+            q,
+            pieces[i, pl.ds(at, BLK), :],
+            pieces[i, pl.ds(PAIR + at, BLK), :].T,
+            after,
+            after,
+            lambda t: [(term, None, mask)],
+        )
+
+
+def state_shapes(slots):
+    return [pltpu.VMEM((STATE, BOTH), F32)] * slots
+
+
+def own_kernel(meta, cache, cache_scale, swap, own, own_q, own_kv, *refs):
+    out7, out2, out3, kv, q_all = refs[:5]
+    states = refs[5:7]
+    firsts = refs[7:9]
+    other, sem, stage7, stage2, stage3, sems, out_sems = refs[9:]
+    c = pltpu.make_async_copy(swap, other, sem)
+    c.start()
+    jobs = [
+        (7, (0,), (stage7,)),
+        (2, (0, 1), (stage2.at[0], stage2.at[1])),
+        (3, (0, 1), (stage3.at[0], stage3.at[1])),
+    ]
+    waits = gather_pieces(meta, cache, cache_scale, jobs, sems)
+    leaving = leave([stage7, stage2, stage3], [out7, out2, out3], waits, out_sems)
+    m = meta[META_M]
+    for slot in range(2):
+        for h in range(PER):
+            q_all[slot, h * ROWS : (h + 1) * ROWS, :] = own_q[slot, :, h * HD : (h + 1) * HD]
+        kv[slot, 0] = own_kv[slot]
+    c.wait()
+    for slot in range(2):
+        for h in range(PER):
+            q_all[slot, WIDE + h * ROWS : WIDE + (h + 1) * ROWS, :] = other[
+                slot, :, h * HD : (h + 1) * HD
+            ]
+        kv[slot, 1, :ROWS, :] = other[slot, :, WIDE : WIDE + HD]
+        kv[slot, 1, ROWS:, :] = other[slot, :, WIDE + HD :]
+    key = lax.broadcasted_iota(jnp.int32, (BLK, TILE), 0)
+    row = lax.broadcasted_iota(jnp.int32, (BLK, TILE), 1) % ROWS
+    causal = key <= row
+    odd = (m % 2) == 1
+
+    def blocks_of(t):
+        if t * TILE < WIDE:
+            return [(UNIT, None, causal), (UNIT, jnp.logical_not(odd), None)]
+        return [(UNIT, odd, None), (UNIT, None, causal)]
+
+    for slot in range(2):
+        first = firsts[slot]
+        first[:HD, :] = jnp.zeros((HD, BOTH), F32)
+        first[REF_ROW : REF_ROW + 8, :] = jnp.full((8, BOTH), masked_score, F32)
+        first[SUM_ROW : SUM_ROW + 8, :] = jnp.zeros((8, BOTH), F32)
+        keys = jnp.concatenate([kv[slot, 0, :ROWS], kv[slot, 1, :ROWS]], axis=0)
+        values = jnp.concatenate([kv[slot, 0, ROWS:].T, kv[slot, 1, ROWS:].T], axis=1)
+        fold(q_all.at[slot], keys, values, first, first, blocks_of)
+        add_pieces(q_all.at[slot], first, states[slot], own.at[pl.ds(slot, 1)], (0,), meta)
+    for c in leaving:
+        c.wait()
+
+
+def own_call(meta, cache, cache_scale, swap, own, own_q, own_kv):
+    out = pl.pallas_call(
+        own_kernel,
+        out_shape=[
+            PIECE_1,
+            PIECE_2,
+            PIECE_2,
+            jax.ShapeDtypeStruct((2, 2, 2 * ROWS, HD), BF16),
+            pltpu.VMEM((2, BOTH, HD), BF16),
+        ]
+        + state_shapes(2),
+        in_specs=[IN_SMEM, IN_HBM, IN_VMEM, IN_HBM, IN_VMEM, IN_VMEM, IN_VMEM],
+        out_specs=[IN_HBM] * 3 + [IN_VMEM] * 4,
+        scratch_shapes=state_shapes(2)
+        + [
+            pltpu.VMEM((2, ROWS, SWAP), BF16),
+            pltpu.SemaphoreType.DMA,
+            pltpu.VMEM((PIECE, HD), BF16),
+            pltpu.VMEM((2, PIECE, HD), BF16),
+            pltpu.VMEM((2, PIECE, HD), BF16),
+            pltpu.SemaphoreType.DMA((20,)),
+            pltpu.SemaphoreType.DMA((3,)),
+        ],
+        compiler_params=pltpu.CompilerParams(vmem_limit_bytes=VMEM_LIMIT),
+        cost_estimate=COST,
+    )(meta, cache, cache_scale, swap, own, own_q, own_kv)
+    return out[:4], out[4], out[5:]
+
+
+def add_kernel(slots, ks, last, meta, q_all, *refs):
+    refs = list(refs)
+    take = lambda n: [refs.pop(0) for _ in range(n)]
+    before = take(len(slots))
+    sources = take(len(ks))
+    if last:
+        whole = take(1)[0] if slots[0] == 0 else take(2)[1]
+        other, state, mine, sem = take(4)
+        after = [state]
+    else:
+        after = take(len(slots))
+    kv = take(1)[0]
+    for w, slot in enumerate(slots):
+        for i, s in enumerate(sources):
+            kv[w, i] = s[slot] if len(s.shape) == 3 else s[...]
+        add_pieces(q_all.at[slot], before[w], after[w], kv.at[w], ks, meta)
+    if last:
+        for side, ref in enumerate((mine, other)):
+            member = meta[META_M] ^ side
+            row = lax.broadcasted_iota(jnp.int32, (ROWS, HD), 0) + member * ROWS
+            for i in range(PER):
+                cols = pl.ds(side * WIDE + i * ROWS, ROWS)
+                piece = (state[:HD, cols] / state[SUM_ROW : SUM_ROW + 1, cols]).T
+                piece = jnp.where(row < meta[META_SUF], piece, 0.0)
+                ref[:, i * HD : (i + 1) * HD] = piece.astype(BF16)
+        column = pl.multiple_of((meta[META_M] ^ (2 * slots[0])) * WIDE, WIDE)
+        c = pltpu.make_async_copy(mine, whole.at[:, pl.ds(column, WIDE)], sem)
+        c.start()
+        c.wait()
+
+
+def add_call(meta, q_all, states, sources, slots, ks, last=False, whole=None):
+    flat = [states[s] for s in slots]
+    n = len(ks)
+    args = [meta, q_all, *flat, *sources]
+    in_specs = [IN_SMEM] + [IN_VMEM] * (len(args) - 1)
+    scratch = [pltpu.VMEM((len(slots), n, PIECE, HD), BF16)]
+    aliases = {}
+    if last:
+        out_shape = [
+            jax.ShapeDtypeStruct((ROWS, QH * HD), BF16),
+            jax.ShapeDtypeStruct((ROWS, WIDE), BF16),
+        ]
+        out_specs = [IN_HBM, IN_VMEM]
+        scratch = (
+            state_shapes(1) + [pltpu.VMEM((ROWS, WIDE), BF16), pltpu.SemaphoreType.DMA] + scratch
+        )
+        if whole is not None:
+            aliases = {len(args): 0}
+            args.append(whole)
+            in_specs.append(IN_HBM)
+    else:
+        out_shape = state_shapes(len(slots))
+        out_specs = [IN_VMEM] * len(slots)
+    out = pl.pallas_call(
+        functools.partial(add_kernel, slots, ks, last),
+        out_shape=out_shape,
+        in_specs=in_specs,
+        out_specs=out_specs,
+        scratch_shapes=scratch,
+        input_output_aliases=aliases,
+        compiler_params=pltpu.CompilerParams(vmem_limit_bytes=VMEM_LIMIT),
+        cost_estimate=COST,
+    )(*args)
+    if last:
+        return out
+    states = list(states)
+    for w, slot in enumerate(slots):
+        states[slot] = out[w]
+    return states
+
+
+def early_kernel(meta, q_all, *refs):
+    before = refs[0:2]
+    kv = refs[2]
+    after = refs[3:5]
+    m = meta[META_M]
+
+    @pl.when(m < 2)
+    def _():
+        for a, b in zip(before, after):
+            b[...] = a[...]
+
+    @pl.when(m >= 2)
+    def _():
+        for slot in range(2):
+            fold(
+                q_all.at[slot],
+                jnp.concatenate([kv[1 - slot, side, :ROWS] for side in range(2)], axis=0),
+                jnp.concatenate([kv[1 - slot, side, ROWS:].T for side in range(2)], axis=1),
+                before[slot],
+                after[slot],
+                lambda t: [(UNIT, None, None)] * 2,
+            )
+
+
+def early_call(meta, q_all, states, kv):
+    return pl.pallas_call(
+        early_kernel,
+        out_shape=state_shapes(2),
+        in_specs=[IN_SMEM] + [IN_VMEM] * 4,
+        out_specs=[IN_VMEM] * 2,
+        compiler_params=pltpu.CompilerParams(vmem_limit_bytes=VMEM_LIMIT),
+        cost_estimate=COST,
+    )(meta, q_all, *states, kv)
+
+
+def join_kernel(meta, c, d, _, out, sems):
+    made = []
+    for i, src in enumerate((c, d)):
+        column = pl.multiple_of((meta[META_M] ^ (1 + 2 * i)) * WIDE, WIDE)
+        made.append(pltpu.make_async_copy(src, out.at[:, pl.ds(column, WIDE)], sems.at[i]))
+        made[-1].start()
+    for x in made:
+        x.wait()
+
+
+def join_call(meta, c, d, whole):
+    return pl.pallas_call(
+        join_kernel,
+        out_shape=jax.ShapeDtypeStruct((ROWS, QH * HD), BF16),
+        in_specs=[IN_SMEM, IN_VMEM, IN_VMEM, IN_HBM],
+        out_specs=IN_HBM,
+        scratch_shapes=[pltpu.SemaphoreType.DMA((2,))],
+        input_output_aliases={3: 0},
+        cost_estimate=COST,
+    )(meta, c, d, whole)
+
+
+def permute(x, axis, count, k):
+    return lax.ppermute(x, axis, [(i, i ^ k) for i in range(count)])
+
+
+def per_device_small(
+    queries, suffix_kv, cache, cache_scale, prefix_len, suffix_len, block_table, session_group
+):
+    ids = jnp.stack([lax.axis_index("pool"), lax.axis_index("blk")]).astype(jnp.int32)
+    tables = [block_table, session_group, prefix_len, suffix_len]
+    queries, suffix_kv, cache, *tables = [
+        pltpu.with_memory_space_constraint(x, pltpu.HBM)
+        for x in (queries, suffix_kv, cache, *tables)
+    ]
+    blocks = (cache, cache_scale.T)
+    far_in, near_in = {}, {}
+    meta, far4, far5 = far_call(ids, *tables, *blocks)
+    far_in[4] = permute(far4, "pool", POOL, 4)
+    far_in[5] = permute(far5, "pool", POOL, 5)
+    far6, near1, swap, own, own_q, own_kv = near_call(meta, *blocks, queries, suffix_kv)
+    swap_in = permute(swap, "blk", 4, 1)
+    far_in[6] = permute(far6, "pool", POOL, 6)
+    near_in[1] = permute(near1, "pool", POOL, 1)
+    (far7, near2, near3, kv), q_all, states = own_call(
+        meta, *blocks, swap_in, own, own_q, own_kv
+    )
+    far_in[7] = permute(far7, "pool", POOL, 7)
+    near_in[2] = permute(near2, "pool", POOL, 2)
+    near_in[3] = permute(near3, "pool", POOL, 3)
+    early = permute(kv, "blk", 4, 2)
+    across = {k: permute(far_in[k], "blk", 4, 2) for k in (4, 5, 6, 7)}
+
+    states = add_call(meta, q_all, states, [near_in[1]], (0, 1), (1,))
+    states = early_call(meta, q_all, states, early)
+    states = add_call(meta, q_all, states, [near_in[2], near_in[3]], (0, 1), (2, 3))
+    states = add_call(meta, q_all, states, [far_in[4], far_in[5]], (0,), (4, 5))
+    states = add_call(meta, q_all, states, [across[4], across[5]], (1,), (4, 5))
+    whole = None
+    yours = []
+    for slot, source in ((0, far_in), (1, across)):
+        whole, other = add_call(
+            meta, q_all, states, [source[6], source[7]], (slot,), (6, 7), last=True, whole=whole
+        )
+        yours.append(permute(other, "blk", 4, 1))
+    return join_call(meta, *yours, whole)
 
 
 def fold_keys(running, query_heads, key_rows, value_rows, key_scale, value_scale, usable):
@@ -29,7 +630,7 @@
     return (new_highest, weight_sum, weighted)
 
 
-def per_device(
+def per_device_any(
     queries, suffix_kv, cache, cache_scale, prefix_len, suffix_len, block_table, session_group
 ):
     local_rows = queries.shape[0]
@@ -126,8 +727,9 @@
 
 
 def solution(mesh):
+    small = dict(mesh.shape) == {"pool": POOL, "blk": 4}
     return jax.shard_map(
-        per_device,
+        per_device_small if small else per_device_any,
         mesh=mesh,
         in_specs=(
             P(("pool", "blk"), None),

time: 143 us -> 67.9 us (0.47)
  the two profiles are of different devices: /device:TPU:9 before, /device:TPU:23 now
where the time goes in v1:
time: 67.9 us; the launch traced here: 66.6 us
  Pallas kernels  35.4 us (52%)
  starting transfers between devices  17.3 us (25%)
  waiting for transfers between devices  12.2 us (18%)
  local copies, waits for them, and re-layouts  1.39 us (2%)
    pallas_call x6, Pallas kernels, add_call(): pl.pallas_call(functools.partial(add_kernel, slots, ks, last), out_shape=...  17.5 us
    ppermute x15, starting transfers between devices, permute(): return lax.ppermute(x, axis, [(i, i ^ k) for i in range(count)])  17.3 us
    ppermute x15, waiting for transfers between devices, permute(): return lax.ppermute(x, axis, [(i, i ^ k) for i in range(count)])  12.2 us
    pallas_call x1, Pallas kernels, own_call(): pl.pallas_call(own_kernel, out_shape=[PIECE_1, PIECE_2, PIECE_2, jax.Shap...  6.66 us
    pallas_call x1, Pallas kernels, far_call(): pl.pallas_call(far_kernel, out_shape=[jax.ShapeDtypeStruct((META_SIZE,),...  3.58 us
    pallas_call x1, Pallas kernels, early_call(): pl.pallas_call(early_kernel, out_shape=state_shapes(2), in_specs=[IN_SMEM...  2.88 us
    pallas_call x1, Pallas kernels, near_call(): pl.pallas_call(near_kernel, out_shape=[PIECE_1, PIECE_2, jax.ShapeDtypeSt...  2.88 us
    pallas_call x1, Pallas kernels, join_call(): pl.pallas_call(join_kernel, out_shape=jax.ShapeDtypeStruct((ROWS, QH * HD...  1.85 us
  transfers between devices with their start and end apart: 15, of which 6 were waited for; matrix products, arithmetic and copies ran while one was open for 0% of the time, Pallas kernels for 36%

profile of v1, /device:TPU:23, one launch (start us, length us, event | category | flops | bytes accessed | tf_op | source)
XLA Modules:
  0.0 66.6 jit_solution(11270885861180450440)
XLA Ops:
  0.1 0.7 %copy-done.1 = bf16[16,8]{0,1:T(8,128)(2,1)S(1)} copy-done((bf16[16,8]{0,1:T(8,128)(2,1)S(1)}, bf16[16,8]{0,1:T(8,128)(2,1)}, u32[]{:S(2)}) %copy-start.1) | copy-done | bytes 280
  0.8 3.6 %shard_map.82 = (s32[40]{0:T(128)S(1)}, bf16[528,128]{1,0:T(8,128)(2,1)S(1)}, bf16[528,128]{1,0:T(8,128)(2,1)S(1)}) custom-call(s32[2]{0:T(128)S(1)} %pad_add_fusion.ids, s32[8,16]{1,0:T(8,128)} %table_.1, s32[8]{0:T(128)} %groups_.1, s32[8]{0:T(128)} %lengths_.1, s32[8]{0:T(128)} %suffixes_.1, bf16[16,128,1024]{2,1,0:T(8,128)(2,1)} %cache.5, ...), custom_call_target="tpu_custom_call" | custom-call | flops 1024 | bytes 1024 | tf_op jit(solution)/shard_map/pallas_call | solution.py:158
  4.4 2.9 %shard_map.83 = (bf16[528,128]{1,0:T(8,128)(2,1)S(1)}, bf16[2,528,128]{2,1,0:T(8,128)(2,1)S(1)}, bf16[2,128,1280]{2,1,0:T(8,128)(2,1)S(1)}, bf16[2,528,128]{2,1,...) custom-call(s32[40]{0:T(128)S(1)} %get-tuple-element.31.meta, ...), custom_call_target="tpu_custom_call" | custom-call | flops 1024 | bytes 1024 | tf_op jit(solution)/shard_map/pallas_call | solution.py:217
  7.2 0.7 %collective-permute-start = (bf16[2,128,1280]{2,1,0:T(8,128)(2,1)S(1)}, bf16[2,128,1280]{2,1,0:T(8,128)(2,1)S(1)}, u32[]{:S(2)}, u32[]{:S(2)}) collective-permute-start(bf16[2,128,1280]{2,1,0:T(8,128)(2,1)S(1)} %get-tuple-element.32), channel_id=1, source_target_pairs={{0,1},{1,0},{2,3},{3,2},{4,5},{5,4},{6,7},{7,6},{8,9},{9,8},{10,11... | collective-permute-start | bytes 1966088 | tf_op jit(solution)/shard_map/ppermute | solution.py:572
  8.1 2.3 %collective-permute-start.6 = (bf16[528,128]{1,0:T(8,128)(2,1)S(1)}, bf16[528,128]{1,0:T(8,128)(2,1)S(1)}, u32[]{:S(2)}, u32[]{:S(2)}) collective-permute-start(bf16[528,128]{1,0:T(8,128)(2,1)S(1)} %get-tuple-element.49), channel_id=1, source_target_pairs={{0,20},{4,16},{8,28},{12,24},{16,4},{20,0},{24,12},{28,8},{1,21},{... | collective-permute-start | bytes 405512 | tf_op jit(solution)/shard_map/ppermute | solution.py:572
  10.3 1.2 %collective-permute-start.1 = (bf16[2,528,128]{2,1,0:T(8,128)(2,1)S(1)}, bf16[2,528,128]{2,1,0:T(8,128)(2,1)S(1)}, u32[]{:S(2)}, u32[]{:S(2)}) collective-permute-start(bf16[2,528,128]{2,1,0:T(8,128)(2,1)S(1)} %get-tuple-element.39), channel_id=1, source_target_pairs={{0,4},{4,0},{8,12},{12,8},{16,20},{20,16},{24,28},{28,24},{1,5},{5... | collective-permute-start | bytes 811016 | tf_op jit(solution)/shard_map/ppermute | solution.py:572
  11.7 6.7 %shard_map.84 = (bf16[528,128]{1,0:T(8,128)(2,1)S(1)}, bf16[2,528,128]{2,1,0:T(8,128)(2,1)S(1)}, bf16[2,528,128]{2,1,0:T(8,128)(2,1)S(1)}, bf16[2,2,256,128]{3,2...) custom-call(s32[40]{0:T(128)S(1)} %get-tuple-element.31.meta, ...), custom_call_target="tpu_custom_call" | custom-call | flops 1024 | bytes 1024 | tf_op jit(solution)/shard_map/pallas_call | solution.py:414
  18.4 1.2 %collective-permute-start.3 = (bf16[2,528,128]{2,1,0:T(8,128)(2,1)S(1)}, bf16[2,528,128]{2,1,0:T(8,128)(2,1)S(1)}, u32[]{:S(2)}, u32[]{:S(2)}) collective-permute-start(bf16[2,528,128]{2,1,0:T(8,128)(2,1)S(1)} %get-tuple-element.45), channel_id=1, source_target_pairs={{0,8},{4,12},{8,0},{12,4},{16,24},{20,28},{24,16},{28,20},{1,9},{5... | collective-permute-start | bytes 811016 | tf_op jit(solution)/shard_map/ppermute | solution.py:572
  19.9 2.7 %collective-permute-done.6.refs_2_ = bf16[528,128]{1,0:T(8,128)(2,1)S(1)} collective-permute-done((bf16[528,128]{1,0:T(8,128)(2,1)S(1)}, bf16[528,128]{1,0:T(8,128)(2,1)S(1)}, u32[]{:S(2)}, u32[]{:S(2)}) %collective-permute-start.6) | collective-permute-done | bytes 135200 | tf_op jit(solution)/shard_map/ppermute | solution.py:572
  22.6 5.6 %collective-permute-start.4 = (bf16[2,528,128]{2,1,0:T(8,128)(2,1)S(1)}, bf16[2,528,128]{2,1,0:T(8,128)(2,1)S(1)}, u32[]{:S(2)}, u32[]{:S(2)}) collective-permute-start(bf16[2,528,128]{2,1,0:T(8,128)(2,1)S(1)} %get-tuple-element.46), channel_id=1, source_target_pairs={{0,12},{4,8},{8,4},{12,0},{16,28},{20,24},{24,20},{28,16},{1,13},{... | collective-permute-start | bytes 811016 | tf_op jit(solution)/shard_map/ppermute | solution.py:572
  28.2 0.8 %collective-permute-done.7.refs_1_ = bf16[528,128]{1,0:T(8,128)(2,1)S(1)} collective-permute-done((bf16[528,128]{1,0:T(8,128)(2,1)S(1)}, bf16[528,128]{1,0:T(8,128)(2,1)S(1)}, u32[]{:S(2)}, u32[]{:S(2)}) %collective-permute-start.7) | collective-permute-done | bytes 135200 | tf_op jit(solution)/shard_map/ppermute | solution.py:572
  29.2 7.1 %collective-permute-done.8.refs_2_ = bf16[528,128]{1,0:T(8,128)(2,1)S(1)} collective-permute-done((bf16[528,128]{1,0:T(8,128)(2,1)S(1)}, bf16[528,128]{1,0:T(8,128)(2,1)S(1)}, u32[]{:S(2)}, u32[]{:S(2)}) %collective-permute-start.8) | collective-permute-done | bytes 135200 | tf_op jit(solution)/shard_map/ppermute | solution.py:572
  36.5 1.2 %collective-permute-start.12 = (bf16[528,128]{1,0:T(8,128)(2,1)S(1)}, bf16[528,128]{1,0:T(8,128)(2,1)S(1)}, u32[]{:S(2)}, u32[]{:S(2)}) collective-permute-start(bf16[528,128]{1,0:T(8,128)(2,1)S(1)} %collective-permute-done.7.refs_1_), channel_id=1, source_target_pairs={{0,2},{1,3},{2,0},{3,1},{4,6},{5,7},{6,4},{7,5},{8,10},{9,11},{10,... | collective-permute-start | bytes 405512 | tf_op jit(solution)/shard_map/ppermute | solution.py:572
  38.0 2.7 %shard_map.85 = (f32[144,2048]{1,0:T(8,128)S(1)}, f32[144,2048]{1,0:T(8,128)S(1)}) custom-call(s32[40]{0:T(128)S(1)} %get-tuple-element.31.meta, bf16[2,2048,128]{2,1,0:T(8,128)(2,1)S(1)} %get-tuple-element.36.q_all, f32[144,2048]{1,0:T(8,128)S(1)} %get-tuple-element.37.refs_0_, f32[144,2048]{1,0:T(8,128)S(1)} %get-tuple-element.38.refs_1_, ...), custom_call_target="tpu_custom_call" | custom-call | flops 1024 | bytes 1024 | tf_op jit(solution)/shard_map/pallas_call | solution.py:496
  40.7 2.9 %shard_map.86 = (f32[144,2048]{1,0:T(8,128)S(1)}, f32[144,2048]{1,0:T(8,128)S(1)}) custom-call(s32[40]{0:T(128)S(1)} %get-tuple-element.31.meta, bf16[2,2048,128]{2,1,0:T(8,128)(2,1)S(1)} %get-tuple-element.36.q_all, f32[144,2048]{1,0:T(8,128)S(1)} %get-tuple-element.40.refs_0_, f32[144,2048]{1,0:T(8,128)S(1)} %get-tuple-element.41.refs_1_, ...), custom_call_target="tpu_custom_call" | custom-call | flops 1024 | bytes 1024 | tf_op jit(solution)/shard_map/pallas_call | solution.py:539
  43.6 3.9 %shard_map.87 = (f32[144,2048]{1,0:T(8,128)S(1)}, f32[144,2048]{1,0:T(8,128)S(1)}) custom-call(s32[40]{0:T(128)S(1)} %get-tuple-element.31.meta, bf16[2,2048,128]{2,1,0:T(8,128)(2,1)S(1)} %get-tuple-element.36.q_all, f32[144,2048]{1,0:T(8,128)S(1)} %get-tuple-element.43.refs_0_, f32[144,2048]{1,0:T(8,128)S(1)} %get-tuple-element.44.refs_1_, ...), custom_call_target="tpu_custom_call" | custom-call | flops 1024 | bytes 1024 | tf_op jit(solution)/shard_map/pallas_call | solution.py:496
  47.6 2.2 %shard_map.88.refs_0_ = f32[144,2048]{1,0:T(8,128)S(1)} custom-call(s32[40]{0:T(128)S(1)} %get-tuple-element.31.meta, bf16[2,2048,128]{2,1,0:T(8,128)(2,1)S(1)} %get-tuple-element.36.q_all, f32[144,2048]{1,0:T(8,128)S(1)} %get-tuple-element.47.refs_0_, bf16[528,128]{1,0:T(8,128)(2,1)S(1)} %collective-permute-done.5.refs_1_, ...), custom_call_target="tpu_custom_call" | custom-call | flops 1024 | bytes 1024 | tf_op jit(solution)/shard_map/pallas_call | solution.py:496
  49.8 3.1 %shard_map.89 = (bf16[128,4096]{1,0:T(8,128)(2,1)}, bf16[128,1024]{1,0:T(8,128)(2,1)S(1)}) custom-call(s32[40]{0:T(128)S(1)} %get-tuple-element.31.meta, bf16[2,2048,128]{2,1,0:T(8,128)(2,1)S(1)} %get-tuple-element.36.q_all, f32[144,2048]{1,0:T(8,128)S(1)} %shard_map.88.refs_0_, bf16[528,128]{1,0:T(8,128)(2,1)S(1)} %collective-permute-done.7.refs_1_, ...), custom_call_target="tpu_custom_call" | custom-call | flops 1024 | bytes 1024 | tf_op jit(solution)/shard_map/pallas_call | solution.py:496
  52.9 2.5 %shard_map.90.refs_0_ = f32[144,2048]{1,0:T(8,128)S(1)} custom-call(s32[40]{0:T(128)S(1)} %get-tuple-element.31.meta, bf16[2,2048,128]{2,1,0:T(8,128)(2,1)S(1)} %get-tuple-element.36.q_all, f32[144,2048]{1,0:T(8,128)S(1)} %get-tuple-element.53.refs_0_, bf16[528,128]{1,0:T(8,128)(2,1)S(1)} %collective-permute-done.10.refs_1_, ...), custom_call_target="tpu_custom_call" | custom-call | flops 1024 | bytes 1024 | tf_op jit(solution)/shard_map/pallas_call | solution.py:496
  55.4 3.1 %shard_map.91 = (bf16[128,4096]{1,0:T(8,128)(2,1)}, bf16[128,1024]{1,0:T(8,128)(2,1)S(1)}) custom-call(s32[40]{0:T(128)S(1)} %get-tuple-element.31.meta, bf16[2,2048,128]{2,1,0:T(8,128)(2,1)S(1)} %get-tuple-element.36.q_all, f32[144,2048]{1,0:T(8,128)S(1)} %shard_map.90.refs_0_, ...), custom_call_target="tpu_custom_call", output_to_operand_aliasing={{0}: (5, {})} | custom-call | flops 1024 | bytes 1024 | tf_op jit(solution)/shard_map/pallas_call | solution.py:496
  58.5 3.8 %collective-permute-start.14 = (bf16[128,1024]{1,0:T(8,128)(2,1)S(1)}, bf16[128,1024]{1,0:T(8,128)(2,1)S(1)}, u32[]{:S(2)}, u32[]{:S(2)}) collective-permute-start(bf16[128,1024]{1,0:T(8,128)(2,1)S(1)} %get-tuple-element.55), channel_id=1, source_target_pairs={{0,1},{1,0},{2,3},{3,2},{4,5},{5,4},{6,7},{7,6},{8,9},{9,8},{10,11... | collective-permute-start | bytes 786440 | tf_op jit(solution)/shard_map/ppermute | solution.py:572
  62.4 1.1 %collective-permute-done.14.d = bf16[128,1024]{1,0:T(8,128)(2,1)S(1)} collective-permute-done((bf16[128,1024]{1,0:T(8,128)(2,1)S(1)}, bf16[128,1024]{1,0:T(8,128)(2,1)S(1)}, u32[]{:S(2)}, u32[]{:S(2)}) %collective-permute-start.14) | collective-permute-done | bytes 262176 | tf_op jit(solution)/shard_map/ppermute | solution.py:572
  64.2 0.4 copy-done.3
  64.6 1.8 %shard_map.92 = bf16[128,4096]{1,0:T(8,128)(2,1)} custom-call(s32[40]{0:T(128)} %copy-done, bf16[128,1024]{1,0:T(8,128)(2,1)} %copy-done.3, bf16[128,1024]{1,0:T(8,128)(2,1)} %copy-done.2, bf16[128,4096]{1,0:T(8,128)(2,1)} %get-tuple-element.56._), custom_call_target="tpu_custom_call", output_to_operand_aliasing={{}: (3, {})} | custom-call | flops 1024 | bytes 1024 | tf_op jit(solution)/shard_map/pallas_call | solution.py:560
  (26 shorter events, 2.1 us)
Async XLA Ops:
  0.1 0.7 %copy-start.1 = (bf16[16,8]{0,1:T(8,128)(2,1)S(1)}, bf16[16,8]{0,1:T(8,128)(2,1)}, u32[]{:S(2)}) copy-start(bf16[16,8]{0,1:T(8,128)(2,1)} %param.11) | copy-start | bytes 772
  4.3 51.1 %copy-start = (s32[40]{0:T(128)}, s32[40]{0:T(128)S(1)}, u32[]{:S(2)}) copy-start(s32[40]{0:T(128)S(1)} %get-tuple-element.31.meta) | copy-start | bytes 484
  7.2 4.5 %collective-permute-start = (bf16[2,128,1280]{2,1,0:T(8,128)(2,1)S(1)}, bf16[2,128,1280]{2,1,0:T(8,128)(2,1)S(1)}, u32[]{:S(2)}, u32[]{:S(2)}) collective-permute-start(bf16[2,128,1280]{2,1,0:T(8,128)(2,1)S(1)} %get-tuple-element.32), channel_id=1, source_target_pairs={{0,1},{1,0},{2,3},{3,2},{4,5},{5,4},{6,7},{7,6},{8,9},{9,8},{10,11... | collective-permute-start | bytes 1966088 | tf_op jit(solution)/shard_map/ppermute | solution.py:572
  8.0 11.7 %collective-permute-start.5 = (bf16[528,128]{1,0:T(8,128)(2,1)S(1)}, bf16[528,128]{1,0:T(8,128)(2,1)S(1)}, u32[]{:S(2)}, u32[]{:S(2)}) collective-permute-start(bf16[528,128]{1,0:T(8,128)(2,1)S(1)} %get-tuple-element.48), channel_id=1, source_target_pairs={{0,16},{4,20},{8,24},{12,28},{16,0},{20,4},{24,8},{28,12},{1,17},{... | collective-permute-start | bytes 405512 | tf_op jit(solution)/shard_map/ppermute | solution.py:572
  8.1 14.5 %collective-permute-start.6 = (bf16[528,128]{1,0:T(8,128)(2,1)S(1)}, bf16[528,128]{1,0:T(8,128)(2,1)S(1)}, u32[]{:S(2)}, u32[]{:S(2)}) collective-permute-start(bf16[528,128]{1,0:T(8,128)(2,1)S(1)} %get-tuple-element.49), channel_id=1, source_target_pairs={{0,20},{4,16},{8,28},{12,24},{16,4},{20,0},{24,12},{28,8},{1,21},{... | collective-permute-start | bytes 405512 | tf_op jit(solution)/shard_map/ppermute | solution.py:572
  10.3 18.6 %collective-permute-start.1 = (bf16[2,528,128]{2,1,0:T(8,128)(2,1)S(1)}, bf16[2,528,128]{2,1,0:T(8,128)(2,1)S(1)}, u32[]{:S(2)}, u32[]{:S(2)}) collective-permute-start(bf16[2,528,128]{2,1,0:T(8,128)(2,1)S(1)} %get-tuple-element.39), channel_id=1, source_target_pairs={{0,4},{4,0},{8,12},{12,8},{16,20},{20,16},{24,28},{28,24},{1,5},{5... | collective-permute-start | bytes 811016 | tf_op jit(solution)/shard_map/ppermute | solution.py:572
  11.5 17.4 %collective-permute-start.7 = (bf16[528,128]{1,0:T(8,128)(2,1)S(1)}, bf16[528,128]{1,0:T(8,128)(2,1)S(1)}, u32[]{:S(2)}, u32[]{:S(2)}) collective-permute-start(bf16[528,128]{1,0:T(8,128)(2,1)S(1)} %get-tuple-element.50), channel_id=1, source_target_pairs={{0,24},{4,28},{8,16},{12,20},{16,8},{20,12},{24,0},{28,4},{1,25},{... | collective-permute-start | bytes 405512 | tf_op jit(solution)/shard_map/ppermute | solution.py:572
  18.4 19.4 %collective-permute-start.3 = (bf16[2,528,128]{2,1,0:T(8,128)(2,1)S(1)}, bf16[2,528,128]{2,1,0:T(8,128)(2,1)S(1)}, u32[]{:S(2)}, u32[]{:S(2)}) collective-permute-start(bf16[2,528,128]{2,1,0:T(8,128)(2,1)S(1)} %get-tuple-element.45), channel_id=1, source_target_pairs={{0,8},{4,12},{8,0},{12,4},{16,24},{20,28},{24,16},{28,20},{1,9},{5... | collective-permute-start | bytes 811016 | tf_op jit(solution)/shard_map/ppermute | solution.py:572
  19.7 16.8 %collective-permute-start.2 = (bf16[2,2,256,128]{3,2,1,0:T(8,128)(2,1)S(1)}, bf16[2,2,256,128]{3,2,1,0:T(8,128)(2,1)S(1)}, u32[]{:S(2)}, u32[]{:S(2)}) collective-permute-start(bf16[2,2,256,128]{3,2,1,0:T(8,128)(2,1)S(1)} %get-tuple-element.42), channel_id=1, source_target_pairs={{0,2},{1,3},{2,0},{3,1},{4,6},{5,7},{6,4},{7,5},{8,10},{9,11},{10,... | collective-permute-start | bytes 786440 | tf_op jit(solution)/shard_map/ppermute | solution.py:572
  22.6 21.0 %collective-permute-start.4 = (bf16[2,528,128]{2,1,0:T(8,128)(2,1)S(1)}, bf16[2,528,128]{2,1,0:T(8,128)(2,1)S(1)}, u32[]{:S(2)}, u32[]{:S(2)}) collective-permute-start(bf16[2,528,128]{2,1,0:T(8,128)(2,1)S(1)} %get-tuple-element.46), channel_id=1, source_target_pairs={{0,12},{4,8},{8,4},{12,0},{16,28},{20,24},{24,20},{28,16},{1,13},{... | collective-permute-start | bytes 811016 | tf_op jit(solution)/shard_map/ppermute | solution.py:572
  29.0 7.3 %collective-permute-start.8 = (bf16[528,128]{1,0:T(8,128)(2,1)S(1)}, bf16[528,128]{1,0:T(8,128)(2,1)S(1)}, u32[]{:S(2)}, u32[]{:S(2)}) collective-permute-start(bf16[528,128]{1,0:T(8,128)(2,1)S(1)} %get-tuple-element.51), channel_id=1, source_target_pairs={{0,28},{4,24},{8,20},{12,16},{16,12},{20,8},{24,4},{28,0},{1,29},{... | collective-permute-start | bytes 405512 | tf_op jit(solution)/shard_map/ppermute | solution.py:572
  29.0 23.9 %collective-permute-start.10 = (bf16[528,128]{1,0:T(8,128)(2,1)S(1)}, bf16[528,128]{1,0:T(8,128)(2,1)S(1)}, u32[]{:S(2)}, u32[]{:S(2)}) collective-permute-start(bf16[528,128]{1,0:T(8,128)(2,1)S(1)} %collective-permute-done.5.refs_1_), channel_id=1, source_target_pairs={{0,2},{1,3},{2,0},{3,1},{4,6},{5,7},{6,4},{7,5},{8,10},{9,11},{10,... | collective-permute-start | bytes 405512 | tf_op jit(solution)/shard_map/ppermute | solution.py:572
  36.3 16.6 %collective-permute-start.11 = (bf16[528,128]{1,0:T(8,128)(2,1)S(1)}, bf16[528,128]{1,0:T(8,128)(2,1)S(1)}, u32[]{:S(2)}, u32[]{:S(2)}) collective-permute-start(bf16[528,128]{1,0:T(8,128)(2,1)S(1)} %collective-permute-done.6.refs_2_), channel_id=1, source_target_pairs={{0,2},{1,3},{2,0},{3,1},{4,6},{5,7},{6,4},{7,5},{8,10},{9,11},{10,... | collective-permute-start | bytes 405512 | tf_op jit(solution)/shard_map/ppermute | solution.py:572
  36.5 18.9 %collective-permute-start.12 = (bf16[528,128]{1,0:T(8,128)(2,1)S(1)}, bf16[528,128]{1,0:T(8,128)(2,1)S(1)}, u32[]{:S(2)}, u32[]{:S(2)}) collective-permute-start(bf16[528,128]{1,0:T(8,128)(2,1)S(1)} %collective-permute-done.7.refs_1_), channel_id=1, source_target_pairs={{0,2},{1,3},{2,0},{3,1},{4,6},{5,7},{6,4},{7,5},{8,10},{9,11},{10,... | collective-permute-start | bytes 405512 | tf_op jit(solution)/shard_map/ppermute | solution.py:572
  37.8 17.6 %collective-permute-start.13 = (bf16[528,128]{1,0:T(8,128)(2,1)S(1)}, bf16[528,128]{1,0:T(8,128)(2,1)S(1)}, u32[]{:S(2)}, u32[]{:S(2)}) collective-permute-start(bf16[528,128]{1,0:T(8,128)(2,1)S(1)} %collective-permute-done.8.refs_2_), channel_id=1, source_target_pairs={{0,2},{1,3},{2,0},{3,1},{4,6},{5,7},{6,4},{7,5},{8,10},{9,11},{10,... | collective-permute-start | bytes 405512 | tf_op jit(solution)/shard_map/ppermute | solution.py:572
  58.5 5.0 %collective-permute-start.14 = (bf16[128,1024]{1,0:T(8,128)(2,1)S(1)}, bf16[128,1024]{1,0:T(8,128)(2,1)S(1)}, u32[]{:S(2)}, u32[]{:S(2)}) collective-permute-start(bf16[128,1024]{1,0:T(8,128)(2,1)S(1)} %get-tuple-element.55), channel_id=1, source_target_pairs={{0,1},{1,0},{2,3},{3,2},{4,5},{5,4},{6,7},{7,6},{8,9},{9,8},{10,11... | collective-permute-start | bytes 786440 | tf_op jit(solution)/shard_map/ppermute | solution.py:572
  62.3 1.5 %collective-permute-start.9 = (bf16[128,1024]{1,0:T(8,128)(2,1)S(1)}, bf16[128,1024]{1,0:T(8,128)(2,1)S(1)}, u32[]{:S(2)}, u32[]{:S(2)}) collective-permute-start(bf16[128,1024]{1,0:T(8,128)(2,1)S(1)} %get-tuple-element.52), channel_id=1, source_target_pairs={{0,1},{1,0},{2,3},{3,2},{4,5},{5,4},{6,7},{7,6},{8,9},{9,8},{10,11... | collective-permute-start | bytes 786440 | tf_op jit(solution)/shard_map/ppermute | solution.py:572
  63.5 0.7 %copy-start.2 = (bf16[128,1024]{1,0:T(8,128)(2,1)}, bf16[128,1024]{1,0:T(8,128)(2,1)S(1)}, u32[]{:S(2)}) copy-start(bf16[128,1024]{1,0:T(8,128)(2,1)S(1)} %collective-permute-done.14.d) | copy-start | bytes 786436
  63.9 0.7 %copy-start.3 = (bf16[128,1024]{1,0:T(8,128)(2,1)}, bf16[128,1024]{1,0:T(8,128)(2,1)S(1)}, u32[]{:S(2)}) copy-start(bf16[128,1024]{1,0:T(8,128)(2,1)S(1)} %collective-permute-done.9.c) | copy-start | bytes 786436

commit v2 on v0

--- a/solution.py
+++ b/solution.py
@@ -1,16 +1,486 @@
+import functools
 import math
 
 import jax
 import jax.numpy as jnp
 from jax import lax
+from jax.experimental import pallas as pl
+from jax.experimental.pallas import tpu as pltpu
 from jax.sharding import PartitionSpec as P
 
 QH = 32
 KVH = 4
 HD = 128
-
+PER = QH // KVH
+LOG2E = math.log2(math.e)
+INV_ROOT = 1.0 / math.sqrt(HD)
 
 masked_score = -1e30
+
+RUNS = 2
+BLK = 128
+PAIR = RUNS * BLK
+PIECE = 2 * PAIR + 16
+ROWS = 128
+WIDE = PER * ROWS
+BOTH = 2 * WIDE
+REF_ROW = HD
+SUM_ROW = HD + 8
+STATE = HD + 16
+POOL = 8
+META_J = 0
+META_LEN = 2 * POOL
+META_SUF = META_LEN + 1
+META_M = META_LEN + 2
+META_SIZE = 24
+TILE = 512
+NT = (((1,), (1,)), ((), ()))
+VMEM_LIMIT = 24 << 20
+BF16 = jnp.bfloat16
+F32 = jnp.float32
+IN_VMEM = pl.BlockSpec(memory_space=pltpu.VMEM)
+IN_SMEM = pl.BlockSpec(memory_space=pltpu.SMEM)
+IN_HBM = pl.BlockSpec(memory_space=pltpu.HBM)
+
+
+COST = pl.CostEstimate(flops=1 << 10, bytes_accessed=1 << 10, transcendentals=0)
+
+
+def write_scales(scales, locals_, head, dst):
+    col_at = lax.broadcasted_iota(jnp.int32, scales.shape, 0)
+    slot_at = lax.broadcasted_iota(jnp.int32, scales.shape, 1)
+    row = lax.broadcasted_iota(jnp.int32, (16, HD), 0)
+    rows = jnp.zeros((16, HD), F32)
+    for half in range(2):
+        for run in range(RUNS):
+            chosen = (slot_at == locals_[run]) & (col_at == half * KVH + head)
+            one = jnp.sum(jnp.where(chosen, scales, 0.0), axis=(0, 1), keepdims=True)
+            rows = jnp.where(row == half * RUNS + run, one, rows)
+    dst[pl.ds(2 * PAIR, 16), :] = rows.astype(BF16)
+
+
+def piece_copies(cache, locals_, head, dst, sems, first):
+    made = []
+    for half in range(2):
+        column = pl.multiple_of((half * KVH + head) * HD, HD)
+        for run in range(RUNS):
+            made.append(
+                pltpu.make_async_copy(
+                    cache.at[locals_[run], :, pl.ds(column, HD)],
+                    dst.at[pl.ds(half * PAIR + run * BLK, BLK), :],
+                    sems.at[first + 2 * half + run],
+                )
+            )
+    return made
+
+
+PIECE_1 = pltpu.VMEM((PIECE, HD), BF16)
+PIECE_2 = pltpu.VMEM((2, PIECE, HD), BF16)
+SWAP = WIDE + 2 * HD
+
+
+def gather_kernel(ids, queries, suffix_kv, cache, *refs):
+    loads = list(zip(refs[:5], refs[17:22]))
+    meta, swap = refs[5:7]
+    far, near, own = refs[7:11], refs[11:14], refs[14]
+    own_q, own_kv = refs[15:17]
+    table, groups, lengths, suffixes, cache_scale = refs[17:22]
+    table_sems, more_sems, sems = refs[22:]
+    p = ids[0]
+    m = ids[1]
+    loads = [
+        pltpu.make_async_copy(a, b, table_sems.at[i]) for i, (a, b) in enumerate(loads)
+    ]
+    for c in loads:
+        c.start()
+    made = []
+    for slot in range(2):
+        mine = m ^ (2 * slot)
+        theirs = mine ^ 1
+        jobs = [
+            (queries, theirs * WIDE, WIDE, swap.at[slot, :, pl.ds(0, WIDE)]),
+            (suffix_kv, theirs * HD, HD, swap.at[slot, :, pl.ds(WIDE, HD)]),
+            (suffix_kv, (KVH + theirs) * HD, HD, swap.at[slot, :, pl.ds(WIDE + HD, HD)]),
+            (queries, mine * WIDE, WIDE, own_q.at[slot]),
+            (suffix_kv, mine * HD, HD, own_kv.at[slot, pl.ds(0, ROWS), :]),
+            (suffix_kv, (KVH + mine) * HD, HD, own_kv.at[slot, pl.ds(ROWS, ROWS), :]),
+        ]
+        for src, at, width, dst in jobs:
+            src = src.at[:, pl.ds(pl.multiple_of(at, HD), width)]
+            c = pltpu.make_async_copy(src, dst, more_sems.at[len(made)])
+            c.start()
+            made.append(c)
+    for c in loads:
+        c.wait()
+    meta[META_M] = m
+    slot_count = cache.shape[0]
+    low = p * slot_count
+    jobs = [(4 + i, (0,), (ref,)) for i, ref in enumerate(far)]
+    jobs += [(1 + i, (0, 1), (ref.at[0], ref.at[1])) for i, ref in enumerate(near)]
+    jobs += [(0, (0, 1), (own.at[0], own.at[1]))]
+    pending = []
+    count = 0
+    for k, slots, outs in jobs:
+        session = groups[p ^ k]
+        locals_ = []
+        for run in range(RUNS):
+            local = jnp.int32(0)
+            for jj in range(POOL):
+                at = table[session, run * POOL + jj] - low
+                local = jnp.where((at >= 0) & (at < slot_count), at, local)
+            locals_.append(local)
+        for slot, out in zip(slots, outs):
+            group = piece_copies(cache, locals_, m ^ (2 * slot), out, sems, count)
+            count += 4
+            for c in group:
+                c.start()
+            made += group
+            pending.append((locals_, m ^ (2 * slot), out))
+    mine = groups[p]
+    for run in range(RUNS):
+        for jj in range(POOL):
+            at = run * POOL + jj
+            meta[META_J + RUNS * ((table[mine, at] // slot_count) ^ p) + run] = at
+    meta[META_LEN] = lengths[mine]
+    meta[META_SUF] = suffixes[mine]
+    scales = cache_scale[...].astype(F32)
+    for locals_, head, out in pending:
+        write_scales(scales, locals_, head, out)
+    for c in made:
+        c.wait()
+
+
+def gather_call(ids, queries, suffix_kv, cache, tables, cache_scale):
+    return pl.pallas_call(
+        gather_kernel,
+        out_shape=[
+            jax.ShapeDtypeStruct((META_SIZE,), jnp.int32),
+            pltpu.VMEM((2, ROWS, SWAP), BF16),
+        ]
+        + [PIECE_1] * 4
+        + [PIECE_2] * 4
+        + [pltpu.VMEM((2, ROWS, WIDE), BF16), pltpu.VMEM((2, 2 * ROWS, HD), BF16)],
+        in_specs=[IN_SMEM] + [IN_HBM] * 8,
+        out_specs=[IN_SMEM] + [IN_VMEM] * 11,
+        scratch_shapes=[pltpu.SMEM(x.shape, jnp.int32) for x in tables]
+        + [
+            pltpu.VMEM(cache_scale.shape, cache_scale.dtype),
+            pltpu.SemaphoreType.DMA((5,)),
+            pltpu.SemaphoreType.DMA((12,)),
+            pltpu.SemaphoreType.DMA((48,)),
+        ],
+        compiler_params=pltpu.CompilerParams(vmem_limit_bytes=VMEM_LIMIT),
+        cost_estimate=COST,
+    )(ids, queries, suffix_kv, cache, *tables, cache_scale)
+
+
+def wide(row):
+    return jnp.concatenate([row] * (TILE // HD), axis=1)
+
+
+def terms(tile, run):
+    key = tile[run : run + 1]
+    value = tile[RUNS + run : RUNS + run + 1]
+    return wide(key * (LOG2E * INV_ROOT)), wide(jnp.log2(value)), wide(1.0 / value)
+
+
+UNIT = None
+
+
+def fold(q, keys, values_t, before, after, blocks_of):
+    tiles = BOTH // TILE
+
+    def score(t):
+        return lax.dot_general(
+            keys, q[pl.ds(t * TILE, TILE), :], NT, preferred_element_type=F32
+        )
+
+    following = score(0)
+    for t in range(tiles):
+        scores = following
+        if t + 1 < tiles:
+            following = score(t + 1)
+        cols = pl.ds(t * TILE, TILE)
+        blocks = blocks_of(t)
+        old = jnp.full((1, TILE), masked_score, F32) if before is None else before[REF_ROW : REF_ROW + 1, cols]
+        parts = []
+        reference = old
+        for b, (term, dead, mask) in enumerate(blocks):
+            part = scores[b * BLK : (b + 1) * BLK]
+            part = part if mask is None else jnp.where(mask, part, masked_score)
+            parts.append(part)
+            top = jnp.max(part, axis=0, keepdims=True)
+            top = top * (LOG2E * INV_ROOT) if term is UNIT else top * term[0]
+            if dead is not None:
+                top = jnp.where(dead, masked_score, top)
+            reference = jnp.maximum(reference, top)
+        if before is None:
+            total = jnp.zeros((1, TILE), F32)
+        else:
+            factor = jnp.exp2(old - reference)
+            total = before[SUM_ROW : SUM_ROW + 1, cols] * factor
+        rounded = []
+        for part, (term, dead, mask) in zip(parts, blocks):
+            shift = reference if term is UNIT else reference - term[1]
+            if dead is not None:
+                shift = jnp.where(dead, -masked_score, shift)
+            scaled = part * (LOG2E * INV_ROOT) if term is UNIT else part * term[0]
+            weights = jnp.exp2(scaled - shift)
+            if mask is not None:
+                weights = jnp.where(mask, weights, 0.0)
+            summed = jnp.sum(weights, axis=0, keepdims=True)
+            total = total + (summed if term is UNIT else summed * term[2])
+            rounded.append(weights.astype(BF16))
+        rounded = jnp.concatenate(rounded, axis=0) if len(rounded) > 1 else rounded[0]
+        product = jnp.dot(values_t, rounded, preferred_element_type=F32)
+        after[:HD, cols] = product if before is None else before[:HD, cols] * factor + product
+        after[REF_ROW : REF_ROW + 1, cols] = reference
+        after[SUM_ROW : SUM_ROW + 1, cols] = total
+
+
+def add_pieces(q, before, after, pieces, ks, meta, extra=None):
+    m = meta[META_M]
+    n = len(ks)
+    reach = jnp.where(((m // 2) * 2) * ROWS < meta[META_SUF], meta[META_LEN], 0)
+    counts = [
+        jnp.clip(reach - meta[META_J + RUNS * k + r] * BLK, 0, BLK) for k in ks for r in range(RUNS)
+    ]
+    most = functools.reduce(jnp.maximum, counts)
+
+    def whole():
+        blocks = []
+        for i in range(n):
+            tile = pieces[i, 2 * PAIR :, :].astype(F32)
+            blocks += [(terms(tile, r), counts[RUNS * i + r] < BLK, None) for r in range(RUNS)]
+        keys = [pieces[i, :PAIR, :] for i in range(n)]
+        values = [pieces[i, PAIR : 2 * PAIR, :].T for i in range(n)]
+        blocks_of = lambda t: blocks
+        if extra is not None:
+            keys = [extra[0]] + keys
+            values = [extra[1]] + values
+            blocks_of = lambda t: extra[2](t) + blocks
+        keys = jnp.concatenate(keys, axis=0) if len(keys) > 1 else keys[0]
+        values = jnp.concatenate(values, axis=1) if len(values) > 1 else values[0]
+        fold(q, keys, values, before, after, blocks_of)
+
+    if extra is not None:
+        whole()
+    else:
+
+        @pl.when(most < BLK)
+        def _():
+            after[...] = before[...]
+
+        pl.when(most == BLK)(whole)
+
+    part = jnp.int32(-1)
+    count = jnp.int32(0)
+    for at, c in enumerate(counts):
+        hit = (c > 0) & (c < BLK)
+        part = jnp.where(hit, at, part)
+        count = jnp.where(hit, c, count)
+
+    @pl.when(part >= 0)
+    def _():
+        i = part // RUNS
+        run = part % RUNS
+        tile = pieces[i, 2 * PAIR :, :].astype(F32)
+        term = [jnp.where(run == 1, b, a) for a, b in zip(terms(tile, 0), terms(tile, 1))]
+        mask = lax.broadcasted_iota(jnp.int32, (BLK, TILE), 0) < count
+        at = pl.multiple_of(run * BLK, BLK)
+        fold(
+            q,
+            pieces[i, pl.ds(at, BLK), :],
+            pieces[i, pl.ds(PAIR + at, BLK), :].T,
+            after,
+            after,
+            lambda t: [(term, None, mask)],
+        )
+
+
+def state_shapes(slots):
+    return [pltpu.VMEM((STATE, BOTH), F32)] * slots
+
+
+def own_kernel(meta, swap, own, own_q, own_kv, kv, q_all, *states):
+    m = meta[META_M]
+    for slot in range(2):
+        for h in range(PER):
+            rows = pl.ds(h * ROWS, ROWS)
+            others = pl.ds(WIDE + h * ROWS, ROWS)
+            q_all[slot, rows, :] = own_q[slot, :, h * HD : (h + 1) * HD]
+            q_all[slot, others, :] = swap[slot, :, h * HD : (h + 1) * HD]
+        kv[slot, 0] = own_kv[slot]
+        kv[slot, 1, :ROWS, :] = swap[slot, :, WIDE : WIDE + HD]
+        kv[slot, 1, ROWS:, :] = swap[slot, :, WIDE + HD :]
+    key = lax.broadcasted_iota(jnp.int32, (BLK, TILE), 0)
+    row = lax.broadcasted_iota(jnp.int32, (BLK, TILE), 1) % ROWS
+    causal = key <= row
+    odd = (m % 2) == 1
+
+    def blocks_of(t):
+        if t * TILE < WIDE:
+            return [(UNIT, None, causal), (UNIT, jnp.logical_not(odd), None)]
+        return [(UNIT, odd, None), (UNIT, None, causal)]
+
+    for slot in range(2):
+        keys = jnp.concatenate([kv[slot, side, :ROWS] for side in range(2)], axis=0)
+        values = jnp.concatenate([kv[slot, side, ROWS:].T for side in range(2)], axis=1)
+        add_pieces(
+            q_all.at[slot],
+            None,
+            states[slot],
+            own.at[pl.ds(slot, 1)],
+            (0,),
+            meta,
+            (keys, values, blocks_of),
+        )
+
+
+def own_call(meta, swap, own, own_q, own_kv):
+    out = pl.pallas_call(
+        own_kernel,
+        out_shape=[pltpu.VMEM((2, 2, 2 * ROWS, HD), BF16), pltpu.VMEM((2, BOTH, HD), BF16)]
+        + state_shapes(2),
+        in_specs=[IN_SMEM] + [IN_VMEM] * 4,
+        out_specs=[IN_VMEM] * 4,
+        compiler_params=pltpu.CompilerParams(vmem_limit_bytes=VMEM_LIMIT),
+        cost_estimate=COST,
+    )(meta, swap, own, own_q, own_kv)
+    return out[0], out[1], out[2:]
+
+
+def add_kernel(slots, ks, early, last, meta, q_all, *refs):
+    refs = list(refs)
+    take = lambda n: [refs.pop(0) for _ in range(n)]
+    before = take(len(slots))
+    sources = take(len(ks))
+    kv_early = take(1)[0] if early else None
+    outs = take(2) if last else None
+    after = take(len(slots))
+    kv = take(1)[0]
+    for w, slot in enumerate(slots):
+        for i, s in enumerate(sources):
+            kv[w, i] = s[slot] if len(s.shape) == 3 else s[...]
+        extra = None
+        if early:
+            unused = meta[META_M] < 2
+            extra = (
+                jnp.concatenate([kv_early[1 - slot, side, :ROWS] for side in range(2)], axis=0),
+                jnp.concatenate([kv_early[1 - slot, side, ROWS:].T for side in range(2)], axis=1),
+                lambda t: [(UNIT, unused, None)] * 2,
+            )
+        add_pieces(q_all.at[slot], before[w], after[w], kv.at[w], ks, meta, extra)
+    if last:
+        state = after[0]
+        for side, out in enumerate(outs):
+            member = meta[META_M] ^ side
+            row = lax.broadcasted_iota(jnp.int32, (HD, ROWS), 1) + member * ROWS
+            for i in range(PER):
+                cols = pl.ds(side * WIDE + i * ROWS, ROWS)
+                piece = state[:HD, cols] * (1.0 / state[SUM_ROW : SUM_ROW + 1, cols])
+                piece = jnp.where(row < meta[META_SUF], piece, 0.0).astype(BF16)
+                out[:, i * HD : (i + 1) * HD] = piece.T
+
+
+def add_call(meta, q_all, states, sources, slots, ks, early=None, last=False):
+    flat = [states[s] for s in slots]
+    n = len(ks)
+    args = [meta, q_all, *flat, *sources] + ([] if early is None else [early])
+    scratch = [pltpu.VMEM((len(slots), n, PIECE, HD), BF16)]
+    if last:
+        out_shape = [pltpu.VMEM((ROWS, WIDE), BF16)] * 2
+        scratch = state_shapes(1) + scratch
+    else:
+        out_shape = state_shapes(len(slots))
+    out = pl.pallas_call(
+        functools.partial(add_kernel, slots, ks, early is not None, last),
+        out_shape=out_shape,
+        in_specs=[IN_SMEM] + [IN_VMEM] * (len(args) - 1),
+        out_specs=[IN_VMEM] * len(out_shape),
+        scratch_shapes=scratch,
+        compiler_params=pltpu.CompilerParams(vmem_limit_bytes=VMEM_LIMIT),
+        cost_estimate=COST,
+    )(*args)
+    if last:
+        return out
+    states = list(states)
+    for w, slot in enumerate(slots):
+        states[slot] = out[w]
+    return states
+
+
+def join_kernel(meta, *refs):
+    out, sems = refs[4:]
+    made = []
+    for i, src in enumerate(refs[:4]):
+        head = meta[META_M] ^ (2 * (i % 2) + i // 2)
+        column = pl.multiple_of(head * WIDE, WIDE)
+        made.append(pltpu.make_async_copy(src, out.at[:, pl.ds(column, WIDE)], sems.at[i]))
+        made[-1].start()
+    for x in made:
+        x.wait()
+
+
+def join_call(meta, mine, yours):
+    return pl.pallas_call(
+        join_kernel,
+        out_shape=jax.ShapeDtypeStruct((ROWS, QH * HD), BF16),
+        in_specs=[IN_SMEM] + [IN_VMEM] * 4,
+        out_specs=IN_HBM,
+        scratch_shapes=[pltpu.SemaphoreType.DMA((4,))],
+        cost_estimate=COST,
+    )(meta, *mine, *yours)
+
+
+def permute(x, axis, count, k):
+    return lax.ppermute(x, axis, [(i, i ^ k) for i in range(count)])
+
+
+def per_device_small(
+    queries, suffix_kv, cache, cache_scale, prefix_len, suffix_len, block_table, session_group
+):
+    ids = jnp.stack([lax.axis_index("pool"), lax.axis_index("blk")]).astype(jnp.int32)
+    tables = [block_table, session_group, prefix_len, suffix_len]
+    queries, suffix_kv, cache, scale, *tables = [
+        pltpu.with_memory_space_constraint(x, pltpu.HBM)
+        for x in (queries, suffix_kv, cache, cache_scale.T, *tables)
+    ]
+    meta, swap, *parts = gather_call(ids, queries, suffix_kv, cache, tables, scale)
+    far, near = parts[:4], parts[4:7]
+    own, own_q, own_kv = parts[7:]
+    far_in, near_in, across = {}, {}, {}
+    swap_in = permute(swap, "blk", 4, 1)
+    for k in (4, 5):
+        far_in[k] = permute(far[k - 4], "pool", POOL, k)
+    for k in (1, 2):
+        near_in[k] = permute(near[k - 1], "pool", POOL, k)
+    kv, q_all, states = own_call(meta, swap_in, own, own_q, own_kv)
+    far[2], near[2], kv, states = lax.optimization_barrier((far[2], near[2], kv, states))
+    far_in[6] = permute(far[2], "pool", POOL, 6)
+    near_in[3] = permute(near[2], "pool", POOL, 3)
+    early = permute(kv, "blk", 4, 2)
+    states = add_call(meta, q_all, states, [near_in[1], near_in[2]], (0, 1), (1, 2))
+    far[3], far_in[4], far_in[5], states = lax.optimization_barrier(
+        (far[3], far_in[4], far_in[5], states)
+    )
+    far_in[7] = permute(far[3], "pool", POOL, 7)
+    for k in (4, 5):
+        across[k] = permute(far_in[k], "blk", 4, 2)
+    states = add_call(meta, q_all, states, [near_in[3]], (0, 1), (3,), early=early)
+    far_in[6], far_in[7], states = lax.optimization_barrier((far_in[6], far_in[7], states))
+    for k in (6, 7):
+        across[k] = permute(far_in[k], "blk", 4, 2)
+    states = add_call(meta, q_all, states, [far_in[4], far_in[5]], (0,), (4, 5))
+    states = add_call(meta, q_all, states, [across[4], across[5]], (1,), (4, 5))
+    mine, yours = [], []
+    for slot, source in ((0, far_in), (1, across)):
+        a, b = add_call(meta, q_all, states, [source[6], source[7]], (slot,), (6, 7), last=True)
+        mine.append(a)
+        yours.append(
+            pltpu.with_memory_space_constraint(permute(b, "blk", 4, 1), pltpu.VMEM)
+        )
+    return join_call(meta, mine, yours)
 
 
 def fold_keys(running, query_heads, key_rows, value_rows, key_scale, value_scale, usable):
@@ -29,7 +499,7 @@
     return (new_highest, weight_sum, weighted)
 
 
-def per_device(
+def per_device_any(
     queries, suffix_kv, cache, cache_scale, prefix_len, suffix_len, block_table, session_group
 ):
     local_rows = queries.shape[0]
@@ -126,8 +596,9 @@
 
 
 def solution(mesh):
+    small = dict(mesh.shape) == {"pool": POOL, "blk": 4}
     return jax.shard_map(
-        per_device,
+        per_device_small if small else per_device_any,
         mesh=mesh,
         in_specs=(
             P(("pool", "blk"), None),

time: 143 us -> 53.7 us (0.38)
  matrix products: 31.7 us -> 0 us
  Pallas kernels: 0 us -> 29.9 us
  waiting for transfers between devices: 36.8 us -> 8.38 us
  local copies, waits for them, and re-layouts: 24.7 us -> 0.7 us
  other arithmetic: 22.5 us -> 0.07 us
  between operations: 13.6 us -> 0.33 us
  starting transfers between devices: 12.4 us -> 14.3 us
    dot_general x6 -> x0, matrix products: 31.7 us -> none  [the longest x3 24 us: fold_keys(): jnp.einsum('kgrn,nkd->kgrd', rounded, value_rows, preferred_element_type=...]
    pallas_call x0 -> x9, Pallas kernels: none -> 29.9 us  [the longest x6 19.2 us: add_call(): pl.pallas_call(functools.partial(add_kernel, slots, ks, early is not None...]
    all_to_all x2 -> x0, waiting for transfers between devices: 22 us -> none  [the longest x1 22 us: per_device(): lax.all_to_all(outgoing, 'pool', split_axis=0, concat_axis=0, tiled=True)]
    reduce_sum x7 -> x0, other arithmetic: 14.9 us -> none  [the longest x3 13 us: fold_keys(): weight_sum = weight_sum * factor + jnp.sum(weights, axis=3)]
    all_gather x2 -> x0, waiting for transfers between devices: 14.8 us -> none  [the longest x1 14.8 us: per_device(): arrived = lax.all_gather(arrived_part, 'blk', axis=3, tiled=True)]
    ppermute x0 -> x15, starting transfers between devices: none -> 14.3 us  [permute(): return lax.ppermute(x, axis, [(i, i ^ k) for i in range(count)])]
    all_to_all x2 -> x0, starting transfers between devices: 12.3 us -> none  [the longest x1 6.63 us: per_device(): lax.all_to_all(scale_rows, 'pool', split_axis=0, concat_axis=0, tiled=True)]
    ppermute x0 -> x15, waiting for transfers between devices: none -> 8.38 us  [permute(): return lax.ppermute(x, axis, [(i, i ^ k) for i in range(count)])]
  transfers between devices with their start and end apart: 4 -> 15, of which waited for: 2 -> 4; matrix products, arithmetic and copies ran while one was open for 12% -> 0% of each run, Pallas kernels for 0% -> 44%
where the time goes in v2:
time: 53.7 us; the launch traced here: 53.6 us
  Pallas kernels  29.9 us (56%)
  starting transfers between devices  14.3 us (27%)
  waiting for transfers between devices  8.38 us (16%)
  local copies, waits for them, and re-layouts  0.7 us (1%)
    pallas_call x6, Pallas kernels, add_call(): pl.pallas_call(functools.partial(add_kernel, slots, ks, early is not None...  19.2 us
    ppermute x15, starting transfers between devices, permute(): return lax.ppermute(x, axis, [(i, i ^ k) for i in range(count)])  14.3 us
    ppermute x15, waiting for transfers between devices, permute(): return lax.ppermute(x, axis, [(i, i ^ k) for i in range(count)])  8.38 us
    pallas_call x1, Pallas kernels, gather_call(): pl.pallas_call(gather_kernel, out_shape=[jax.ShapeDtypeStruct((META_SIZE,...  4.42 us
    pallas_call x1, Pallas kernels, own_call(): pl.pallas_call(own_kernel, out_shape=[pltpu.VMEM((2, 2, 2 * ROWS, HD), BF...  4.2 us
    pallas_call x1, Pallas kernels, join_call(): pl.pallas_call(join_kernel, out_shape=jax.ShapeDtypeStruct((ROWS, QH * HD...  2.04 us
  transfers between devices with their start and end apart: 15, of which 4 were waited for; matrix products, arithmetic and copies ran while one was open for 0% of the time, Pallas kernels for 44%

profile of v2, /device:TPU:9, one launch (start us, length us, event | category | flops | bytes accessed | tf_op | source)
XLA Modules:
  0.0 53.6 jit_solution(10683738240279594987)
XLA Ops:
  0.1 4.4 %shard_map.82 = (s32[24]{0:T(128)S(1)}, bf16[2,128,1280]{2,1,0:T(8,128)(2,1)S(1)}, bf16[528,128]{1,0:T(8,128)(2,1)S(1)}, bf16[528,128]{1,0:T(8,128)(2,1)S(1)}, b...) custom-call(s32[2]{0:T(128)S(1)} %pad_add_fusion.ids, ...), custom_call_target="tpu_custom_call" | custom-call | flops 1024 | bytes 1024 | tf_op jit(solution)/shard_map/pallas_call | solution.py:154
  4.5 0.7 %collective-permute-start = (bf16[2,128,1280]{2,1,0:T(8,128)(2,1)S(1)}, bf16[2,128,1280]{2,1,0:T(8,128)(2,1)S(1)}, u32[]{:S(2)}, u32[]{:S(2)}) collective-permute-start(bf16[2,128,1280]{2,1,0:T(8,128)(2,1)S(1)} %get-tuple-element.44), channel_id=1, source_target_pairs={{0,1},{1,0},{2,3},{3,2},{4,5},{5,4},{6,7},{7,6},{8,9},{9,8},{10,11... | collective-permute-start | bytes 1966088 | tf_op jit(solution)/shard_map/ppermute | solution.py:437
  5.3 1.2 %collective-permute-start.4 = (bf16[2,528,128]{2,1,0:T(8,128)(2,1)S(1)}, bf16[2,528,128]{2,1,0:T(8,128)(2,1)S(1)}, u32[]{:S(2)}, u32[]{:S(2)}) collective-permute-start(bf16[2,528,128]{2,1,0:T(8,128)(2,1)S(1)} %get-tuple-element.60), channel_id=1, source_target_pairs={{0,4},{4,0},{8,12},{12,8},{16,20},{20,16},{24,28},{28,24},{1,5},{5... | collective-permute-start | bytes 811016 | tf_op jit(solution)/shard_map/ppermute | solution.py:437
  6.7 2.3 %collective-permute-start.2 = (bf16[528,128]{1,0:T(8,128)(2,1)S(1)}, bf16[528,128]{1,0:T(8,128)(2,1)S(1)}, u32[]{:S(2)}, u32[]{:S(2)}) collective-permute-start(bf16[528,128]{1,0:T(8,128)(2,1)S(1)} %get-tuple-element.56), channel_id=1, source_target_pairs={{0,16},{4,20},{8,24},{12,28},{16,0},{20,4},{24,8},{28,12},{1,17},{... | collective-permute-start | bytes 405512 | tf_op jit(solution)/shard_map/ppermute | solution.py:437
  9.0 4.2 %shard_map.83 = (bf16[2,2,256,128]{3,2,1,0:T(8,128)(2,1)S(1)}, bf16[2,2048,128]{2,1,0:T(8,128)(2,1)S(1)}, f32[144,2048]{1,0:T(8,128)S(1)}, f32[144,2048]{1,0:T(8,128)S(1)}) custom-call(s32[24]{0:T(128)S(1)} %get-tuple-element.43.meta, bf16[2,128,1280]{2,1,0:T(8,128)(2,1)S(1)} %collective-permute-done.swap, bf16[2,528,128]{2,1,0:T(8,128)(2,1)S(1)} %get-tuple-element.45.own, ...), custom_call_target="tpu_custom_call" | custom-call | flops 1024 | bytes 1024 | tf_op jit(solution)/shard_map/pallas_call | solution.py:341
  13.2 2.3 %collective-permute-start.7 = (bf16[2,528,128]{2,1,0:T(8,128)(2,1)S(1)}, bf16[2,528,128]{2,1,0:T(8,128)(2,1)S(1)}, u32[]{:S(2)}, u32[]{:S(2)}) collective-permute-start(bf16[2,528,128]{2,1,0:T(8,128)(2,1)S(1)} %get-tuple-element.67), channel_id=1, source_target_pairs={{0,12},{4,8},{8,4},{12,0},{16,28},{20,24},{24,20},{28,16},{1,13},{... | collective-permute-start | bytes 811016 | tf_op jit(solution)/shard_map/ppermute | solution.py:437
  15.5 1.2 %collective-permute-start.8 = (bf16[2,2,256,128]{3,2,1,0:T(8,128)(2,1)S(1)}, bf16[2,2,256,128]{3,2,1,0:T(8,128)(2,1)S(1)}, u32[]{:S(2)}, u32[]{:S(2)}) collective-permute-start(bf16[2,2,256,128]{3,2,1,0:T(8,128)(2,1)S(1)} %get-tuple-element.68), channel_id=1, source_target_pairs={{0,2},{1,3},{2,0},{3,1},{4,6},{5,7},{6,4},{7,5},{8,10},{9,11},{10,... | collective-permute-start | bytes 786440 | tf_op jit(solution)/shard_map/ppermute | solution.py:437
  16.7 1.1 %collective-permute-done.5.refs_3_ = bf16[2,528,128]{2,1,0:T(8,128)(2,1)S(1)} collective-permute-done((bf16[2,528,128]{2,1,0:T(8,128)(2,1)S(1)}, bf16[2,528,128]{2,1,0:T(8,128)(2,1)S(1)}, u32[]{:S(2)}, u32[]{:S(2)}) %collective-permute-start.5) | collective-permute-done | bytes 270368 | tf_op jit(solution)/shard_map/ppermute | solution.py:437
  17.9 1.3 %collective-permute-start.1 = (bf16[528,128]{1,0:T(8,128)(2,1)S(1)}, bf16[528,128]{1,0:T(8,128)(2,1)S(1)}, u32[]{:S(2)}, u32[]{:S(2)}) collective-permute-start(bf16[528,128]{1,0:T(8,128)(2,1)S(1)} %get-tuple-element.54), channel_id=1, source_target_pairs={{0,24},{4,28},{8,16},{12,20},{16,8},{20,12},{24,0},{28,4},{1,25},{... | collective-permute-start | bytes 405512 | tf_op jit(solution)/shard_map/ppermute | solution.py:437
  19.2 4.1 %shard_map.84 = (f32[144,2048]{1,0:T(8,128)S(1)}, f32[144,2048]{1,0:T(8,128)S(1)}) custom-call(s32[24]{0:T(128)S(1)} %get-tuple-element.43.meta, bf16[2,2048,128]{2,1,0:T(8,128)(2,1)S(1)} %get-tuple-element.48.q_all, f32[144,2048]{1,0:T(8,128)S(1)} %get-tuple-element.58.refs_0_, f32[144,2048]{1,0:T(8,128)S(1)} %get-tuple-element.59.refs_1_, ...), custom_call_target="tpu_custom_call" | custom-call | flops 1024 | bytes 1024 | tf_op jit(solution)/shard_map/pallas_call | solution.py:396
  23.4 1.3 %collective-permute-start.9 = (bf16[528,128]{1,0:T(8,128)(2,1)S(1)}, bf16[528,128]{1,0:T(8,128)(2,1)S(1)}, u32[]{:S(2)}, u32[]{:S(2)}) collective-permute-start(bf16[528,128]{1,0:T(8,128)(2,1)S(1)} %collective-permute-done.2.refs_1_), channel_id=1, source_target_pairs={{0,2},{1,3},{2,0},{3,1},{4,6},{5,7},{6,4},{7,5},{8,10},{9,11},{10,... | collective-permute-start | bytes 405512 | tf_op jit(solution)/shard_map/ppermute | solution.py:437
  24.7 0.2 collective-permute-start.10
  24.9 1.9 %collective-permute-done.7.refs_2_ = bf16[2,528,128]{2,1,0:T(8,128)(2,1)S(1)} collective-permute-done((bf16[2,528,128]{2,1,0:T(8,128)(2,1)S(1)}, bf16[2,528,128]{2,1,0:T(8,128)(2,1)S(1)}, u32[]{:S(2)}, u32[]{:S(2)}) %collective-permute-start.7) | collective-permute-done | bytes 270368 | tf_op jit(solution)/shard_map/ppermute | solution.py:437
  26.8 4.1 %shard_map.85 = (f32[144,2048]{1,0:T(8,128)S(1)}, f32[144,2048]{1,0:T(8,128)S(1)}) custom-call(s32[24]{0:T(128)S(1)} %get-tuple-element.43.meta, bf16[2,2048,128]{2,1,0:T(8,128)(2,1)S(1)} %get-tuple-element.48.q_all, f32[144,2048]{1,0:T(8,128)S(1)} %get-tuple-element.65.refs_0_, f32[144,2048]{1,0:T(8,128)S(1)} %get-tuple-element.66.refs_1_, ...), custom_call_target="tpu_custom_call" | custom-call | flops 1024 | bytes 1024 | tf_op jit(solution)/shard_map/pallas_call | solution.py:396
  30.9 3.8 %collective-permute-done.6.refs_2_ = bf16[528,128]{1,0:T(8,128)(2,1)S(1)} collective-permute-done((bf16[528,128]{1,0:T(8,128)(2,1)S(1)}, bf16[528,128]{1,0:T(8,128)(2,1)S(1)}, u32[]{:S(2)}, u32[]{:S(2)}) %collective-permute-start.6) | collective-permute-done | bytes 135200 | tf_op jit(solution)/shard_map/ppermute | solution.py:437
  34.7 1.2 %collective-permute-start.11 = (bf16[528,128]{1,0:T(8,128)(2,1)S(1)}, bf16[528,128]{1,0:T(8,128)(2,1)S(1)}, u32[]{:S(2)}, u32[]{:S(2)}) collective-permute-start(bf16[528,128]{1,0:T(8,128)(2,1)S(1)} %collective-permute-done.1.refs_1_), channel_id=1, source_target_pairs={{0,2},{1,3},{2,0},{3,1},{4,6},{5,7},{6,4},{7,5},{8,10},{9,11},{10,... | collective-permute-start | bytes 405512 | tf_op jit(solution)/shard_map/ppermute | solution.py:437
  36.2 3.1 %shard_map.86.refs_0_ = f32[144,2048]{1,0:T(8,128)S(1)} custom-call(s32[24]{0:T(128)S(1)} %get-tuple-element.43.meta, bf16[2,2048,128]{2,1,0:T(8,128)(2,1)S(1)} %get-tuple-element.48.q_all, f32[144,2048]{1,0:T(8,128)S(1)} %get-tuple-element.71.refs_0_, bf16[528,128]{1,0:T(8,128)(2,1)S(1)} %collective-permute-done.2.refs_1_, ...), custom_call_target="tpu_custom_call" | custom-call | flops 1024 | bytes 1024 | tf_op jit(solution)/shard_map/pallas_call | solution.py:396
  39.3 2.4 %shard_map.87 = (bf16[128,1024]{1,0:T(8,128)(2,1)S(1)}, bf16[128,1024]{1,0:T(8,128)(2,1)S(1)}) custom-call(s32[24]{0:T(128)S(1)} %get-tuple-element.43.meta, bf16[2,2048,128]{2,1,0:T(8,128)(2,1)S(1)} %get-tuple-element.48.q_all, f32[144,2048]{1,0:T(8,128)S(1)} %shard_map.86.refs_0_, bf16[528,128]{1,0:T(8,128)(2,1)S(1)} %collective-permute-done.1.refs_1_, ...), custom_call_target="tpu_custom_call" | custom-call | flops 1024 | bytes 1024 | tf_op jit(solution)/shard_map/pallas_call | solution.py:396
  41.7 1.9 %collective-permute-start.13 = (bf16[128,1024]{1,0:T(8,128)(2,1)S(1)}, bf16[128,1024]{1,0:T(8,128)(2,1)S(1)}, u32[]{:S(2)}, u32[]{:S(2)}) collective-permute-start(bf16[128,1024]{1,0:T(8,128)(2,1)S(1)} %get-tuple-element.79), channel_id=1, source_target_pairs={{0,1},{1,0},{2,3},{3,2},{4,5},{5,4},{6,7},{7,6},{8,9},{9,8},{10,11... | collective-permute-start | bytes 786440 | tf_op jit(solution)/shard_map/ppermute | solution.py:437
  43.6 3.1 %shard_map.88.refs_0_ = f32[144,2048]{1,0:T(8,128)S(1)} custom-call(s32[24]{0:T(128)S(1)} %get-tuple-element.43.meta, bf16[2,2048,128]{2,1,0:T(8,128)(2,1)S(1)} %get-tuple-element.48.q_all, f32[144,2048]{1,0:T(8,128)S(1)} %get-tuple-element.77.refs_0_, bf16[528,128]{1,0:T(8,128)(2,1)S(1)} %collective-permute-done.9.refs_1_, ...), custom_call_target="tpu_custom_call" | custom-call | flops 1024 | bytes 1024 | tf_op jit(solution)/shard_map/pallas_call | solution.py:396
  46.8 2.4 %shard_map.89 = (bf16[128,1024]{1,0:T(8,128)(2,1)S(1)}, bf16[128,1024]{1,0:T(8,128)(2,1)S(1)}) custom-call(s32[24]{0:T(128)S(1)} %get-tuple-element.43.meta, bf16[2,2048,128]{2,1,0:T(8,128)(2,1)S(1)} %get-tuple-element.48.q_all, f32[144,2048]{1,0:T(8,128)S(1)} %shard_map.88.refs_0_, bf16[528,128]{1,0:T(8,128)(2,1)S(1)} %collective-permute-done.11.refs_1_, ...), custom_call_target="tpu_custom_call" | custom-call | flops 1024 | bytes 1024 | tf_op jit(solution)/shard_map/pallas_call | solution.py:396
  49.2 0.7 %copy-done.1 = bf16[128,1024]{1,0:T(8,128)(2,1)} copy-done((bf16[128,1024]{1,0:T(8,128)(2,1)}, bf16[128,1024]{1,0:T(8,128)(2,1)S(1)}, u32[]{:S(2)}) %copy-start.1) | copy-done | bytes 262168
  49.9 1.5 %collective-permute-done.14.refs_3_ = bf16[128,1024]{1,0:T(8,128)(2,1)S(1)} collective-permute-done((bf16[128,1024]{1,0:T(8,128)(2,1)S(1)}, bf16[128,1024]{1,0:T(8,128)(2,1)S(1)}, u32[]{:S(2)}, u32[]{:S(2)}) %collective-permute-start.14) | collective-permute-done | bytes 262176 | tf_op jit(solution)/shard_map/ppermute | solution.py:437
  51.4 2.0 %shard_map.90 = bf16[128,4096]{1,0:T(8,128)(2,1)} custom-call(s32[24]{0:T(128)} %copy-done.2, bf16[128,1024]{1,0:T(8,128)(2,1)} %copy-done, bf16[128,1024]{1,0:T(8,128)(2,1)} %copy-done.1, bf16[128,1024]{1,0:T(8,128)(2,1)S(1)} %collective-permute-done.13.refs_2_, bf16[128,1024]{1,0:T(8,128)(2,1)S(1)} %collective-permute-done.14.refs_3_), custom_call_target="tpu_custom_call" | custom-call | flops 1024 | bytes 1024 | tf_op jit(solution)/shard_map/pallas_call | solution.py:426
  (22 shorter events, 0.6 us)
Async XLA Ops:
  4.5 42.2 %copy-start.2 = (s32[24]{0:T(128)}, s32[24]{0:T(128)S(1)}, u32[]{:S(2)}) copy-start(s32[24]{0:T(128)S(1)} %get-tuple-element.43.meta) | copy-start | bytes 292
  4.5 4.5 %collective-permute-start = (bf16[2,128,1280]{2,1,0:T(8,128)(2,1)S(1)}, bf16[2,128,1280]{2,1,0:T(8,128)(2,1)S(1)}, u32[]{:S(2)}, u32[]{:S(2)}) collective-permute-start(bf16[2,128,1280]{2,1,0:T(8,128)(2,1)S(1)} %get-tuple-element.44), channel_id=1, source_target_pairs={{0,1},{1,0},{2,3},{3,2},{4,5},{5,4},{6,7},{7,6},{8,9},{9,8},{10,11... | collective-permute-start | bytes 1966088 | tf_op jit(solution)/shard_map/ppermute | solution.py:437
  5.3 10.2 %collective-permute-start.4 = (bf16[2,528,128]{2,1,0:T(8,128)(2,1)S(1)}, bf16[2,528,128]{2,1,0:T(8,128)(2,1)S(1)}, u32[]{:S(2)}, u32[]{:S(2)}) collective-permute-start(bf16[2,528,128]{2,1,0:T(8,128)(2,1)S(1)} %get-tuple-element.60), channel_id=1, source_target_pairs={{0,4},{4,0},{8,12},{12,8},{16,20},{20,16},{24,28},{28,24},{1,5},{5... | collective-permute-start | bytes 811016 | tf_op jit(solution)/shard_map/ppermute | solution.py:437
  6.5 11.4 %collective-permute-start.5 = (bf16[2,528,128]{2,1,0:T(8,128)(2,1)S(1)}, bf16[2,528,128]{2,1,0:T(8,128)(2,1)S(1)}, u32[]{:S(2)}, u32[]{:S(2)}) collective-permute-start(bf16[2,528,128]{2,1,0:T(8,128)(2,1)S(1)} %get-tuple-element.61), channel_id=1, source_target_pairs={{0,8},{4,12},{8,0},{12,4},{16,24},{20,28},{24,16},{28,20},{1,9},{5... | collective-permute-start | bytes 811016 | tf_op jit(solution)/shard_map/ppermute | solution.py:437
  6.7 16.6 %collective-permute-start.2 = (bf16[528,128]{1,0:T(8,128)(2,1)S(1)}, bf16[528,128]{1,0:T(8,128)(2,1)S(1)}, u32[]{:S(2)}, u32[]{:S(2)}) collective-permute-start(bf16[528,128]{1,0:T(8,128)(2,1)S(1)} %get-tuple-element.56), channel_id=1, source_target_pairs={{0,16},{4,20},{8,24},{12,28},{16,0},{20,4},{24,8},{28,12},{1,17},{... | collective-permute-start | bytes 405512 | tf_op jit(solution)/shard_map/ppermute | solution.py:437
  9.0 14.3 %collective-permute-start.3 = (bf16[528,128]{1,0:T(8,128)(2,1)S(1)}, bf16[528,128]{1,0:T(8,128)(2,1)S(1)}, u32[]{:S(2)}, u32[]{:S(2)}) collective-permute-start(bf16[528,128]{1,0:T(8,128)(2,1)S(1)} %get-tuple-element.57), channel_id=1, source_target_pairs={{0,20},{4,16},{8,28},{12,24},{16,4},{20,0},{24,12},{28,8},{1,21},{... | collective-permute-start | bytes 405512 | tf_op jit(solution)/shard_map/ppermute | solution.py:437
  13.2 13.6 %collective-permute-start.7 = (bf16[2,528,128]{2,1,0:T(8,128)(2,1)S(1)}, bf16[2,528,128]{2,1,0:T(8,128)(2,1)S(1)}, u32[]{:S(2)}, u32[]{:S(2)}) collective-permute-start(bf16[2,528,128]{2,1,0:T(8,128)(2,1)S(1)} %get-tuple-element.67), channel_id=1, source_target_pairs={{0,12},{4,8},{8,4},{12,0},{16,28},{20,24},{24,20},{28,16},{1,13},{... | collective-permute-start | bytes 811016 | tf_op jit(solution)/shard_map/ppermute | solution.py:437
  15.5 9.2 %collective-permute-start.8 = (bf16[2,2,256,128]{3,2,1,0:T(8,128)(2,1)S(1)}, bf16[2,2,256,128]{3,2,1,0:T(8,128)(2,1)S(1)}, u32[]{:S(2)}, u32[]{:S(2)}) collective-permute-start(bf16[2,2,256,128]{3,2,1,0:T(8,128)(2,1)S(1)} %get-tuple-element.68), channel_id=1, source_target_pairs={{0,2},{1,3},{2,0},{3,1},{4,6},{5,7},{6,4},{7,5},{8,10},{9,11},{10,... | collective-permute-start | bytes 786440 | tf_op jit(solution)/shard_map/ppermute | solution.py:437
  17.9 13.1 %collective-permute-start.1 = (bf16[528,128]{1,0:T(8,128)(2,1)S(1)}, bf16[528,128]{1,0:T(8,128)(2,1)S(1)}, u32[]{:S(2)}, u32[]{:S(2)}) collective-permute-start(bf16[528,128]{1,0:T(8,128)(2,1)S(1)} %get-tuple-element.54), channel_id=1, source_target_pairs={{0,24},{4,28},{8,16},{12,20},{16,8},{20,12},{24,0},{28,4},{1,25},{... | collective-permute-start | bytes 405512 | tf_op jit(solution)/shard_map/ppermute | solution.py:437
  23.3 11.4 %collective-permute-start.6 = (bf16[528,128]{1,0:T(8,128)(2,1)S(1)}, bf16[528,128]{1,0:T(8,128)(2,1)S(1)}, u32[]{:S(2)}, u32[]{:S(2)}) collective-permute-start(bf16[528,128]{1,0:T(8,128)(2,1)S(1)} %get-tuple-element.64), channel_id=1, source_target_pairs={{0,28},{4,24},{8,20},{12,16},{16,12},{20,8},{24,4},{28,0},{1,29},{... | collective-permute-start | bytes 405512 | tf_op jit(solution)/shard_map/ppermute | solution.py:437
  23.4 20.3 %collective-permute-start.9 = (bf16[528,128]{1,0:T(8,128)(2,1)S(1)}, bf16[528,128]{1,0:T(8,128)(2,1)S(1)}, u32[]{:S(2)}, u32[]{:S(2)}) collective-permute-start(bf16[528,128]{1,0:T(8,128)(2,1)S(1)} %collective-permute-done.2.refs_1_), channel_id=1, source_target_pairs={{0,2},{1,3},{2,0},{3,1},{4,6},{5,7},{6,4},{7,5},{8,10},{9,11},{10,... | collective-permute-start | bytes 405512 | tf_op jit(solution)/shard_map/ppermute | solution.py:437
  24.7 19.0 %collective-permute-start.10 = (bf16[528,128]{1,0:T(8,128)(2,1)S(1)}, bf16[528,128]{1,0:T(8,128)(2,1)S(1)}, u32[]{:S(2)}, u32[]{:S(2)}) collective-permute-start(bf16[528,128]{1,0:T(8,128)(2,1)S(1)} %collective-permute-done.3.refs_2_), channel_id=1, source_target_pairs={{0,2},{1,3},{2,0},{3,1},{4,6},{5,7},{6,4},{7,5},{8,10},{9,11},{10,... | collective-permute-start | bytes 405512 | tf_op jit(solution)/shard_map/ppermute | solution.py:437
  34.7 12.0 %collective-permute-start.11 = (bf16[528,128]{1,0:T(8,128)(2,1)S(1)}, bf16[528,128]{1,0:T(8,128)(2,1)S(1)}, u32[]{:S(2)}, u32[]{:S(2)}) collective-permute-start(bf16[528,128]{1,0:T(8,128)(2,1)S(1)} %collective-permute-done.1.refs_1_), channel_id=1, source_target_pairs={{0,2},{1,3},{2,0},{3,1},{4,6},{5,7},{6,4},{7,5},{8,10},{9,11},{10,... | collective-permute-start | bytes 405512 | tf_op jit(solution)/shard_map/ppermute | solution.py:437
  35.9 10.8 %collective-permute-start.12 = (bf16[528,128]{1,0:T(8,128)(2,1)S(1)}, bf16[528,128]{1,0:T(8,128)(2,1)S(1)}, u32[]{:S(2)}, u32[]{:S(2)}) collective-permute-start(bf16[528,128]{1,0:T(8,128)(2,1)S(1)} %collective-permute-done.6.refs_2_), channel_id=1, source_target_pairs={{0,2},{1,3},{2,0},{3,1},{4,6},{5,7},{6,4},{7,5},{8,10},{9,11},{10,... | collective-permute-start | bytes 405512 | tf_op jit(solution)/shard_map/ppermute | solution.py:437
  41.7 5.0 %copy-start = (bf16[128,1024]{1,0:T(8,128)(2,1)}, bf16[128,1024]{1,0:T(8,128)(2,1)S(1)}, u32[]{:S(2)}) copy-start(bf16[128,1024]{1,0:T(8,128)(2,1)S(1)} %get-tuple-element.76.refs_0_) | copy-start | bytes 786436
  41.7 8.2 %collective-permute-start.13 = (bf16[128,1024]{1,0:T(8,128)(2,1)S(1)}, bf16[128,1024]{1,0:T(8,128)(2,1)S(1)}, u32[]{:S(2)}, u32[]{:S(2)}) collective-permute-start(bf16[128,1024]{1,0:T(8,128)(2,1)S(1)} %get-tuple-element.79), channel_id=1, source_target_pairs={{0,1},{1,0},{2,3},{3,2},{4,5},{5,4},{6,7},{7,6},{8,9},{9,8},{10,11... | collective-permute-start | bytes 786440 | tf_op jit(solution)/shard_map/ppermute | solution.py:437
  49.2 0.7 %copy-start.1 = (bf16[128,1024]{1,0:T(8,128)(2,1)}, bf16[128,1024]{1,0:T(8,128)(2,1)S(1)}, u32[]{:S(2)}) copy-start(bf16[128,1024]{1,0:T(8,128)(2,1)S(1)} %get-tuple-element.78.refs_1_) | copy-start | bytes 786436
  49.9 1.5 %collective-permute-start.14 = (bf16[128,1024]{1,0:T(8,128)(2,1)S(1)}, bf16[128,1024]{1,0:T(8,128)(2,1)S(1)}, u32[]{:S(2)}, u32[]{:S(2)}) collective-permute-start(bf16[128,1024]{1,0:T(8,128)(2,1)S(1)} %get-tuple-element.80), channel_id=1, source_target_pairs={{0,1},{1,0},{2,3},{3,2},{4,5},{5,4},{6,7},{7,6},{8,9},{9,8},{10,11... | collective-permute-start | bytes 786440 | tf_op jit(solution)/shard_map/ppermute | solution.py:437

commit v3 on v2

--- a/solution.py
+++ b/solution.py
@@ -33,8 +33,7 @@
 META_SUF = META_LEN + 1
 META_M = META_LEN + 2
 META_SIZE = 24
-TILE = 512
-NT = (((1,), (1,)), ((), ()))
+TILE = 1024
 VMEM_LIMIT = 24 << 20
 BF16 = jnp.bfloat16
 F32 = jnp.float32
@@ -46,15 +45,22 @@
 COST = pl.CostEstimate(flops=1 << 10, bytes_accessed=1 << 10, transcendentals=0)
 
 
-def write_scales(scales, locals_, head, dst):
-    col_at = lax.broadcasted_iota(jnp.int32, scales.shape, 0)
-    slot_at = lax.broadcasted_iota(jnp.int32, scales.shape, 1)
+def spread_scales(cache_scale, m, spread):
+    scales = cache_scale[...].astype(F32).T
+    column = lax.broadcasted_iota(jnp.int32, scales.shape, 1)
+    for slot in range(2):
+        for half in range(2):
+            chosen = jnp.where(column == half * KVH + (m ^ (2 * slot)), scales, 0.0)
+            one = jnp.sum(chosen, axis=1, keepdims=True)
+            spread[2 * slot + half] = jnp.broadcast_to(one, (scales.shape[0], HD))
+
+
+def write_scales(spread, locals_, slot, dst):
     row = lax.broadcasted_iota(jnp.int32, (16, HD), 0)
-    rows = jnp.zeros((16, HD), F32)
+    rows = jnp.ones((16, HD), F32)
     for half in range(2):
         for run in range(RUNS):
-            chosen = (slot_at == locals_[run]) & (col_at == half * KVH + head)
-            one = jnp.sum(jnp.where(chosen, scales, 0.0), axis=(0, 1), keepdims=True)
+            one = spread[2 * slot + half, pl.ds(locals_[run], 1), :]
             rows = jnp.where(row == half * RUNS + run, one, rows)
     dst[pl.ds(2 * PAIR, 16), :] = rows.astype(BF16)
 
@@ -85,7 +91,7 @@
     far, near, own = refs[7:11], refs[11:14], refs[14]
     own_q, own_kv = refs[15:17]
     table, groups, lengths, suffixes, cache_scale = refs[17:22]
-    table_sems, more_sems, sems = refs[22:]
+    spread, table_sems, more_sems, sems = refs[22:]
     p = ids[0]
     m = ids[1]
     loads = [
@@ -135,7 +141,7 @@
             for c in group:
                 c.start()
             made += group
-            pending.append((locals_, m ^ (2 * slot), out))
+            pending.append((locals_, slot, out))
     mine = groups[p]
     for run in range(RUNS):
         for jj in range(POOL):
@@ -143,9 +149,9 @@
             meta[META_J + RUNS * ((table[mine, at] // slot_count) ^ p) + run] = at
     meta[META_LEN] = lengths[mine]
     meta[META_SUF] = suffixes[mine]
-    scales = cache_scale[...].astype(F32)
-    for locals_, head, out in pending:
-        write_scales(scales, locals_, head, out)
+    spread_scales(cache_scale, m, spread)
+    for locals_, slot, out in pending:
+        write_scales(spread, locals_, slot, out)
     for c in made:
         c.wait()
 
@@ -165,6 +171,7 @@
         scratch_shapes=[pltpu.SMEM(x.shape, jnp.int32) for x in tables]
         + [
             pltpu.VMEM(cache_scale.shape, cache_scale.dtype),
+            pltpu.VMEM((4, cache.shape[0], HD), F32),
             pltpu.SemaphoreType.DMA((5,)),
             pltpu.SemaphoreType.DMA((12,)),
             pltpu.SemaphoreType.DMA((48,)),
@@ -175,7 +182,7 @@
 
 
 def wide(row):
-    return jnp.concatenate([row] * (TILE // HD), axis=1)
+    return jnp.broadcast_to(jnp.concatenate([row] * (TILE // HD), axis=1), (8, TILE))
 
 
 def terms(tile, run):
@@ -191,9 +198,7 @@
     tiles = BOTH // TILE
 
     def score(t):
-        return lax.dot_general(
-            keys, q[pl.ds(t * TILE, TILE), :], NT, preferred_element_type=F32
-        )
+        return jnp.dot(keys, q[:, pl.ds(t * TILE, TILE)], preferred_element_type=F32)
 
     following = score(0)
     for t in range(tiles):
@@ -202,40 +207,45 @@
             following = score(t + 1)
         cols = pl.ds(t * TILE, TILE)
         blocks = blocks_of(t)
-        old = jnp.full((1, TILE), masked_score, F32) if before is None else before[REF_ROW : REF_ROW + 1, cols]
+        if before is None:
+            old = jnp.full((8, TILE), masked_score, F32)
+        else:
+            old = before[REF_ROW : REF_ROW + 8, cols]
         parts = []
-        reference = old
+        highest = old
         for b, (term, dead, mask) in enumerate(blocks):
             part = scores[b * BLK : (b + 1) * BLK]
             part = part if mask is None else jnp.where(mask, part, masked_score)
+            part = part.reshape(BLK // 8, 8, TILE)
             parts.append(part)
-            top = jnp.max(part, axis=0, keepdims=True)
-            top = top * (LOG2E * INV_ROOT) if term is UNIT else top * term[0]
+            top = jnp.max(part, axis=0) * (LOG2E * INV_ROOT if term is UNIT else term[0])
             if dead is not None:
                 top = jnp.where(dead, masked_score, top)
-            reference = jnp.maximum(reference, top)
+            highest = jnp.maximum(highest, top)
+        reference = jnp.broadcast_to(jnp.max(highest, axis=0, keepdims=True), (8, TILE))
         if before is None:
-            total = jnp.zeros((1, TILE), F32)
+            total = jnp.zeros((8, TILE), F32)
         else:
             factor = jnp.exp2(old - reference)
-            total = before[SUM_ROW : SUM_ROW + 1, cols] * factor
+            total = before[SUM_ROW : SUM_ROW + 8, cols] * factor
         rounded = []
         for part, (term, dead, mask) in zip(parts, blocks):
             shift = reference if term is UNIT else reference - term[1]
             if dead is not None:
                 shift = jnp.where(dead, -masked_score, shift)
-            scaled = part * (LOG2E * INV_ROOT) if term is UNIT else part * term[0]
+            scaled = part * (LOG2E * INV_ROOT if term is UNIT else term[0])
             weights = jnp.exp2(scaled - shift)
-            if mask is not None:
-                weights = jnp.where(mask, weights, 0.0)
-            summed = jnp.sum(weights, axis=0, keepdims=True)
+            summed = jnp.sum(weights, axis=0)
             total = total + (summed if term is UNIT else summed * term[2])
-            rounded.append(weights.astype(BF16))
+            rounded.append(weights.reshape(BLK, TILE).astype(BF16))
         rounded = jnp.concatenate(rounded, axis=0) if len(rounded) > 1 else rounded[0]
         product = jnp.dot(values_t, rounded, preferred_element_type=F32)
-        after[:HD, cols] = product if before is None else before[:HD, cols] * factor + product
-        after[REF_ROW : REF_ROW + 1, cols] = reference
-        after[SUM_ROW : SUM_ROW + 1, cols] = total
+        if before is not None:
+            held = before[:HD, cols].reshape(HD // 8, 8, TILE) * factor
+            product = held.reshape(HD, TILE) + product
+        after[:HD, cols] = product
+        after[REF_ROW : REF_ROW + 8, cols] = reference
+        after[SUM_ROW : SUM_ROW + 8, cols] = total
 
 
 def add_pieces(q, before, after, pieces, ks, meta, extra=None):
@@ -246,14 +256,18 @@
         jnp.clip(reach - meta[META_J + RUNS * k + r] * BLK, 0, BLK) for k in ks for r in range(RUNS)
     ]
     most = functools.reduce(jnp.maximum, counts)
-
-    def whole():
+    ragged = functools.reduce(jnp.logical_or, [(c > 0) & (c < BLK) for c in counts])
+
+    def whole(masked):
         blocks = []
+        place = lax.broadcasted_iota(jnp.int32, (BLK, TILE), 0) if masked else None
         for i in range(n):
-            tile = pieces[i, 2 * PAIR :, :].astype(F32)
-            blocks += [(terms(tile, r), counts[RUNS * i + r] < BLK, None) for r in range(RUNS)]
-        keys = [pieces[i, :PAIR, :] for i in range(n)]
-        values = [pieces[i, PAIR : 2 * PAIR, :].T for i in range(n)]
+            tile = pieces[i][2 * PAIR :, :].astype(F32)
+            for r in range(RUNS):
+                c = counts[RUNS * i + r]
+                blocks.append((terms(tile, r),) + ((None, place < c) if masked else (c < BLK, None)))
+        keys = [pieces[i][:PAIR, :] for i in range(n)]
+        values = [pieces[i][PAIR : 2 * PAIR, :].T for i in range(n)]
         blocks_of = lambda t: blocks
         if extra is not None:
             keys = [extra[0]] + keys
@@ -263,56 +277,46 @@
         values = jnp.concatenate(values, axis=1) if len(values) > 1 else values[0]
         fold(q, keys, values, before, after, blocks_of)
 
-    if extra is not None:
-        whole()
-    else:
-
-        @pl.when(most < BLK)
+    if extra is None:
+
+        @pl.when(most == 0)
         def _():
             after[...] = before[...]
 
-        pl.when(most == BLK)(whole)
-
-    part = jnp.int32(-1)
-    count = jnp.int32(0)
-    for at, c in enumerate(counts):
-        hit = (c > 0) & (c < BLK)
-        part = jnp.where(hit, at, part)
-        count = jnp.where(hit, c, count)
-
-    @pl.when(part >= 0)
-    def _():
-        i = part // RUNS
-        run = part % RUNS
-        tile = pieces[i, 2 * PAIR :, :].astype(F32)
-        term = [jnp.where(run == 1, b, a) for a, b in zip(terms(tile, 0), terms(tile, 1))]
-        mask = lax.broadcasted_iota(jnp.int32, (BLK, TILE), 0) < count
-        at = pl.multiple_of(run * BLK, BLK)
-        fold(
-            q,
-            pieces[i, pl.ds(at, BLK), :],
-            pieces[i, pl.ds(PAIR + at, BLK), :].T,
-            after,
-            after,
-            lambda t: [(term, None, mask)],
-        )
+    some = jnp.bool_(True) if extra is not None else most > 0
+    pl.when(some & jnp.logical_not(ragged))(functools.partial(whole, False))
+    pl.when(some & ragged)(functools.partial(whole, True))
 
 
 def state_shapes(slots):
     return [pltpu.VMEM((STATE, BOTH), F32)] * slots
 
 
-def own_kernel(meta, swap, own, own_q, own_kv, kv, q_all, *states):
-    m = meta[META_M]
+def prepare_kernel(swap, own_q, own_kv, kv, q_all):
     for slot in range(2):
+        kv[slot, 0] = own_kv[slot]
+        kv[slot, 1, :ROWS, :] = swap[slot, :, WIDE : WIDE + HD]
+        kv[slot, 1, ROWS:, :] = swap[slot, :, WIDE + HD :]
         for h in range(PER):
             rows = pl.ds(h * ROWS, ROWS)
             others = pl.ds(WIDE + h * ROWS, ROWS)
-            q_all[slot, rows, :] = own_q[slot, :, h * HD : (h + 1) * HD]
-            q_all[slot, others, :] = swap[slot, :, h * HD : (h + 1) * HD]
-        kv[slot, 0] = own_kv[slot]
-        kv[slot, 1, :ROWS, :] = swap[slot, :, WIDE : WIDE + HD]
-        kv[slot, 1, ROWS:, :] = swap[slot, :, WIDE + HD :]
+            q_all[slot, :, rows] = own_q[slot, :, h * HD : (h + 1) * HD].T
+            q_all[slot, :, others] = swap[slot, :, h * HD : (h + 1) * HD].T
+
+
+def prepare_call(swap, own_q, own_kv):
+    return pl.pallas_call(
+        prepare_kernel,
+        out_shape=[pltpu.VMEM((2, 2, 2 * ROWS, HD), BF16), pltpu.VMEM((2, HD, BOTH), BF16)],
+        in_specs=[IN_VMEM] * 3,
+        out_specs=[IN_VMEM] * 2,
+        compiler_params=pltpu.CompilerParams(vmem_limit_bytes=VMEM_LIMIT),
+        cost_estimate=COST,
+    )(swap, own_q, own_kv)
+
+
+def own_kernel(meta, q_all, kv, own, *states):
+    m = meta[META_M]
     key = lax.broadcasted_iota(jnp.int32, (BLK, TILE), 0)
     row = lax.broadcasted_iota(jnp.int32, (BLK, TILE), 1) % ROWS
     causal = key <= row
@@ -330,24 +334,22 @@
             q_all.at[slot],
             None,
             states[slot],
-            own.at[pl.ds(slot, 1)],
+            [own.at[slot]],
             (0,),
             meta,
             (keys, values, blocks_of),
         )
 
 
-def own_call(meta, swap, own, own_q, own_kv):
-    out = pl.pallas_call(
+def own_call(meta, q_all, kv, own):
+    return pl.pallas_call(
         own_kernel,
-        out_shape=[pltpu.VMEM((2, 2, 2 * ROWS, HD), BF16), pltpu.VMEM((2, BOTH, HD), BF16)]
-        + state_shapes(2),
-        in_specs=[IN_SMEM] + [IN_VMEM] * 4,
-        out_specs=[IN_VMEM] * 4,
+        out_shape=state_shapes(2),
+        in_specs=[IN_SMEM] + [IN_VMEM] * 3,
+        out_specs=[IN_VMEM] * 2,
         compiler_params=pltpu.CompilerParams(vmem_limit_bytes=VMEM_LIMIT),
         cost_estimate=COST,
-    )(meta, swap, own, own_q, own_kv)
-    return out[0], out[1], out[2:]
+    )(meta, q_all, kv, own)
 
 
 def add_kernel(slots, ks, early, last, meta, q_all, *refs):
@@ -358,10 +360,8 @@
     kv_early = take(1)[0] if early else None
     outs = take(2) if last else None
     after = take(len(slots))
-    kv = take(1)[0]
     for w, slot in enumerate(slots):
-        for i, s in enumerate(sources):
-            kv[w, i] = s[slot] if len(s.shape) == 3 else s[...]
+        pieces = [s.at[slot] if len(s.shape) == 3 else s for s in sources]
         extra = None
         if early:
             unused = meta[META_M] < 2
@@ -370,7 +370,7 @@
                 jnp.concatenate([kv_early[1 - slot, side, ROWS:].T for side in range(2)], axis=1),
                 lambda t: [(UNIT, unused, None)] * 2,
             )
-        add_pieces(q_all.at[slot], before[w], after[w], kv.at[w], ks, meta, extra)
+        add_pieces(q_all.at[slot], before[w], after[w], pieces, ks, meta, extra)
     if last:
         state = after[0]
         for side, out in enumerate(outs):
@@ -378,19 +378,18 @@
             row = lax.broadcasted_iota(jnp.int32, (HD, ROWS), 1) + member * ROWS
             for i in range(PER):
                 cols = pl.ds(side * WIDE + i * ROWS, ROWS)
-                piece = state[:HD, cols] * (1.0 / state[SUM_ROW : SUM_ROW + 1, cols])
+                piece = state[:HD, cols] * (1.0 / jnp.sum(state[SUM_ROW : SUM_ROW + 8, cols], axis=0, keepdims=True))
                 piece = jnp.where(row < meta[META_SUF], piece, 0.0).astype(BF16)
                 out[:, i * HD : (i + 1) * HD] = piece.T
 
 
 def add_call(meta, q_all, states, sources, slots, ks, early=None, last=False):
     flat = [states[s] for s in slots]
-    n = len(ks)
     args = [meta, q_all, *flat, *sources] + ([] if early is None else [early])
-    scratch = [pltpu.VMEM((len(slots), n, PIECE, HD), BF16)]
+    scratch = []
     if last:
         out_shape = [pltpu.VMEM((ROWS, WIDE), BF16)] * 2
-        scratch = state_shapes(1) + scratch
+        scratch = state_shapes(1)
     else:
         out_shape = state_shapes(len(slots))
     out = pl.pallas_call(
@@ -455,28 +454,30 @@
         far_in[k] = permute(far[k - 4], "pool", POOL, k)
     for k in (1, 2):
         near_in[k] = permute(near[k - 1], "pool", POOL, k)
-    kv, q_all, states = own_call(meta, swap_in, own, own_q, own_kv)
-    far[2], near[2], kv, states = lax.optimization_barrier((far[2], near[2], kv, states))
-    far_in[6] = permute(far[2], "pool", POOL, 6)
+    kv, q_all = prepare_call(swap_in, own_q, own_kv)
+    early = permute(kv, "blk", 4, 2)
+    states = own_call(meta, q_all, kv, own)
+    near[2], states = lax.optimization_barrier((near[2], states))
     near_in[3] = permute(near[2], "pool", POOL, 3)
-    early = permute(kv, "blk", 4, 2)
-    states = add_call(meta, q_all, states, [near_in[1], near_in[2]], (0, 1), (1, 2))
-    far[3], far_in[4], far_in[5], states = lax.optimization_barrier(
-        (far[3], far_in[4], far_in[5], states)
-    )
-    far_in[7] = permute(far[3], "pool", POOL, 7)
+    states = add_call(meta, q_all, states, [near_in[1]], (0, 1), (1,), early=early)
+    far[2], far[3], near_in[2], far_in[4], far_in[5], states = lax.optimization_barrier(
+        (far[2], far[3], near_in[2], far_in[4], far_in[5], states)
+    )
+    for k in (6, 7):
+        far_in[k] = permute(far[k - 4], "pool", POOL, k)
     for k in (4, 5):
         across[k] = permute(far_in[k], "blk", 4, 2)
-    states = add_call(meta, q_all, states, [near_in[3]], (0, 1), (3,), early=early)
+    states = add_call(meta, q_all, states, [far_in[4], far_in[5]], (0,), (4, 5))
+    near_in[3], states = lax.optimization_barrier((near_in[3], states))
+    states = add_call(meta, q_all, states, [near_in[2], near_in[3]], (0, 1), (2, 3))
     far_in[6], far_in[7], states = lax.optimization_barrier((far_in[6], far_in[7], states))
     for k in (6, 7):
         across[k] = permute(far_in[k], "blk", 4, 2)
-    states = add_call(meta, q_all, states, [far_in[4], far_in[5]], (0,), (4, 5))
     states = add_call(meta, q_all, states, [across[4], across[5]], (1,), (4, 5))
     mine, yours = [], []
     for slot, source in ((0, far_in), (1, across)):
         a, b = add_call(meta, q_all, states, [source[6], source[7]], (slot,), (6, 7), last=True)
-        mine.append(a)
+        mine.append(pltpu.with_memory_space_constraint(a, pltpu.VMEM))
         yours.append(
             pltpu.with_memory_space_constraint(permute(b, "blk", 4, 1), pltpu.VMEM)
         )

time: 53.7 us -> 51.3 us (0.955)
  the two profiles are of different devices: /device:TPU:9 before, /device:TPU:25 now
where the time goes in v3:
time: 51.3 us; the launch traced here: 51.8 us
  Pallas kernels  27.1 us (53%)
  starting transfers between devices  19.6 us (38%)
  waiting for transfers between devices  4.71 us (9%)
    ppermute x15, starting transfers between devices, permute(): return lax.ppermute(x, axis, [(i, i ^ k) for i in range(count)])  19.6 us
    pallas_call x6, Pallas kernels, add_call(): pl.pallas_call(functools.partial(add_kernel, slots, ks, early is not None...  17 us
    ppermute x15, waiting for transfers between devices, permute(): return lax.ppermute(x, axis, [(i, i ^ k) for i in range(count)])  4.71 us
    pallas_call x1, Pallas kernels, gather_call(): pl.pallas_call(gather_kernel, out_shape=[jax.ShapeDtypeStruct((META_SIZE,...  4.33 us
    pallas_call x1, Pallas kernels, own_call(): pl.pallas_call(own_kernel, out_shape=state_shapes(2), in_specs=[IN_SMEM]...  3.7 us
    pallas_call x1, Pallas kernels, join_call(): pl.pallas_call(join_kernel, out_shape=jax.ShapeDtypeStruct((ROWS, QH * HD...  1.66 us
  transfers between devices with their start and end apart: 15, of which 3 were waited for; matrix products, arithmetic and copies ran while one was open for 0% of the time, Pallas kernels for 41%

profile of v3, /device:TPU:25, one launch (start us, length us, event | category | flops | bytes accessed | tf_op | source)
XLA Modules:
  0.0 51.8 jit_solution(4693026790396574885)
XLA Ops:
  0.1 4.3 %shard_map.82 = (s32[24]{0:T(128)S(1)}, bf16[2,128,1280]{2,1,0:T(8,128)(2,1)S(1)}, bf16[528,128]{1,0:T(8,128)(2,1)S(1)}, bf16[528,128]{1,0:T(8,128)(2,1)S(1)}, b...) custom-call(s32[2]{0:T(128)S(1)} %pad_add_fusion.ids, ...), custom_call_target="tpu_custom_call" | custom-call | flops 1024 | bytes 1024 | tf_op jit(solution)/shard_map/pallas_call | solution.py:160
  4.4 0.7 %collective-permute-start = (bf16[2,128,1280]{2,1,0:T(8,128)(2,1)S(1)}, bf16[2,128,1280]{2,1,0:T(8,128)(2,1)S(1)}, u32[]{:S(2)}, u32[]{:S(2)}) collective-permute-start(bf16[2,128,1280]{2,1,0:T(8,128)(2,1)S(1)} %get-tuple-element.47), channel_id=1, source_target_pairs={{0,1},{1,0},{2,3},{3,2},{4,5},{5,4},{6,7},{7,6},{8,9},{9,8},{10,11... | collective-permute-start | bytes 1966088 | tf_op jit(solution)/shard_map/ppermute | solution.py:436
  5.2 1.2 %collective-permute-start.4 = (bf16[2,528,128]{2,1,0:T(8,128)(2,1)S(1)}, bf16[2,528,128]{2,1,0:T(8,128)(2,1)S(1)}, u32[]{:S(2)}, u32[]{:S(2)}) collective-permute-start(bf16[2,528,128]{2,1,0:T(8,128)(2,1)S(1)} %get-tuple-element.63), channel_id=1, source_target_pairs={{0,4},{4,0},{8,12},{12,8},{16,20},{20,16},{24,28},{28,24},{1,5},{5... | collective-permute-start | bytes 811016 | tf_op jit(solution)/shard_map/ppermute | solution.py:436
  6.6 0.3 collective-permute-done.swap
  6.9 0.4 shard_map.83
  7.3 1.3 %collective-permute-start.5 = (bf16[2,2,256,128]{3,2,1,0:T(8,128)(2,1)S(1)}, bf16[2,2,256,128]{3,2,1,0:T(8,128)(2,1)S(1)}, u32[]{:S(2)}, u32[]{:S(2)}) collective-permute-start(bf16[2,2,256,128]{3,2,1,0:T(8,128)(2,1)S(1)} %get-tuple-element.57.kv), channel_id=1, source_target_pairs={{0,2},{1,3},{2,0},{3,1},{4,6},{5,7},{6,4},{7,5},{8,10},{9,11},{10,... | collective-permute-start | bytes 786440 | tf_op jit(solution)/shard_map/ppermute | solution.py:436
  8.6 3.2 %collective-permute-start.3 = (bf16[528,128]{1,0:T(8,128)(2,1)S(1)}, bf16[528,128]{1,0:T(8,128)(2,1)S(1)}, u32[]{:S(2)}, u32[]{:S(2)}) collective-permute-start(bf16[528,128]{1,0:T(8,128)(2,1)S(1)} %get-tuple-element.55), channel_id=1, source_target_pairs={{0,20},{4,16},{8,28},{12,24},{16,4},{20,0},{24,12},{28,8},{1,21},{... | collective-permute-start | bytes 405512 | tf_op jit(solution)/shard_map/ppermute | solution.py:436
  11.9 3.7 %shard_map.84 = (f32[144,2048]{1,0:T(8,128)S(1)}, f32[144,2048]{1,0:T(8,128)S(1)}) custom-call(s32[24]{0:T(128)S(1)} %get-tuple-element.46.meta, bf16[2,128,2048]{2,1,0:T(8,128)(2,1)S(1)} %get-tuple-element.50.q_all, bf16[2,2,256,128]{3,2,1,0:T(8,128)(2,1)S(1)} %get-tuple-element.57.kv, bf16[2,528,128]{2,1,0:T(8,128)(2,1)S(1)} %get-tuple-element.58.own), custom_call_target="tpu_custom_call" | custom-call | flops 1024 | bytes 1024 | tf_op jit(solution)/shard_map/pallas_call | solution.py:345
  15.6 1.1 %collective-permute-start.8 = (bf16[2,528,128]{2,1,0:T(8,128)(2,1)S(1)}, bf16[2,528,128]{2,1,0:T(8,128)(2,1)S(1)}, u32[]{:S(2)}, u32[]{:S(2)}) collective-permute-start(bf16[2,528,128]{2,1,0:T(8,128)(2,1)S(1)} %get-tuple-element.68), channel_id=1, source_target_pairs={{0,12},{4,8},{8,4},{12,0},{16,28},{20,24},{24,20},{28,16},{1,13},{... | collective-permute-start | bytes 811016 | tf_op jit(solution)/shard_map/ppermute | solution.py:436
  16.7 4.2 %shard_map.85 = (f32[144,2048]{1,0:T(8,128)S(1)}, f32[144,2048]{1,0:T(8,128)S(1)}) custom-call(s32[24]{0:T(128)S(1)} %get-tuple-element.46.meta, bf16[2,128,2048]{2,1,0:T(8,128)(2,1)S(1)} %get-tuple-element.50.q_all, f32[144,2048]{1,0:T(8,128)S(1)} %get-tuple-element.61.refs_0_, f32[144,2048]{1,0:T(8,128)S(1)} %get-tuple-element.62.refs_1_, ...), custom_call_target="tpu_custom_call" | custom-call | flops 1024 | bytes 1024 | tf_op jit(solution)/shard_map/pallas_call | solution.py:395
  21.0 2.8 %collective-permute-done.3.refs_2_ = bf16[528,128]{1,0:T(8,128)(2,1)S(1)} collective-permute-done((bf16[528,128]{1,0:T(8,128)(2,1)S(1)}, bf16[528,128]{1,0:T(8,128)(2,1)S(1)}, u32[]{:S(2)}, u32[]{:S(2)}) %collective-permute-start.3) | collective-permute-done | bytes 135200 | tf_op jit(solution)/shard_map/ppermute | solution.py:436
  23.9 3.1 %collective-permute-start.7 = (bf16[528,128]{1,0:T(8,128)(2,1)S(1)}, bf16[528,128]{1,0:T(8,128)(2,1)S(1)}, u32[]{:S(2)}, u32[]{:S(2)}) collective-permute-start(bf16[528,128]{1,0:T(8,128)(2,1)S(1)} %get-tuple-element.67), channel_id=1, source_target_pairs={{0,28},{4,24},{8,20},{12,16},{16,12},{20,8},{24,4},{28,0},{1,29},{... | collective-permute-start | bytes 405512 | tf_op jit(solution)/shard_map/ppermute | solution.py:436
  26.9 0.2 collective-permute-start.9
  27.1 1.3 %collective-permute-start.10 = (bf16[528,128]{1,0:T(8,128)(2,1)S(1)}, bf16[528,128]{1,0:T(8,128)(2,1)S(1)}, u32[]{:S(2)}, u32[]{:S(2)}) collective-permute-start(bf16[528,128]{1,0:T(8,128)(2,1)S(1)} %collective-permute-done.3.refs_2_), channel_id=1, source_target_pairs={{0,2},{1,3},{2,0},{3,1},{4,6},{5,7},{6,4},{7,5},{8,10},{9,11},{10,... | collective-permute-start | bytes 405512 | tf_op jit(solution)/shard_map/ppermute | solution.py:436
  28.4 2.1 %shard_map.86.refs_0_ = f32[144,2048]{1,0:T(8,128)S(1)} custom-call(s32[24]{0:T(128)S(1)} %get-tuple-element.46.meta, bf16[2,128,2048]{2,1,0:T(8,128)(2,1)S(1)} %get-tuple-element.50.q_all, f32[144,2048]{1,0:T(8,128)S(1)} %get-tuple-element.69.refs_0_, bf16[528,128]{1,0:T(8,128)(2,1)S(1)} %collective-permute-done.2.refs_1_, ...), custom_call_target="tpu_custom_call" | custom-call | flops 1024 | bytes 1024 | tf_op jit(solution)/shard_map/pallas_call | solution.py:395
  30.5 3.8 %shard_map.87 = (f32[144,2048]{1,0:T(8,128)S(1)}, f32[144,2048]{1,0:T(8,128)S(1)}) custom-call(s32[24]{0:T(128)S(1)} %get-tuple-element.46.meta, bf16[2,128,2048]{2,1,0:T(8,128)(2,1)S(1)} %get-tuple-element.50.q_all, f32[144,2048]{1,0:T(8,128)S(1)} %shard_map.86.refs_0_, f32[144,2048]{1,0:T(8,128)S(1)} %get-tuple-element.74.refs_1_, ...), custom_call_target="tpu_custom_call" | custom-call | flops 1024 | bytes 1024 | tf_op jit(solution)/shard_map/pallas_call | solution.py:395
  34.4 0.3 collective-permute-start.11
  34.6 1.3 %collective-permute-start.12 = (bf16[528,128]{1,0:T(8,128)(2,1)S(1)}, bf16[528,128]{1,0:T(8,128)(2,1)S(1)}, u32[]{:S(2)}, u32[]{:S(2)}) collective-permute-start(bf16[528,128]{1,0:T(8,128)(2,1)S(1)} %collective-permute-done.7.refs_2_), channel_id=1, source_target_pairs={{0,2},{1,3},{2,0},{3,1},{4,6},{5,7},{6,4},{7,5},{8,10},{9,11},{10,... | collective-permute-start | bytes 405512 | tf_op jit(solution)/shard_map/ppermute | solution.py:436
  35.9 2.5 %shard_map.88 = (bf16[128,1024]{1,0:T(8,128)(2,1)S(1)}, bf16[128,1024]{1,0:T(8,128)(2,1)S(1)}) custom-call(s32[24]{0:T(128)S(1)} %get-tuple-element.46.meta, bf16[2,128,2048]{2,1,0:T(8,128)(2,1)S(1)} %get-tuple-element.50.q_all, f32[144,2048]{1,0:T(8,128)S(1)} %get-tuple-element.79.refs_0_, bf16[528,128]{1,0:T(8,128)(2,1)S(1)} %collective-permute-done.6.refs_1_, ...), custom_call_target="tpu_custom_call" | custom-call | flops 1024 | bytes 1024 | tf_op jit(solution)/shard_map/pallas_call | solution.py:395
  38.4 5.5 %collective-permute-start.13 = (bf16[128,1024]{1,0:T(8,128)(2,1)S(1)}, bf16[128,1024]{1,0:T(8,128)(2,1)S(1)}, u32[]{:S(2)}, u32[]{:S(2)}) collective-permute-start(bf16[128,1024]{1,0:T(8,128)(2,1)S(1)} %get-tuple-element.85), channel_id=1, source_target_pairs={{0,1},{1,0},{2,3},{3,2},{4,5},{5,4},{6,7},{7,6},{8,9},{9,8},{10,11... | collective-permute-start | bytes 786440 | tf_op jit(solution)/shard_map/ppermute | solution.py:436
  43.9 2.1 %shard_map.89.refs_0_ = f32[144,2048]{1,0:T(8,128)S(1)} custom-call(s32[24]{0:T(128)S(1)} %get-tuple-element.46.meta, bf16[2,128,2048]{2,1,0:T(8,128)(2,1)S(1)} %get-tuple-element.50.q_all, f32[144,2048]{1,0:T(8,128)S(1)} %get-tuple-element.83.refs_0_, bf16[528,128]{1,0:T(8,128)(2,1)S(1)} %collective-permute-done.9.refs_1_, ...), custom_call_target="tpu_custom_call" | custom-call | flops 1024 | bytes 1024 | tf_op jit(solution)/shard_map/pallas_call | solution.py:395
  46.1 2.3 %shard_map.90 = (bf16[128,1024]{1,0:T(8,128)(2,1)S(1)}, bf16[128,1024]{1,0:T(8,128)(2,1)S(1)}) custom-call(s32[24]{0:T(128)S(1)} %get-tuple-element.46.meta, bf16[2,128,2048]{2,1,0:T(8,128)(2,1)S(1)} %get-tuple-element.50.q_all, f32[144,2048]{1,0:T(8,128)S(1)} %shard_map.89.refs_0_, bf16[528,128]{1,0:T(8,128)(2,1)S(1)} %collective-permute-done.11.refs_1_, ...), custom_call_target="tpu_custom_call" | custom-call | flops 1024 | bytes 1024 | tf_op jit(solution)/shard_map/pallas_call | solution.py:395
  48.5 1.5 %collective-permute-done.14.refs_3_ = bf16[128,1024]{1,0:T(8,128)(2,1)S(1)} collective-permute-done((bf16[128,1024]{1,0:T(8,128)(2,1)S(1)}, bf16[128,1024]{1,0:T(8,128)(2,1)S(1)}, u32[]{:S(2)}, u32[]{:S(2)}) %collective-permute-start.14) | collective-permute-done | bytes 262176 | tf_op jit(solution)/shard_map/ppermute | solution.py:436
  50.0 1.7 %shard_map.91 = bf16[128,4096]{1,0:T(8,128)(2,1)} custom-call(s32[24]{0:T(128)} %copy-done, bf16[128,1024]{1,0:T(8,128)(2,1)S(1)} %get-tuple-element.82.refs_0_, bf16[128,1024]{1,0:T(8,128)(2,1)S(1)} %get-tuple-element.84.refs_1_, bf16[128,1024]{1,0:T(8,128)(2,1)S(1)} %collective-permute-done.13.refs_2_, bf16[128,1024]{1,0:T(8,128)(2,1)S(1)} %collective-permute-done.14.refs_3_), custom_call_target="tpu_custom_call" | custom-call | flops 1024 | bytes 1024 | tf_op jit(solution)/shard_map/pallas_call | solution.py:425
  (19 shorter events, 0.5 us)
Async XLA Ops:
  4.4 41.6 %copy-start = (s32[24]{0:T(128)}, s32[24]{0:T(128)S(1)}, u32[]{:S(2)}) copy-start(s32[24]{0:T(128)S(1)} %get-tuple-element.46.meta) | copy-start | bytes 292
  4.4 2.5 %collective-permute-start = (bf16[2,128,1280]{2,1,0:T(8,128)(2,1)S(1)}, bf16[2,128,1280]{2,1,0:T(8,128)(2,1)S(1)}, u32[]{:S(2)}, u32[]{:S(2)}) collective-permute-start(bf16[2,128,1280]{2,1,0:T(8,128)(2,1)S(1)} %get-tuple-element.47), channel_id=1, source_target_pairs={{0,1},{1,0},{2,3},{3,2},{4,5},{5,4},{6,7},{7,6},{8,9},{9,8},{10,11... | collective-permute-start | bytes 1966088 | tf_op jit(solution)/shard_map/ppermute | solution.py:436
  5.2 10.4 %collective-permute-start.4 = (bf16[2,528,128]{2,1,0:T(8,128)(2,1)S(1)}, bf16[2,528,128]{2,1,0:T(8,128)(2,1)S(1)}, u32[]{:S(2)}, u32[]{:S(2)}) collective-permute-start(bf16[2,528,128]{2,1,0:T(8,128)(2,1)S(1)} %get-tuple-element.63), channel_id=1, source_target_pairs={{0,4},{4,0},{8,12},{12,8},{16,20},{20,16},{24,28},{28,24},{1,5},{5... | collective-permute-start | bytes 811016 | tf_op jit(solution)/shard_map/ppermute | solution.py:436
  6.4 17.4 %collective-permute-start.1 = (bf16[2,528,128]{2,1,0:T(8,128)(2,1)S(1)}, bf16[2,528,128]{2,1,0:T(8,128)(2,1)S(1)}, u32[]{:S(2)}, u32[]{:S(2)}) collective-permute-start(bf16[2,528,128]{2,1,0:T(8,128)(2,1)S(1)} %get-tuple-element.53), channel_id=1, source_target_pairs={{0,8},{4,12},{8,0},{12,4},{16,24},{20,28},{24,16},{28,20},{1,9},{5... | collective-permute-start | bytes 811016 | tf_op jit(solution)/shard_map/ppermute | solution.py:436
  7.3 9.4 %collective-permute-start.5 = (bf16[2,2,256,128]{3,2,1,0:T(8,128)(2,1)S(1)}, bf16[2,2,256,128]{3,2,1,0:T(8,128)(2,1)S(1)}, u32[]{:S(2)}, u32[]{:S(2)}) collective-permute-start(bf16[2,2,256,128]{3,2,1,0:T(8,128)(2,1)S(1)} %get-tuple-element.57.kv), channel_id=1, source_target_pairs={{0,2},{1,3},{2,0},{3,1},{4,6},{5,7},{6,4},{7,5},{8,10},{9,11},{10,... | collective-permute-start | bytes 786440 | tf_op jit(solution)/shard_map/ppermute | solution.py:436
  8.6 12.4 %collective-permute-start.2 = (bf16[528,128]{1,0:T(8,128)(2,1)S(1)}, bf16[528,128]{1,0:T(8,128)(2,1)S(1)}, u32[]{:S(2)}, u32[]{:S(2)}) collective-permute-start(bf16[528,128]{1,0:T(8,128)(2,1)S(1)} %get-tuple-element.54), channel_id=1, source_target_pairs={{0,16},{4,20},{8,24},{12,28},{16,0},{20,4},{24,8},{28,12},{1,17},{... | collective-permute-start | bytes 405512 | tf_op jit(solution)/shard_map/ppermute | solution.py:436
  8.6 15.2 %collective-permute-start.3 = (bf16[528,128]{1,0:T(8,128)(2,1)S(1)}, bf16[528,128]{1,0:T(8,128)(2,1)S(1)}, u32[]{:S(2)}, u32[]{:S(2)}) collective-permute-start(bf16[528,128]{1,0:T(8,128)(2,1)S(1)} %get-tuple-element.55), channel_id=1, source_target_pairs={{0,20},{4,16},{8,28},{12,24},{16,4},{20,0},{24,12},{28,8},{1,21},{... | collective-permute-start | bytes 405512 | tf_op jit(solution)/shard_map/ppermute | solution.py:436
  15.6 14.9 %collective-permute-start.8 = (bf16[2,528,128]{2,1,0:T(8,128)(2,1)S(1)}, bf16[2,528,128]{2,1,0:T(8,128)(2,1)S(1)}, u32[]{:S(2)}, u32[]{:S(2)}) collective-permute-start(bf16[2,528,128]{2,1,0:T(8,128)(2,1)S(1)} %get-tuple-element.68), channel_id=1, source_target_pairs={{0,12},{4,8},{8,4},{12,0},{16,28},{20,24},{24,20},{28,16},{1,13},{... | collective-permute-start | bytes 811016 | tf_op jit(solution)/shard_map/ppermute | solution.py:436
  23.8 10.5 %collective-permute-start.6 = (bf16[528,128]{1,0:T(8,128)(2,1)S(1)}, bf16[528,128]{1,0:T(8,128)(2,1)S(1)}, u32[]{:S(2)}, u32[]{:S(2)}) collective-permute-start(bf16[528,128]{1,0:T(8,128)(2,1)S(1)} %get-tuple-element.66), channel_id=1, source_target_pairs={{0,24},{4,28},{8,16},{12,20},{16,8},{20,12},{24,0},{28,4},{1,25},{... | collective-permute-start | bytes 405512 | tf_op jit(solution)/shard_map/ppermute | solution.py:436
  23.9 10.5 %collective-permute-start.7 = (bf16[528,128]{1,0:T(8,128)(2,1)S(1)}, bf16[528,128]{1,0:T(8,128)(2,1)S(1)}, u32[]{:S(2)}, u32[]{:S(2)}) collective-permute-start(bf16[528,128]{1,0:T(8,128)(2,1)S(1)} %get-tuple-element.67), channel_id=1, source_target_pairs={{0,28},{4,24},{8,20},{12,16},{16,12},{20,8},{24,4},{28,0},{1,29},{... | collective-permute-start | bytes 405512 | tf_op jit(solution)/shard_map/ppermute | solution.py:436
  26.9 17.0 %collective-permute-start.9 = (bf16[528,128]{1,0:T(8,128)(2,1)S(1)}, bf16[528,128]{1,0:T(8,128)(2,1)S(1)}, u32[]{:S(2)}, u32[]{:S(2)}) collective-permute-start(bf16[528,128]{1,0:T(8,128)(2,1)S(1)} %collective-permute-done.2.refs_1_), channel_id=1, source_target_pairs={{0,2},{1,3},{2,0},{3,1},{4,6},{5,7},{6,4},{7,5},{8,10},{9,11},{10,... | collective-permute-start | bytes 405512 | tf_op jit(solution)/shard_map/ppermute | solution.py:436
  27.1 16.8 %collective-permute-start.10 = (bf16[528,128]{1,0:T(8,128)(2,1)S(1)}, bf16[528,128]{1,0:T(8,128)(2,1)S(1)}, u32[]{:S(2)}, u32[]{:S(2)}) collective-permute-start(bf16[528,128]{1,0:T(8,128)(2,1)S(1)} %collective-permute-done.3.refs_2_), channel_id=1, source_target_pairs={{0,2},{1,3},{2,0},{3,1},{4,6},{5,7},{6,4},{7,5},{8,10},{9,11},{10,... | collective-permute-start | bytes 405512 | tf_op jit(solution)/shard_map/ppermute | solution.py:436
  34.4 11.7 %collective-permute-start.11 = (bf16[528,128]{1,0:T(8,128)(2,1)S(1)}, bf16[528,128]{1,0:T(8,128)(2,1)S(1)}, u32[]{:S(2)}, u32[]{:S(2)}) collective-permute-start(bf16[528,128]{1,0:T(8,128)(2,1)S(1)} %collective-permute-done.6.refs_1_), channel_id=1, source_target_pairs={{0,2},{1,3},{2,0},{3,1},{4,6},{5,7},{6,4},{7,5},{8,10},{9,11},{10,... | collective-permute-start | bytes 405512 | tf_op jit(solution)/shard_map/ppermute | solution.py:436
  34.6 11.4 %collective-permute-start.12 = (bf16[528,128]{1,0:T(8,128)(2,1)S(1)}, bf16[528,128]{1,0:T(8,128)(2,1)S(1)}, u32[]{:S(2)}, u32[]{:S(2)}) collective-permute-start(bf16[528,128]{1,0:T(8,128)(2,1)S(1)} %collective-permute-done.7.refs_2_), channel_id=1, source_target_pairs={{0,2},{1,3},{2,0},{3,1},{4,6},{5,7},{6,4},{7,5},{8,10},{9,11},{10,... | collective-permute-start | bytes 405512 | tf_op jit(solution)/shard_map/ppermute | solution.py:436
  38.4 10.1 %collective-permute-start.13 = (bf16[128,1024]{1,0:T(8,128)(2,1)S(1)}, bf16[128,1024]{1,0:T(8,128)(2,1)S(1)}, u32[]{:S(2)}, u32[]{:S(2)}) collective-permute-start(bf16[128,1024]{1,0:T(8,128)(2,1)S(1)} %get-tuple-element.85), channel_id=1, source_target_pairs={{0,1},{1,0},{2,3},{3,2},{4,5},{5,4},{6,7},{7,6},{8,9},{9,8},{10,11... | collective-permute-start | bytes 786440 | tf_op jit(solution)/shard_map/ppermute | solution.py:436
  48.4 1.6 %collective-permute-start.14 = (bf16[128,1024]{1,0:T(8,128)(2,1)S(1)}, bf16[128,1024]{1,0:T(8,128)(2,1)S(1)}, u32[]{:S(2)}, u32[]{:S(2)}) collective-permute-start(bf16[128,1024]{1,0:T(8,128)(2,1)S(1)} %get-tuple-element.86), channel_id=1, source_target_pairs={{0,1},{1,0},{2,3},{3,2},{4,5},{5,4},{6,7},{7,6},{8,9},{9,8},{10,11... | collective-permute-start | bytes 786440 | tf_op jit(solution)/shard_map/ppermute | solution.py:436

commit v4 on v3

--- a/solution.py
+++ b/solution.py
@@ -186,9 +186,14 @@
 
 
 def terms(tile, run):
-    key = tile[run : run + 1]
     value = tile[RUNS + run : RUNS + run + 1]
-    return wide(key * (LOG2E * INV_ROOT)), wide(jnp.log2(value)), wide(1.0 / value)
+    return wide(jnp.log2(value)), wide(1.0 / value)
+
+
+def scaled_keys(keys, scale):
+    whole = keys.astype(F32) * (scale * (LOG2E * INV_ROOT))
+    high = whole.astype(BF16)
+    return jnp.concatenate([high, (whole - high.astype(F32)).astype(BF16)], axis=1)
 
 
 UNIT = None
@@ -218,7 +223,7 @@
             part = part if mask is None else jnp.where(mask, part, masked_score)
             part = part.reshape(BLK // 8, 8, TILE)
             parts.append(part)
-            top = jnp.max(part, axis=0) * (LOG2E * INV_ROOT if term is UNIT else term[0])
+            top = jnp.max(part, axis=0)
             if dead is not None:
                 top = jnp.where(dead, masked_score, top)
             highest = jnp.maximum(highest, top)
@@ -230,13 +235,12 @@
             total = before[SUM_ROW : SUM_ROW + 8, cols] * factor
         rounded = []
         for part, (term, dead, mask) in zip(parts, blocks):
-            shift = reference if term is UNIT else reference - term[1]
+            shift = reference if term is UNIT else reference - term[0]
             if dead is not None:
                 shift = jnp.where(dead, -masked_score, shift)
-            scaled = part * (LOG2E * INV_ROOT if term is UNIT else term[0])
-            weights = jnp.exp2(scaled - shift)
+            weights = jnp.exp2(part - shift)
             summed = jnp.sum(weights, axis=0)
-            total = total + (summed if term is UNIT else summed * term[2])
+            total = total + (summed if term is UNIT else summed * term[1])
             rounded.append(weights.reshape(BLK, TILE).astype(BF16))
         rounded = jnp.concatenate(rounded, axis=0) if len(rounded) > 1 else rounded[0]
         product = jnp.dot(values_t, rounded, preferred_element_type=F32)
@@ -266,14 +270,19 @@
             for r in range(RUNS):
                 c = counts[RUNS * i + r]
                 blocks.append((terms(tile, r),) + ((None, place < c) if masked else (c < BLK, None)))
-        keys = [pieces[i][:PAIR, :] for i in range(n)]
+        keys = []
+        for i in range(n):
+            tile = pieces[i][2 * PAIR :, :].astype(F32)
+            for r in range(RUNS):
+                block = pieces[i][r * BLK : (r + 1) * BLK, :]
+                keys.append(scaled_keys(block, tile[r : r + 1]))
         values = [pieces[i][PAIR : 2 * PAIR, :].T for i in range(n)]
         blocks_of = lambda t: blocks
         if extra is not None:
-            keys = [extra[0]] + keys
+            keys = [scaled_keys(extra[0], 1.0)] + keys
             values = [extra[1]] + values
             blocks_of = lambda t: extra[2](t) + blocks
-        keys = jnp.concatenate(keys, axis=0) if len(keys) > 1 else keys[0]
+        keys = jnp.concatenate(keys, axis=0)
         values = jnp.concatenate(values, axis=1) if len(values) > 1 else values[0]
         fold(q, keys, values, before, after, blocks_of)
 
@@ -300,14 +309,17 @@
         for h in range(PER):
             rows = pl.ds(h * ROWS, ROWS)
             others = pl.ds(WIDE + h * ROWS, ROWS)
-            q_all[slot, :, rows] = own_q[slot, :, h * HD : (h + 1) * HD].T
-            q_all[slot, :, others] = swap[slot, :, h * HD : (h + 1) * HD].T
+            mine = own_q[slot, :, h * HD : (h + 1) * HD].T
+            theirs = swap[slot, :, h * HD : (h + 1) * HD].T
+            for copy in range(2):
+                q_all[slot, copy * HD : (copy + 1) * HD, rows] = mine
+                q_all[slot, copy * HD : (copy + 1) * HD, others] = theirs
 
 
 def prepare_call(swap, own_q, own_kv):
     return pl.pallas_call(
         prepare_kernel,
-        out_shape=[pltpu.VMEM((2, 2, 2 * ROWS, HD), BF16), pltpu.VMEM((2, HD, BOTH), BF16)],
+        out_shape=[pltpu.VMEM((2, 2, 2 * ROWS, HD), BF16), pltpu.VMEM((2, 2 * HD, BOTH), BF16)],
         in_specs=[IN_VMEM] * 3,
         out_specs=[IN_VMEM] * 2,
         compiler_params=pltpu.CompilerParams(vmem_limit_bytes=VMEM_LIMIT),
@@ -459,9 +471,9 @@
     states = own_call(meta, q_all, kv, own)
     near[2], states = lax.optimization_barrier((near[2], states))
     near_in[3] = permute(near[2], "pool", POOL, 3)
-    states = add_call(meta, q_all, states, [near_in[1]], (0, 1), (1,), early=early)
-    far[2], far[3], near_in[2], far_in[4], far_in[5], states = lax.optimization_barrier(
-        (far[2], far[3], near_in[2], far_in[4], far_in[5], states)
+    states = add_call(meta, q_all, states, [near_in[1], near_in[2]], (0, 1), (1, 2), early=early)
+    far[2], far[3], far_in[4], far_in[5], states = lax.optimization_barrier(
+        (far[2], far[3], far_in[4], far_in[5], states)
     )
     for k in (6, 7):
         far_in[k] = permute(far[k - 4], "pool", POOL, k)
@@ -469,7 +481,7 @@
         across[k] = permute(far_in[k], "blk", 4, 2)
     states = add_call(meta, q_all, states, [far_in[4], far_in[5]], (0,), (4, 5))
     near_in[3], states = lax.optimization_barrier((near_in[3], states))
-    states = add_call(meta, q_all, states, [near_in[2], near_in[3]], (0, 1), (2, 3))
+    states = add_call(meta, q_all, states, [near_in[3]], (0, 1), (3,))
     far_in[6], far_in[7], states = lax.optimization_barrier((far_in[6], far_in[7], states))
     for k in (6, 7):
         across[k] = permute(far_in[k], "blk", 4, 2)

time: 51.3 us -> 50.8 us (level)
  the two profiles are of different devices: /device:TPU:25 before, /device:TPU:9 now
where the time goes in v4:
time: 50.8 us; the launch traced here: 50.2 us
  Pallas kernels  26.2 us (52%)
  starting transfers between devices  16.5 us (32%)
  waiting for transfers between devices  7.09 us (14%)
    ppermute x15, starting transfers between devices, permute(): return lax.ppermute(x, axis, [(i, i ^ k) for i in range(count)])  16.5 us
    pallas_call x6, Pallas kernels, add_call(): pl.pallas_call(functools.partial(add_kernel, slots, ks, early is not None...  16.2 us
    ppermute x15, waiting for transfers between devices, permute(): return lax.ppermute(x, axis, [(i, i ^ k) for i in range(count)])  7.09 us
    pallas_call x1, Pallas kernels, gather_call(): pl.pallas_call(gather_kernel, out_shape=[jax.ShapeDtypeStruct((META_SIZE,...  4.33 us
    pallas_call x1, Pallas kernels, own_call(): pl.pallas_call(own_kernel, out_shape=state_shapes(2), in_specs=[IN_SMEM]...  3.47 us
    pallas_call x1, Pallas kernels, join_call(): pl.pallas_call(join_kernel, out_shape=jax.ShapeDtypeStruct((ROWS, QH * HD...  1.66 us
  transfers between devices with their start and end apart: 15, of which 4 were waited for; matrix products, arithmetic and copies ran while one was open for 0% of the time, Pallas kernels for 40%

profile of v4, /device:TPU:9, one launch (start us, length us, event | category | flops | bytes accessed | tf_op | source)
XLA Modules:
  0.0 50.2 jit_solution(9529862581788350759)
XLA Ops:
  0.1 4.3 %shard_map.82 = (s32[24]{0:T(128)S(1)}, bf16[2,128,1280]{2,1,0:T(8,128)(2,1)S(1)}, bf16[528,128]{1,0:T(8,128)(2,1)S(1)}, bf16[528,128]{1,0:T(8,128)(2,1)S(1)}, b...) custom-call(s32[2]{0:T(128)S(1)} %pad_add_fusion.ids, ...), custom_call_target="tpu_custom_call" | custom-call | flops 1024 | bytes 1024 | tf_op jit(solution)/shard_map/pallas_call | solution.py:160
  4.4 0.7 %collective-permute-start = (bf16[2,128,1280]{2,1,0:T(8,128)(2,1)S(1)}, bf16[2,128,1280]{2,1,0:T(8,128)(2,1)S(1)}, u32[]{:S(2)}, u32[]{:S(2)}) collective-permute-start(bf16[2,128,1280]{2,1,0:T(8,128)(2,1)S(1)} %get-tuple-element.46), channel_id=1, source_target_pairs={{0,1},{1,0},{2,3},{3,2},{4,5},{5,4},{6,7},{7,6},{8,9},{9,8},{10,11... | collective-permute-start | bytes 1966088 | tf_op jit(solution)/shard_map/ppermute | solution.py:448
  5.2 1.2 %collective-permute-start.3 = (bf16[2,528,128]{2,1,0:T(8,128)(2,1)S(1)}, bf16[2,528,128]{2,1,0:T(8,128)(2,1)S(1)}, u32[]{:S(2)}, u32[]{:S(2)}) collective-permute-start(bf16[2,528,128]{2,1,0:T(8,128)(2,1)S(1)} %get-tuple-element.61), channel_id=1, source_target_pairs={{0,4},{4,0},{8,12},{12,8},{16,20},{20,16},{24,28},{28,24},{1,5},{5... | collective-permute-start | bytes 811016 | tf_op jit(solution)/shard_map/ppermute | solution.py:448
  6.9 0.6 %shard_map.83 = (bf16[2,2,256,128]{3,2,1,0:T(8,128)(2,1)S(1)}, bf16[2,256,2048]{2,1,0:T(8,128)(2,1)S(1)}) custom-call(bf16[2,128,1280]{2,1,0:T(8,128)(2,1)S(1)} %collective-permute-done.swap, bf16[2,128,1024]{2,1,0:T(8,128)(2,1)S(1)} %get-tuple-element.47.own_q, bf16[2,256,128]{2,1,0:T(8,128)(2,1)S(1)} %get-tuple-element.48.own_kv), custom_call_target="tpu_custom_call" | custom-call | flops 1024 | bytes 1024 | tf_op jit(solution)/shard_map/pallas_call | solution.py:320
  7.5 1.3 %collective-permute-start.5 = (bf16[2,2,256,128]{3,2,1,0:T(8,128)(2,1)S(1)}, bf16[2,2,256,128]{3,2,1,0:T(8,128)(2,1)S(1)}, u32[]{:S(2)}, u32[]{:S(2)}) collective-permute-start(bf16[2,2,256,128]{3,2,1,0:T(8,128)(2,1)S(1)} %get-tuple-element.55.kv), channel_id=1, source_target_pairs={{0,2},{1,3},{2,0},{3,1},{4,6},{5,7},{6,4},{7,5},{8,10},{9,11},{10,... | collective-permute-start | bytes 786440 | tf_op jit(solution)/shard_map/ppermute | solution.py:448
  8.8 2.3 %collective-permute-start.1 = (bf16[528,128]{1,0:T(8,128)(2,1)S(1)}, bf16[528,128]{1,0:T(8,128)(2,1)S(1)}, u32[]{:S(2)}, u32[]{:S(2)}) collective-permute-start(bf16[528,128]{1,0:T(8,128)(2,1)S(1)} %get-tuple-element.52), channel_id=1, source_target_pairs={{0,16},{4,20},{8,24},{12,28},{16,0},{20,4},{24,8},{28,12},{1,17},{... | collective-permute-start | bytes 405512 | tf_op jit(solution)/shard_map/ppermute | solution.py:448
  11.1 1.0 %collective-permute-start.2 = (bf16[528,128]{1,0:T(8,128)(2,1)S(1)}, bf16[528,128]{1,0:T(8,128)(2,1)S(1)}, u32[]{:S(2)}, u32[]{:S(2)}) collective-permute-start(bf16[528,128]{1,0:T(8,128)(2,1)S(1)} %get-tuple-element.53), channel_id=1, source_target_pairs={{0,20},{4,16},{8,28},{12,24},{16,4},{20,0},{24,12},{28,8},{1,21},{... | collective-permute-start | bytes 405512 | tf_op jit(solution)/shard_map/ppermute | solution.py:448
  12.1 3.5 %shard_map.84 = (f32[144,2048]{1,0:T(8,128)S(1)}, f32[144,2048]{1,0:T(8,128)S(1)}) custom-call(s32[24]{0:T(128)S(1)} %get-tuple-element.45.meta, bf16[2,256,2048]{2,1,0:T(8,128)(2,1)S(1)} %get-tuple-element.49.q_all, bf16[2,2,256,128]{3,2,1,0:T(8,128)(2,1)S(1)} %get-tuple-element.55.kv, bf16[2,528,128]{2,1,0:T(8,128)(2,1)S(1)} %get-tuple-element.56.own), custom_call_target="tpu_custom_call" | custom-call | flops 1024 | bytes 1024 | tf_op jit(solution)/shard_map/pallas_call | solution.py:357
  15.6 1.0 %collective-permute-start.8 = (bf16[2,528,128]{2,1,0:T(8,128)(2,1)S(1)}, bf16[2,528,128]{2,1,0:T(8,128)(2,1)S(1)}, u32[]{:S(2)}, u32[]{:S(2)}) collective-permute-start(bf16[2,528,128]{2,1,0:T(8,128)(2,1)S(1)} %get-tuple-element.67), channel_id=1, source_target_pairs={{0,12},{4,8},{8,4},{12,0},{16,28},{20,24},{24,20},{28,16},{1,13},{... | collective-permute-start | bytes 811016 | tf_op jit(solution)/shard_map/ppermute | solution.py:448
  16.6 5.2 %shard_map.85 = (f32[144,2048]{1,0:T(8,128)S(1)}, f32[144,2048]{1,0:T(8,128)S(1)}) custom-call(s32[24]{0:T(128)S(1)} %get-tuple-element.45.meta, bf16[2,256,2048]{2,1,0:T(8,128)(2,1)S(1)} %get-tuple-element.49.q_all, f32[144,2048]{1,0:T(8,128)S(1)} %get-tuple-element.59.refs_0_, f32[144,2048]{1,0:T(8,128)S(1)} %get-tuple-element.60.refs_1_, ...), custom_call_target="tpu_custom_call" | custom-call | flops 1024 | bytes 1024 | tf_op jit(solution)/shard_map/pallas_call | solution.py:407
  21.8 0.4 collective-permute-done.2.refs_2_
  22.2 1.3 %collective-permute-start.6 = (bf16[528,128]{1,0:T(8,128)(2,1)S(1)}, bf16[528,128]{1,0:T(8,128)(2,1)S(1)}, u32[]{:S(2)}, u32[]{:S(2)}) collective-permute-start(bf16[528,128]{1,0:T(8,128)(2,1)S(1)} %get-tuple-element.65), channel_id=1, source_target_pairs={{0,24},{4,28},{8,16},{12,20},{16,8},{20,12},{24,0},{28,4},{1,25},{... | collective-permute-start | bytes 405512 | tf_op jit(solution)/shard_map/ppermute | solution.py:448
  23.5 1.3 %collective-permute-start.7 = (bf16[528,128]{1,0:T(8,128)(2,1)S(1)}, bf16[528,128]{1,0:T(8,128)(2,1)S(1)}, u32[]{:S(2)}, u32[]{:S(2)}) collective-permute-start(bf16[528,128]{1,0:T(8,128)(2,1)S(1)} %get-tuple-element.66), channel_id=1, source_target_pairs={{0,28},{4,24},{8,20},{12,16},{16,12},{20,8},{24,4},{28,0},{1,29},{... | collective-permute-start | bytes 405512 | tf_op jit(solution)/shard_map/ppermute | solution.py:448
  24.8 1.4 %collective-permute-start.10 = (bf16[528,128]{1,0:T(8,128)(2,1)S(1)}, bf16[528,128]{1,0:T(8,128)(2,1)S(1)}, u32[]{:S(2)}, u32[]{:S(2)}) collective-permute-start(bf16[528,128]{1,0:T(8,128)(2,1)S(1)} %collective-permute-done.2.refs_2_), channel_id=1, source_target_pairs={{0,2},{1,3},{2,0},{3,1},{4,6},{5,7},{6,4},{7,5},{8,10},{9,11},{10,... | collective-permute-start | bytes 405512 | tf_op jit(solution)/shard_map/ppermute | solution.py:448
  26.3 2.0 %shard_map.86.refs_0_ = f32[144,2048]{1,0:T(8,128)S(1)} custom-call(s32[24]{0:T(128)S(1)} %get-tuple-element.45.meta, bf16[2,256,2048]{2,1,0:T(8,128)(2,1)S(1)} %get-tuple-element.49.q_all, f32[144,2048]{1,0:T(8,128)S(1)} %get-tuple-element.68.refs_0_, bf16[528,128]{1,0:T(8,128)(2,1)S(1)} %collective-permute-done.1.refs_1_, ...), custom_call_target="tpu_custom_call" | custom-call | flops 1024 | bytes 1024 | tf_op jit(solution)/shard_map/pallas_call | solution.py:407
  28.3 2.4 %shard_map.87 = (f32[144,2048]{1,0:T(8,128)S(1)}, f32[144,2048]{1,0:T(8,128)S(1)}) custom-call(s32[24]{0:T(128)S(1)} %get-tuple-element.45.meta, bf16[2,256,2048]{2,1,0:T(8,128)(2,1)S(1)} %get-tuple-element.49.q_all, f32[144,2048]{1,0:T(8,128)S(1)} %shard_map.86.refs_0_, f32[144,2048]{1,0:T(8,128)S(1)} %get-tuple-element.73.refs_1_, ...), custom_call_target="tpu_custom_call" | custom-call | flops 1024 | bytes 1024 | tf_op jit(solution)/shard_map/pallas_call | solution.py:407
  30.7 4.8 %collective-permute-done.7.refs_2_ = bf16[528,128]{1,0:T(8,128)(2,1)S(1)} collective-permute-done((bf16[528,128]{1,0:T(8,128)(2,1)S(1)}, bf16[528,128]{1,0:T(8,128)(2,1)S(1)}, u32[]{:S(2)}, u32[]{:S(2)}) %collective-permute-start.7) | collective-permute-done | bytes 135200 | tf_op jit(solution)/shard_map/ppermute | solution.py:448
  35.7 1.3 %collective-permute-start.12 = (bf16[528,128]{1,0:T(8,128)(2,1)S(1)}, bf16[528,128]{1,0:T(8,128)(2,1)S(1)}, u32[]{:S(2)}, u32[]{:S(2)}) collective-permute-start(bf16[528,128]{1,0:T(8,128)(2,1)S(1)} %collective-permute-done.7.refs_2_), channel_id=1, source_target_pairs={{0,2},{1,3},{2,0},{3,1},{4,6},{5,7},{6,4},{7,5},{8,10},{9,11},{10,... | collective-permute-start | bytes 405512 | tf_op jit(solution)/shard_map/ppermute | solution.py:448
  37.0 2.4 %shard_map.88 = (bf16[128,1024]{1,0:T(8,128)(2,1)S(1)}, bf16[128,1024]{1,0:T(8,128)(2,1)S(1)}) custom-call(s32[24]{0:T(128)S(1)} %get-tuple-element.45.meta, bf16[2,256,2048]{2,1,0:T(8,128)(2,1)S(1)} %get-tuple-element.49.q_all, f32[144,2048]{1,0:T(8,128)S(1)} %get-tuple-element.77.refs_0_, bf16[528,128]{1,0:T(8,128)(2,1)S(1)} %collective-permute-done.6.refs_1_, ...), custom_call_target="tpu_custom_call" | custom-call | flops 1024 | bytes 1024 | tf_op jit(solution)/shard_map/pallas_call | solution.py:407
  39.4 3.1 %collective-permute-start.13 = (bf16[128,1024]{1,0:T(8,128)(2,1)S(1)}, bf16[128,1024]{1,0:T(8,128)(2,1)S(1)}, u32[]{:S(2)}, u32[]{:S(2)}) collective-permute-start(bf16[128,1024]{1,0:T(8,128)(2,1)S(1)} %get-tuple-element.83), channel_id=1, source_target_pairs={{0,1},{1,0},{2,3},{3,2},{4,5},{5,4},{6,7},{7,6},{8,9},{9,8},{10,11... | collective-permute-start | bytes 786440 | tf_op jit(solution)/shard_map/ppermute | solution.py:448
  42.5 2.0 %shard_map.89.refs_0_ = f32[144,2048]{1,0:T(8,128)S(1)} custom-call(s32[24]{0:T(128)S(1)} %get-tuple-element.45.meta, bf16[2,256,2048]{2,1,0:T(8,128)(2,1)S(1)} %get-tuple-element.49.q_all, f32[144,2048]{1,0:T(8,128)S(1)} %get-tuple-element.81.refs_0_, bf16[528,128]{1,0:T(8,128)(2,1)S(1)} %collective-permute-done.9.refs_1_, ...), custom_call_target="tpu_custom_call" | custom-call | flops 1024 | bytes 1024 | tf_op jit(solution)/shard_map/pallas_call | solution.py:407
  44.6 2.2 %shard_map.90 = (bf16[128,1024]{1,0:T(8,128)(2,1)S(1)}, bf16[128,1024]{1,0:T(8,128)(2,1)S(1)}) custom-call(s32[24]{0:T(128)S(1)} %get-tuple-element.45.meta, bf16[2,256,2048]{2,1,0:T(8,128)(2,1)S(1)} %get-tuple-element.49.q_all, f32[144,2048]{1,0:T(8,128)S(1)} %shard_map.89.refs_0_, bf16[528,128]{1,0:T(8,128)(2,1)S(1)} %collective-permute-done.11.refs_1_, ...), custom_call_target="tpu_custom_call" | custom-call | flops 1024 | bytes 1024 | tf_op jit(solution)/shard_map/pallas_call | solution.py:407
  46.8 1.5 %collective-permute-done.14.refs_3_ = bf16[128,1024]{1,0:T(8,128)(2,1)S(1)} collective-permute-done((bf16[128,1024]{1,0:T(8,128)(2,1)S(1)}, bf16[128,1024]{1,0:T(8,128)(2,1)S(1)}, u32[]{:S(2)}, u32[]{:S(2)}) %collective-permute-start.14) | collective-permute-done | bytes 262176 | tf_op jit(solution)/shard_map/ppermute | solution.py:448
  48.4 1.7 %shard_map.91 = bf16[128,4096]{1,0:T(8,128)(2,1)} custom-call(s32[24]{0:T(128)} %copy-done, bf16[128,1024]{1,0:T(8,128)(2,1)S(1)} %get-tuple-element.80.refs_0_, bf16[128,1024]{1,0:T(8,128)(2,1)S(1)} %get-tuple-element.82.refs_1_, bf16[128,1024]{1,0:T(8,128)(2,1)S(1)} %collective-permute-done.13.refs_2_, bf16[128,1024]{1,0:T(8,128)(2,1)S(1)} %collective-permute-done.14.refs_3_), custom_call_target="tpu_custom_call" | custom-call | flops 1024 | bytes 1024 | tf_op jit(solution)/shard_map/pallas_call | solution.py:437
  (19 shorter events, 1.0 us)
Async XLA Ops:
  4.4 40.1 %copy-start = (s32[24]{0:T(128)}, s32[24]{0:T(128)S(1)}, u32[]{:S(2)}) copy-start(s32[24]{0:T(128)S(1)} %get-tuple-element.45.meta) | copy-start | bytes 292
  4.4 2.5 %collective-permute-start = (bf16[2,128,1280]{2,1,0:T(8,128)(2,1)S(1)}, bf16[2,128,1280]{2,1,0:T(8,128)(2,1)S(1)}, u32[]{:S(2)}, u32[]{:S(2)}) collective-permute-start(bf16[2,128,1280]{2,1,0:T(8,128)(2,1)S(1)} %get-tuple-element.46), channel_id=1, source_target_pairs={{0,1},{1,0},{2,3},{3,2},{4,5},{5,4},{6,7},{7,6},{8,9},{9,8},{10,11... | collective-permute-start | bytes 1966088 | tf_op jit(solution)/shard_map/ppermute | solution.py:448
  5.2 10.4 %collective-permute-start.3 = (bf16[2,528,128]{2,1,0:T(8,128)(2,1)S(1)}, bf16[2,528,128]{2,1,0:T(8,128)(2,1)S(1)}, u32[]{:S(2)}, u32[]{:S(2)}) collective-permute-start(bf16[2,528,128]{2,1,0:T(8,128)(2,1)S(1)} %get-tuple-element.61), channel_id=1, source_target_pairs={{0,4},{4,0},{8,12},{12,8},{16,20},{20,16},{24,28},{28,24},{1,5},{5... | collective-permute-start | bytes 811016 | tf_op jit(solution)/shard_map/ppermute | solution.py:448
  6.4 10.2 %collective-permute-start.4 = (bf16[2,528,128]{2,1,0:T(8,128)(2,1)S(1)}, bf16[2,528,128]{2,1,0:T(8,128)(2,1)S(1)}, u32[]{:S(2)}, u32[]{:S(2)}) collective-permute-start(bf16[2,528,128]{2,1,0:T(8,128)(2,1)S(1)} %get-tuple-element.62), channel_id=1, source_target_pairs={{0,8},{4,12},{8,0},{12,4},{16,24},{20,28},{24,16},{28,20},{1,9},{5... | collective-permute-start | bytes 811016 | tf_op jit(solution)/shard_map/ppermute | solution.py:448
  7.5 9.1 %collective-permute-start.5 = (bf16[2,2,256,128]{3,2,1,0:T(8,128)(2,1)S(1)}, bf16[2,2,256,128]{3,2,1,0:T(8,128)(2,1)S(1)}, u32[]{:S(2)}, u32[]{:S(2)}) collective-permute-start(bf16[2,2,256,128]{3,2,1,0:T(8,128)(2,1)S(1)} %get-tuple-element.55.kv), channel_id=1, source_target_pairs={{0,2},{1,3},{2,0},{3,1},{4,6},{5,7},{6,4},{7,5},{8,10},{9,11},{10,... | collective-permute-start | bytes 786440 | tf_op jit(solution)/shard_map/ppermute | solution.py:448
  8.8 13.0 %collective-permute-start.1 = (bf16[528,128]{1,0:T(8,128)(2,1)S(1)}, bf16[528,128]{1,0:T(8,128)(2,1)S(1)}, u32[]{:S(2)}, u32[]{:S(2)}) collective-permute-start(bf16[528,128]{1,0:T(8,128)(2,1)S(1)} %get-tuple-element.52), channel_id=1, source_target_pairs={{0,16},{4,20},{8,24},{12,28},{16,0},{20,4},{24,8},{28,12},{1,17},{... | collective-permute-start | bytes 405512 | tf_op jit(solution)/shard_map/ppermute | solution.py:448
  11.1 11.1 %collective-permute-start.2 = (bf16[528,128]{1,0:T(8,128)(2,1)S(1)}, bf16[528,128]{1,0:T(8,128)(2,1)S(1)}, u32[]{:S(2)}, u32[]{:S(2)}) collective-permute-start(bf16[528,128]{1,0:T(8,128)(2,1)S(1)} %get-tuple-element.53), channel_id=1, source_target_pairs={{0,20},{4,16},{8,28},{12,24},{16,4},{20,0},{24,12},{28,8},{1,21},{... | collective-permute-start | bytes 405512 | tf_op jit(solution)/shard_map/ppermute | solution.py:448
  15.6 12.7 %collective-permute-start.8 = (bf16[2,528,128]{2,1,0:T(8,128)(2,1)S(1)}, bf16[2,528,128]{2,1,0:T(8,128)(2,1)S(1)}, u32[]{:S(2)}, u32[]{:S(2)}) collective-permute-start(bf16[2,528,128]{2,1,0:T(8,128)(2,1)S(1)} %get-tuple-element.67), channel_id=1, source_target_pairs={{0,12},{4,8},{8,4},{12,0},{16,28},{20,24},{24,20},{28,16},{1,13},{... | collective-permute-start | bytes 811016 | tf_op jit(solution)/shard_map/ppermute | solution.py:448
  22.2 8.5 %collective-permute-start.6 = (bf16[528,128]{1,0:T(8,128)(2,1)S(1)}, bf16[528,128]{1,0:T(8,128)(2,1)S(1)}, u32[]{:S(2)}, u32[]{:S(2)}) collective-permute-start(bf16[528,128]{1,0:T(8,128)(2,1)S(1)} %get-tuple-element.65), channel_id=1, source_target_pairs={{0,24},{4,28},{8,16},{12,20},{16,8},{20,12},{24,0},{28,4},{1,25},{... | collective-permute-start | bytes 405512 | tf_op jit(solution)/shard_map/ppermute | solution.py:448
  23.5 12.0 %collective-permute-start.7 = (bf16[528,128]{1,0:T(8,128)(2,1)S(1)}, bf16[528,128]{1,0:T(8,128)(2,1)S(1)}, u32[]{:S(2)}, u32[]{:S(2)}) collective-permute-start(bf16[528,128]{1,0:T(8,128)(2,1)S(1)} %get-tuple-element.66), channel_id=1, source_target_pairs={{0,28},{4,24},{8,20},{12,16},{16,12},{20,8},{24,4},{28,0},{1,29},{... | collective-permute-start | bytes 405512 | tf_op jit(solution)/shard_map/ppermute | solution.py:448
  24.8 17.7 %collective-permute-start.9 = (bf16[528,128]{1,0:T(8,128)(2,1)S(1)}, bf16[528,128]{1,0:T(8,128)(2,1)S(1)}, u32[]{:S(2)}, u32[]{:S(2)}) collective-permute-start(bf16[528,128]{1,0:T(8,128)(2,1)S(1)} %collective-permute-done.1.refs_1_), channel_id=1, source_target_pairs={{0,2},{1,3},{2,0},{3,1},{4,6},{5,7},{6,4},{7,5},{8,10},{9,11},{10,... | collective-permute-start | bytes 405512 | tf_op jit(solution)/shard_map/ppermute | solution.py:448
  24.8 17.7 %collective-permute-start.10 = (bf16[528,128]{1,0:T(8,128)(2,1)S(1)}, bf16[528,128]{1,0:T(8,128)(2,1)S(1)}, u32[]{:S(2)}, u32[]{:S(2)}) collective-permute-start(bf16[528,128]{1,0:T(8,128)(2,1)S(1)} %collective-permute-done.2.refs_2_), channel_id=1, source_target_pairs={{0,2},{1,3},{2,0},{3,1},{4,6},{5,7},{6,4},{7,5},{8,10},{9,11},{10,... | collective-permute-start | bytes 405512 | tf_op jit(solution)/shard_map/ppermute | solution.py:448
  35.5 9.0 %collective-permute-start.11 = (bf16[528,128]{1,0:T(8,128)(2,1)S(1)}, bf16[528,128]{1,0:T(8,128)(2,1)S(1)}, u32[]{:S(2)}, u32[]{:S(2)}) collective-permute-start(bf16[528,128]{1,0:T(8,128)(2,1)S(1)} %collective-permute-done.6.refs_1_), channel_id=1, source_target_pairs={{0,2},{1,3},{2,0},{3,1},{4,6},{5,7},{6,4},{7,5},{8,10},{9,11},{10,... | collective-permute-start | bytes 405512 | tf_op jit(solution)/shard_map/ppermute | solution.py:448
  35.7 8.8 %collective-permute-start.12 = (bf16[528,128]{1,0:T(8,128)(2,1)S(1)}, bf16[528,128]{1,0:T(8,128)(2,1)S(1)}, u32[]{:S(2)}, u32[]{:S(2)}) collective-permute-start(bf16[528,128]{1,0:T(8,128)(2,1)S(1)} %collective-permute-done.7.refs_2_), channel_id=1, source_target_pairs={{0,2},{1,3},{2,0},{3,1},{4,6},{5,7},{6,4},{7,5},{8,10},{9,11},{10,... | collective-permute-start | bytes 405512 | tf_op jit(solution)/shard_map/ppermute | solution.py:448
  39.4 7.4 %collective-permute-start.13 = (bf16[128,1024]{1,0:T(8,128)(2,1)S(1)}, bf16[128,1024]{1,0:T(8,128)(2,1)S(1)}, u32[]{:S(2)}, u32[]{:S(2)}) collective-permute-start(bf16[128,1024]{1,0:T(8,128)(2,1)S(1)} %get-tuple-element.83), channel_id=1, source_target_pairs={{0,1},{1,0},{2,3},{3,2},{4,5},{5,4},{6,7},{7,6},{8,9},{9,8},{10,11... | collective-permute-start | bytes 786440 | tf_op jit(solution)/shard_map/ppermute | solution.py:448
  46.8 1.6 %collective-permute-start.14 = (bf16[128,1024]{1,0:T(8,128)(2,1)S(1)}, bf16[128,1024]{1,0:T(8,128)(2,1)S(1)}, u32[]{:S(2)}, u32[]{:S(2)}) collective-permute-start(bf16[128,1024]{1,0:T(8,128)(2,1)S(1)} %get-tuple-element.84), channel_id=1, source_target_pairs={{0,1},{1,0},{2,3},{3,2},{4,5},{5,4},{6,7},{7,6},{8,9},{9,8},{10,11... | collective-permute-start | bytes 786440 | tf_op jit(solution)/shard_map/ppermute | solution.py:448

commit v5 on v4

--- a/solution.py
+++ b/solution.py
@@ -65,21 +65,6 @@
     dst[pl.ds(2 * PAIR, 16), :] = rows.astype(BF16)
 
 
-def piece_copies(cache, locals_, head, dst, sems, first):
-    made = []
-    for half in range(2):
-        column = pl.multiple_of((half * KVH + head) * HD, HD)
-        for run in range(RUNS):
-            made.append(
-                pltpu.make_async_copy(
-                    cache.at[locals_[run], :, pl.ds(column, HD)],
-                    dst.at[pl.ds(half * PAIR + run * BLK, BLK), :],
-                    sems.at[first + 2 * half + run],
-                )
-            )
-    return made
-
-
 PIECE_1 = pltpu.VMEM((PIECE, HD), BF16)
 PIECE_2 = pltpu.VMEM((2, PIECE, HD), BF16)
 SWAP = WIDE + 2 * HD
@@ -91,7 +76,7 @@
     far, near, own = refs[7:11], refs[11:14], refs[14]
     own_q, own_kv = refs[15:17]
     table, groups, lengths, suffixes, cache_scale = refs[17:22]
-    spread, table_sems, more_sems, sems = refs[22:]
+    spread, stage, table_sems, more_sems, stage_sems = refs[22:]
     p = ids[0]
     m = ids[1]
     loads = [
@@ -99,6 +84,14 @@
     ]
     for c in loads:
         c.start()
+    staged = []
+    for i in range(4):
+        column = pl.multiple_of((i % 2 * KVH + (m ^ (2 * (i // 2)))) * HD, HD)
+        c = pltpu.make_async_copy(
+            cache.at[:, :, pl.ds(column, HD)], stage.at[i], stage_sems.at[i]
+        )
+        c.start()
+        staged.append(c)
     made = []
     for slot in range(2):
         mine = m ^ (2 * slot)
@@ -125,7 +118,6 @@
     jobs += [(1 + i, (0, 1), (ref.at[0], ref.at[1])) for i, ref in enumerate(near)]
     jobs += [(0, (0, 1), (own.at[0], own.at[1]))]
     pending = []
-    count = 0
     for k, slots, outs in jobs:
         session = groups[p ^ k]
         locals_ = []
@@ -136,11 +128,6 @@
                 local = jnp.where((at >= 0) & (at < slot_count), at, local)
             locals_.append(local)
         for slot, out in zip(slots, outs):
-            group = piece_copies(cache, locals_, m ^ (2 * slot), out, sems, count)
-            count += 4
-            for c in group:
-                c.start()
-            made += group
             pending.append((locals_, slot, out))
     mine = groups[p]
     for run in range(RUNS):
@@ -152,6 +139,13 @@
     spread_scales(cache_scale, m, spread)
     for locals_, slot, out in pending:
         write_scales(spread, locals_, slot, out)
+    for c in staged:
+        c.wait()
+    for locals_, slot, out in pending:
+        for half in range(2):
+            for run in range(RUNS):
+                rows = pl.ds(half * PAIR + run * BLK, BLK)
+                out[rows, :] = stage[2 * slot + half, locals_[run]]
     for c in made:
         c.wait()
 
@@ -172,9 +166,10 @@
         + [
             pltpu.VMEM(cache_scale.shape, cache_scale.dtype),
             pltpu.VMEM((4, cache.shape[0], HD), F32),
+            pltpu.VMEM((4, cache.shape[0], BLK, HD), BF16),
             pltpu.SemaphoreType.DMA((5,)),
             pltpu.SemaphoreType.DMA((12,)),
-            pltpu.SemaphoreType.DMA((48,)),
+            pltpu.SemaphoreType.DMA((4,)),
         ],
         compiler_params=pltpu.CompilerParams(vmem_limit_bytes=VMEM_LIMIT),
         cost_estimate=COST,

time: 50.8 us -> 49.6 us (0.976)
  Pallas kernels: 26.2 us -> 25.4 us
    pallas_call x1, Pallas kernels: 4.33 us -> 3.45 us  [gather_call(): pl.pallas_call(gather_kernel, out_shape=[jax.ShapeDtypeStruct((META_SIZE,...]
  transfers between devices with their start and end apart: 15 -> 15, of which waited for: 4 -> 4; matrix products, arithmetic and copies ran while one was open for 0% -> 0% of each run, Pallas kernels for 40% -> 41%
where the time goes in v5:
time: 49.6 us; the launch traced here: 49.3 us
  Pallas kernels  25.4 us (51%)
  starting transfers between devices  16.5 us (33%)
  waiting for transfers between devices  7.07 us (14%)
    ppermute x15, starting transfers between devices, permute(): return lax.ppermute(x, axis, [(i, i ^ k) for i in range(count)])  16.5 us
    pallas_call x6, Pallas kernels, add_call(): pl.pallas_call(functools.partial(add_kernel, slots, ks, early is not None...  16.2 us
    ppermute x15, waiting for transfers between devices, permute(): return lax.ppermute(x, axis, [(i, i ^ k) for i in range(count)])  7.07 us
    pallas_call x1, Pallas kernels, own_call(): pl.pallas_call(own_kernel, out_shape=state_shapes(2), in_specs=[IN_SMEM]...  3.47 us
    pallas_call x1, Pallas kernels, gather_call(): pl.pallas_call(gather_kernel, out_shape=[jax.ShapeDtypeStruct((META_SIZE,...  3.45 us
    pallas_call x1, Pallas kernels, join_call(): pl.pallas_call(join_kernel, out_shape=jax.ShapeDtypeStruct((ROWS, QH * HD...  1.66 us
  transfers between devices with their start and end apart: 15, of which 4 were waited for; matrix products, arithmetic and copies ran while one was open for 0% of the time, Pallas kernels for 41%

profile of v5, /device:TPU:9, one launch (start us, length us, event | category | flops | bytes accessed | tf_op | source)
XLA Modules:
  0.0 49.3 jit_solution(14716550362839881301)
XLA Ops:
  0.1 3.4 %shard_map.82 = (s32[24]{0:T(128)S(1)}, bf16[2,128,1280]{2,1,0:T(8,128)(2,1)S(1)}, bf16[528,128]{1,0:T(8,128)(2,1)S(1)}, bf16[528,128]{1,0:T(8,128)(2,1)S(1)}, b...) custom-call(s32[2]{0:T(128)S(1)} %pad_add_fusion.ids, ...), custom_call_target="tpu_custom_call" | custom-call | flops 1024 | bytes 1024 | tf_op jit(solution)/shard_map/pallas_call | solution.py:154
  3.5 0.7 %collective-permute-start = (bf16[2,128,1280]{2,1,0:T(8,128)(2,1)S(1)}, bf16[2,128,1280]{2,1,0:T(8,128)(2,1)S(1)}, u32[]{:S(2)}, u32[]{:S(2)}) collective-permute-start(bf16[2,128,1280]{2,1,0:T(8,128)(2,1)S(1)} %get-tuple-element.46), channel_id=1, source_target_pairs={{0,1},{1,0},{2,3},{3,2},{4,5},{5,4},{6,7},{7,6},{8,9},{9,8},{10,11... | collective-permute-start | bytes 1966088 | tf_op jit(solution)/shard_map/ppermute | solution.py:443
  4.3 1.2 %collective-permute-start.3 = (bf16[2,528,128]{2,1,0:T(8,128)(2,1)S(1)}, bf16[2,528,128]{2,1,0:T(8,128)(2,1)S(1)}, u32[]{:S(2)}, u32[]{:S(2)}) collective-permute-start(bf16[2,528,128]{2,1,0:T(8,128)(2,1)S(1)} %get-tuple-element.61), channel_id=1, source_target_pairs={{0,4},{4,0},{8,12},{12,8},{16,20},{20,16},{24,28},{28,24},{1,5},{5... | collective-permute-start | bytes 811016 | tf_op jit(solution)/shard_map/ppermute | solution.py:443
  6.0 0.6 %shard_map.83 = (bf16[2,2,256,128]{3,2,1,0:T(8,128)(2,1)S(1)}, bf16[2,256,2048]{2,1,0:T(8,128)(2,1)S(1)}) custom-call(bf16[2,128,1280]{2,1,0:T(8,128)(2,1)S(1)} %collective-permute-done.swap, bf16[2,128,1024]{2,1,0:T(8,128)(2,1)S(1)} %get-tuple-element.47.own_q, bf16[2,256,128]{2,1,0:T(8,128)(2,1)S(1)} %get-tuple-element.48.own_kv), custom_call_target="tpu_custom_call" | custom-call | flops 1024 | bytes 1024 | tf_op jit(solution)/shard_map/pallas_call | solution.py:315
  6.6 1.3 %collective-permute-start.5 = (bf16[2,2,256,128]{3,2,1,0:T(8,128)(2,1)S(1)}, bf16[2,2,256,128]{3,2,1,0:T(8,128)(2,1)S(1)}, u32[]{:S(2)}, u32[]{:S(2)}) collective-permute-start(bf16[2,2,256,128]{3,2,1,0:T(8,128)(2,1)S(1)} %get-tuple-element.55.kv), channel_id=1, source_target_pairs={{0,2},{1,3},{2,0},{3,1},{4,6},{5,7},{6,4},{7,5},{8,10},{9,11},{10,... | collective-permute-start | bytes 786440 | tf_op jit(solution)/shard_map/ppermute | solution.py:443
  7.9 2.3 %collective-permute-start.1 = (bf16[528,128]{1,0:T(8,128)(2,1)S(1)}, bf16[528,128]{1,0:T(8,128)(2,1)S(1)}, u32[]{:S(2)}, u32[]{:S(2)}) collective-permute-start(bf16[528,128]{1,0:T(8,128)(2,1)S(1)} %get-tuple-element.52), channel_id=1, source_target_pairs={{0,16},{4,20},{8,24},{12,28},{16,0},{20,4},{24,8},{28,12},{1,17},{... | collective-permute-start | bytes 405512 | tf_op jit(solution)/shard_map/ppermute | solution.py:443
  10.2 1.0 %collective-permute-start.2 = (bf16[528,128]{1,0:T(8,128)(2,1)S(1)}, bf16[528,128]{1,0:T(8,128)(2,1)S(1)}, u32[]{:S(2)}, u32[]{:S(2)}) collective-permute-start(bf16[528,128]{1,0:T(8,128)(2,1)S(1)} %get-tuple-element.53), channel_id=1, source_target_pairs={{0,20},{4,16},{8,28},{12,24},{16,4},{20,0},{24,12},{28,8},{1,21},{... | collective-permute-start | bytes 405512 | tf_op jit(solution)/shard_map/ppermute | solution.py:443
  11.2 3.5 %shard_map.84 = (f32[144,2048]{1,0:T(8,128)S(1)}, f32[144,2048]{1,0:T(8,128)S(1)}) custom-call(s32[24]{0:T(128)S(1)} %get-tuple-element.45.meta, bf16[2,256,2048]{2,1,0:T(8,128)(2,1)S(1)} %get-tuple-element.49.q_all, bf16[2,2,256,128]{3,2,1,0:T(8,128)(2,1)S(1)} %get-tuple-element.55.kv, bf16[2,528,128]{2,1,0:T(8,128)(2,1)S(1)} %get-tuple-element.56.own), custom_call_target="tpu_custom_call" | custom-call | flops 1024 | bytes 1024 | tf_op jit(solution)/shard_map/pallas_call | solution.py:352
  14.7 1.0 %collective-permute-start.8 = (bf16[2,528,128]{2,1,0:T(8,128)(2,1)S(1)}, bf16[2,528,128]{2,1,0:T(8,128)(2,1)S(1)}, u32[]{:S(2)}, u32[]{:S(2)}) collective-permute-start(bf16[2,528,128]{2,1,0:T(8,128)(2,1)S(1)} %get-tuple-element.67), channel_id=1, source_target_pairs={{0,12},{4,8},{8,4},{12,0},{16,28},{20,24},{24,20},{28,16},{1,13},{... | collective-permute-start | bytes 811016 | tf_op jit(solution)/shard_map/ppermute | solution.py:443
  15.7 5.2 %shard_map.85 = (f32[144,2048]{1,0:T(8,128)S(1)}, f32[144,2048]{1,0:T(8,128)S(1)}) custom-call(s32[24]{0:T(128)S(1)} %get-tuple-element.45.meta, bf16[2,256,2048]{2,1,0:T(8,128)(2,1)S(1)} %get-tuple-element.49.q_all, f32[144,2048]{1,0:T(8,128)S(1)} %get-tuple-element.59.refs_0_, f32[144,2048]{1,0:T(8,128)S(1)} %get-tuple-element.60.refs_1_, ...), custom_call_target="tpu_custom_call" | custom-call | flops 1024 | bytes 1024 | tf_op jit(solution)/shard_map/pallas_call | solution.py:402
  20.9 0.4 collective-permute-done.2.refs_2_
  21.3 0.8 %collective-permute-start.6 = (bf16[528,128]{1,0:T(8,128)(2,1)S(1)}, bf16[528,128]{1,0:T(8,128)(2,1)S(1)}, u32[]{:S(2)}, u32[]{:S(2)}) collective-permute-start(bf16[528,128]{1,0:T(8,128)(2,1)S(1)} %get-tuple-element.65), channel_id=1, source_target_pairs={{0,24},{4,28},{8,16},{12,20},{16,8},{20,12},{24,0},{28,4},{1,25},{... | collective-permute-start | bytes 405512 | tf_op jit(solution)/shard_map/ppermute | solution.py:443
  22.1 1.8 %collective-permute-start.7 = (bf16[528,128]{1,0:T(8,128)(2,1)S(1)}, bf16[528,128]{1,0:T(8,128)(2,1)S(1)}, u32[]{:S(2)}, u32[]{:S(2)}) collective-permute-start(bf16[528,128]{1,0:T(8,128)(2,1)S(1)} %get-tuple-element.66), channel_id=1, source_target_pairs={{0,28},{4,24},{8,20},{12,16},{16,12},{20,8},{24,4},{28,0},{1,29},{... | collective-permute-start | bytes 405512 | tf_op jit(solution)/shard_map/ppermute | solution.py:443
  24.0 1.4 %collective-permute-start.10 = (bf16[528,128]{1,0:T(8,128)(2,1)S(1)}, bf16[528,128]{1,0:T(8,128)(2,1)S(1)}, u32[]{:S(2)}, u32[]{:S(2)}) collective-permute-start(bf16[528,128]{1,0:T(8,128)(2,1)S(1)} %collective-permute-done.2.refs_2_), channel_id=1, source_target_pairs={{0,2},{1,3},{2,0},{3,1},{4,6},{5,7},{6,4},{7,5},{8,10},{9,11},{10,... | collective-permute-start | bytes 405512 | tf_op jit(solution)/shard_map/ppermute | solution.py:443
  25.4 2.0 %shard_map.86.refs_0_ = f32[144,2048]{1,0:T(8,128)S(1)} custom-call(s32[24]{0:T(128)S(1)} %get-tuple-element.45.meta, bf16[2,256,2048]{2,1,0:T(8,128)(2,1)S(1)} %get-tuple-element.49.q_all, f32[144,2048]{1,0:T(8,128)S(1)} %get-tuple-element.68.refs_0_, bf16[528,128]{1,0:T(8,128)(2,1)S(1)} %collective-permute-done.1.refs_1_, ...), custom_call_target="tpu_custom_call" | custom-call | flops 1024 | bytes 1024 | tf_op jit(solution)/shard_map/pallas_call | solution.py:402
  27.4 2.4 %shard_map.87 = (f32[144,2048]{1,0:T(8,128)S(1)}, f32[144,2048]{1,0:T(8,128)S(1)}) custom-call(s32[24]{0:T(128)S(1)} %get-tuple-element.45.meta, bf16[2,256,2048]{2,1,0:T(8,128)(2,1)S(1)} %get-tuple-element.49.q_all, f32[144,2048]{1,0:T(8,128)S(1)} %shard_map.86.refs_0_, f32[144,2048]{1,0:T(8,128)S(1)} %get-tuple-element.73.refs_1_, ...), custom_call_target="tpu_custom_call" | custom-call | flops 1024 | bytes 1024 | tf_op jit(solution)/shard_map/pallas_call | solution.py:402
  29.8 4.8 %collective-permute-done.7.refs_2_ = bf16[528,128]{1,0:T(8,128)(2,1)S(1)} collective-permute-done((bf16[528,128]{1,0:T(8,128)(2,1)S(1)}, bf16[528,128]{1,0:T(8,128)(2,1)S(1)}, u32[]{:S(2)}, u32[]{:S(2)}) %collective-permute-start.7) | collective-permute-done | bytes 135200 | tf_op jit(solution)/shard_map/ppermute | solution.py:443
  34.6 1.5 %collective-permute-start.12 = (bf16[528,128]{1,0:T(8,128)(2,1)S(1)}, bf16[528,128]{1,0:T(8,128)(2,1)S(1)}, u32[]{:S(2)}, u32[]{:S(2)}) collective-permute-start(bf16[528,128]{1,0:T(8,128)(2,1)S(1)} %collective-permute-done.7.refs_2_), channel_id=1, source_target_pairs={{0,2},{1,3},{2,0},{3,1},{4,6},{5,7},{6,4},{7,5},{8,10},{9,11},{10,... | collective-permute-start | bytes 405512 | tf_op jit(solution)/shard_map/ppermute | solution.py:443
  36.1 2.4 %shard_map.88 = (bf16[128,1024]{1,0:T(8,128)(2,1)S(1)}, bf16[128,1024]{1,0:T(8,128)(2,1)S(1)}) custom-call(s32[24]{0:T(128)S(1)} %get-tuple-element.45.meta, bf16[2,256,2048]{2,1,0:T(8,128)(2,1)S(1)} %get-tuple-element.49.q_all, f32[144,2048]{1,0:T(8,128)S(1)} %get-tuple-element.77.refs_0_, bf16[528,128]{1,0:T(8,128)(2,1)S(1)} %collective-permute-done.6.refs_1_, ...), custom_call_target="tpu_custom_call" | custom-call | flops 1024 | bytes 1024 | tf_op jit(solution)/shard_map/pallas_call | solution.py:402
  38.5 3.1 %collective-permute-start.13 = (bf16[128,1024]{1,0:T(8,128)(2,1)S(1)}, bf16[128,1024]{1,0:T(8,128)(2,1)S(1)}, u32[]{:S(2)}, u32[]{:S(2)}) collective-permute-start(bf16[128,1024]{1,0:T(8,128)(2,1)S(1)} %get-tuple-element.83), channel_id=1, source_target_pairs={{0,1},{1,0},{2,3},{3,2},{4,5},{5,4},{6,7},{7,6},{8,9},{9,8},{10,11... | collective-permute-start | bytes 786440 | tf_op jit(solution)/shard_map/ppermute | solution.py:443
  41.6 2.0 %shard_map.89.refs_0_ = f32[144,2048]{1,0:T(8,128)S(1)} custom-call(s32[24]{0:T(128)S(1)} %get-tuple-element.45.meta, bf16[2,256,2048]{2,1,0:T(8,128)(2,1)S(1)} %get-tuple-element.49.q_all, f32[144,2048]{1,0:T(8,128)S(1)} %get-tuple-element.81.refs_0_, bf16[528,128]{1,0:T(8,128)(2,1)S(1)} %collective-permute-done.9.refs_1_, ...), custom_call_target="tpu_custom_call" | custom-call | flops 1024 | bytes 1024 | tf_op jit(solution)/shard_map/pallas_call | solution.py:402
  43.7 2.2 %shard_map.90 = (bf16[128,1024]{1,0:T(8,128)(2,1)S(1)}, bf16[128,1024]{1,0:T(8,128)(2,1)S(1)}) custom-call(s32[24]{0:T(128)S(1)} %get-tuple-element.45.meta, bf16[2,256,2048]{2,1,0:T(8,128)(2,1)S(1)} %get-tuple-element.49.q_all, f32[144,2048]{1,0:T(8,128)S(1)} %shard_map.89.refs_0_, bf16[528,128]{1,0:T(8,128)(2,1)S(1)} %collective-permute-done.11.refs_1_, ...), custom_call_target="tpu_custom_call" | custom-call | flops 1024 | bytes 1024 | tf_op jit(solution)/shard_map/pallas_call | solution.py:402
  46.0 1.5 %collective-permute-done.14.refs_3_ = bf16[128,1024]{1,0:T(8,128)(2,1)S(1)} collective-permute-done((bf16[128,1024]{1,0:T(8,128)(2,1)S(1)}, bf16[128,1024]{1,0:T(8,128)(2,1)S(1)}, u32[]{:S(2)}, u32[]{:S(2)}) %collective-permute-start.14) | collective-permute-done | bytes 262176 | tf_op jit(solution)/shard_map/ppermute | solution.py:443
  47.5 1.7 %shard_map.91 = bf16[128,4096]{1,0:T(8,128)(2,1)} custom-call(s32[24]{0:T(128)} %copy-done, bf16[128,1024]{1,0:T(8,128)(2,1)S(1)} %get-tuple-element.80.refs_0_, bf16[128,1024]{1,0:T(8,128)(2,1)S(1)} %get-tuple-element.82.refs_1_, bf16[128,1024]{1,0:T(8,128)(2,1)S(1)} %collective-permute-done.13.refs_2_, bf16[128,1024]{1,0:T(8,128)(2,1)S(1)} %collective-permute-done.14.refs_3_), custom_call_target="tpu_custom_call" | custom-call | flops 1024 | bytes 1024 | tf_op jit(solution)/shard_map/pallas_call | solution.py:432
  (19 shorter events, 0.8 us)
Async XLA Ops:
  3.5 40.1 %copy-start = (s32[24]{0:T(128)}, s32[24]{0:T(128)S(1)}, u32[]{:S(2)}) copy-start(s32[24]{0:T(128)S(1)} %get-tuple-element.45.meta) | copy-start | bytes 292
  3.5 2.5 %collective-permute-start = (bf16[2,128,1280]{2,1,0:T(8,128)(2,1)S(1)}, bf16[2,128,1280]{2,1,0:T(8,128)(2,1)S(1)}, u32[]{:S(2)}, u32[]{:S(2)}) collective-permute-start(bf16[2,128,1280]{2,1,0:T(8,128)(2,1)S(1)} %get-tuple-element.46), channel_id=1, source_target_pairs={{0,1},{1,0},{2,3},{3,2},{4,5},{5,4},{6,7},{7,6},{8,9},{9,8},{10,11... | collective-permute-start | bytes 1966088 | tf_op jit(solution)/shard_map/ppermute | solution.py:443
  4.3 10.4 %collective-permute-start.3 = (bf16[2,528,128]{2,1,0:T(8,128)(2,1)S(1)}, bf16[2,528,128]{2,1,0:T(8,128)(2,1)S(1)}, u32[]{:S(2)}, u32[]{:S(2)}) collective-permute-start(bf16[2,528,128]{2,1,0:T(8,128)(2,1)S(1)} %get-tuple-element.61), channel_id=1, source_target_pairs={{0,4},{4,0},{8,12},{12,8},{16,20},{20,16},{24,28},{28,24},{1,5},{5... | collective-permute-start | bytes 811016 | tf_op jit(solution)/shard_map/ppermute | solution.py:443
  5.5 10.2 %collective-permute-start.4 = (bf16[2,528,128]{2,1,0:T(8,128)(2,1)S(1)}, bf16[2,528,128]{2,1,0:T(8,128)(2,1)S(1)}, u32[]{:S(2)}, u32[]{:S(2)}) collective-permute-start(bf16[2,528,128]{2,1,0:T(8,128)(2,1)S(1)} %get-tuple-element.62), channel_id=1, source_target_pairs={{0,8},{4,12},{8,0},{12,4},{16,24},{20,28},{24,16},{28,20},{1,9},{5... | collective-permute-start | bytes 811016 | tf_op jit(solution)/shard_map/ppermute | solution.py:443
  6.6 9.1 %collective-permute-start.5 = (bf16[2,2,256,128]{3,2,1,0:T(8,128)(2,1)S(1)}, bf16[2,2,256,128]{3,2,1,0:T(8,128)(2,1)S(1)}, u32[]{:S(2)}, u32[]{:S(2)}) collective-permute-start(bf16[2,2,256,128]{3,2,1,0:T(8,128)(2,1)S(1)} %get-tuple-element.55.kv), channel_id=1, source_target_pairs={{0,2},{1,3},{2,0},{3,1},{4,6},{5,7},{6,4},{7,5},{8,10},{9,11},{10,... | collective-permute-start | bytes 786440 | tf_op jit(solution)/shard_map/ppermute | solution.py:443
  7.9 13.0 %collective-permute-start.1 = (bf16[528,128]{1,0:T(8,128)(2,1)S(1)}, bf16[528,128]{1,0:T(8,128)(2,1)S(1)}, u32[]{:S(2)}, u32[]{:S(2)}) collective-permute-start(bf16[528,128]{1,0:T(8,128)(2,1)S(1)} %get-tuple-element.52), channel_id=1, source_target_pairs={{0,16},{4,20},{8,24},{12,28},{16,0},{20,4},{24,8},{28,12},{1,17},{... | collective-permute-start | bytes 405512 | tf_op jit(solution)/shard_map/ppermute | solution.py:443
  10.2 11.1 %collective-permute-start.2 = (bf16[528,128]{1,0:T(8,128)(2,1)S(1)}, bf16[528,128]{1,0:T(8,128)(2,1)S(1)}, u32[]{:S(2)}, u32[]{:S(2)}) collective-permute-start(bf16[528,128]{1,0:T(8,128)(2,1)S(1)} %get-tuple-element.53), channel_id=1, source_target_pairs={{0,20},{4,16},{8,28},{12,24},{16,4},{20,0},{24,12},{28,8},{1,21},{... | collective-permute-start | bytes 405512 | tf_op jit(solution)/shard_map/ppermute | solution.py:443
  14.7 12.7 %collective-permute-start.8 = (bf16[2,528,128]{2,1,0:T(8,128)(2,1)S(1)}, bf16[2,528,128]{2,1,0:T(8,128)(2,1)S(1)}, u32[]{:S(2)}, u32[]{:S(2)}) collective-permute-start(bf16[2,528,128]{2,1,0:T(8,128)(2,1)S(1)} %get-tuple-element.67), channel_id=1, source_target_pairs={{0,12},{4,8},{8,4},{12,0},{16,28},{20,24},{24,20},{28,16},{1,13},{... | collective-permute-start | bytes 811016 | tf_op jit(solution)/shard_map/ppermute | solution.py:443
  21.3 8.5 %collective-permute-start.6 = (bf16[528,128]{1,0:T(8,128)(2,1)S(1)}, bf16[528,128]{1,0:T(8,128)(2,1)S(1)}, u32[]{:S(2)}, u32[]{:S(2)}) collective-permute-start(bf16[528,128]{1,0:T(8,128)(2,1)S(1)} %get-tuple-element.65), channel_id=1, source_target_pairs={{0,24},{4,28},{8,16},{12,20},{16,8},{20,12},{24,0},{28,4},{1,25},{... | collective-permute-start | bytes 405512 | tf_op jit(solution)/shard_map/ppermute | solution.py:443
  22.1 12.5 %collective-permute-start.7 = (bf16[528,128]{1,0:T(8,128)(2,1)S(1)}, bf16[528,128]{1,0:T(8,128)(2,1)S(1)}, u32[]{:S(2)}, u32[]{:S(2)}) collective-permute-start(bf16[528,128]{1,0:T(8,128)(2,1)S(1)} %get-tuple-element.66), channel_id=1, source_target_pairs={{0,28},{4,24},{8,20},{12,16},{16,12},{20,8},{24,4},{28,0},{1,29},{... | collective-permute-start | bytes 405512 | tf_op jit(solution)/shard_map/ppermute | solution.py:443
  23.9 17.7 %collective-permute-start.9 = (bf16[528,128]{1,0:T(8,128)(2,1)S(1)}, bf16[528,128]{1,0:T(8,128)(2,1)S(1)}, u32[]{:S(2)}, u32[]{:S(2)}) collective-permute-start(bf16[528,128]{1,0:T(8,128)(2,1)S(1)} %collective-permute-done.1.refs_1_), channel_id=1, source_target_pairs={{0,2},{1,3},{2,0},{3,1},{4,6},{5,7},{6,4},{7,5},{8,10},{9,11},{10,... | collective-permute-start | bytes 405512 | tf_op jit(solution)/shard_map/ppermute | solution.py:443
  24.0 17.7 %collective-permute-start.10 = (bf16[528,128]{1,0:T(8,128)(2,1)S(1)}, bf16[528,128]{1,0:T(8,128)(2,1)S(1)}, u32[]{:S(2)}, u32[]{:S(2)}) collective-permute-start(bf16[528,128]{1,0:T(8,128)(2,1)S(1)} %collective-permute-done.2.refs_2_), channel_id=1, source_target_pairs={{0,2},{1,3},{2,0},{3,1},{4,6},{5,7},{6,4},{7,5},{8,10},{9,11},{10,... | collective-permute-start | bytes 405512 | tf_op jit(solution)/shard_map/ppermute | solution.py:443
  34.6 9.0 %collective-permute-start.11 = (bf16[528,128]{1,0:T(8,128)(2,1)S(1)}, bf16[528,128]{1,0:T(8,128)(2,1)S(1)}, u32[]{:S(2)}, u32[]{:S(2)}) collective-permute-start(bf16[528,128]{1,0:T(8,128)(2,1)S(1)} %collective-permute-done.6.refs_1_), channel_id=1, source_target_pairs={{0,2},{1,3},{2,0},{3,1},{4,6},{5,7},{6,4},{7,5},{8,10},{9,11},{10,... | collective-permute-start | bytes 405512 | tf_op jit(solution)/shard_map/ppermute | solution.py:443
  34.6 9.0 %collective-permute-start.12 = (bf16[528,128]{1,0:T(8,128)(2,1)S(1)}, bf16[528,128]{1,0:T(8,128)(2,1)S(1)}, u32[]{:S(2)}, u32[]{:S(2)}) collective-permute-start(bf16[528,128]{1,0:T(8,128)(2,1)S(1)} %collective-permute-done.7.refs_2_), channel_id=1, source_target_pairs={{0,2},{1,3},{2,0},{3,1},{4,6},{5,7},{6,4},{7,5},{8,10},{9,11},{10,... | collective-permute-start | bytes 405512 | tf_op jit(solution)/shard_map/ppermute | solution.py:443
  38.5 7.5 %collective-permute-start.13 = (bf16[128,1024]{1,0:T(8,128)(2,1)S(1)}, bf16[128,1024]{1,0:T(8,128)(2,1)S(1)}, u32[]{:S(2)}, u32[]{:S(2)}) collective-permute-start(bf16[128,1024]{1,0:T(8,128)(2,1)S(1)} %get-tuple-element.83), channel_id=1, source_target_pairs={{0,1},{1,0},{2,3},{3,2},{4,5},{5,4},{6,7},{7,6},{8,9},{9,8},{10,11... | collective-permute-start | bytes 786440 | tf_op jit(solution)/shard_map/ppermute | solution.py:443
  45.9 1.6 %collective-permute-start.14 = (bf16[128,1024]{1,0:T(8,128)(2,1)S(1)}, bf16[128,1024]{1,0:T(8,128)(2,1)S(1)}, u32[]{:S(2)}, u32[]{:S(2)}) collective-permute-start(bf16[128,1024]{1,0:T(8,128)(2,1)S(1)} %get-tuple-element.84), channel_id=1, source_target_pairs={{0,1},{1,0},{2,3},{3,2},{4,5},{5,4},{6,7},{7,6},{8,9},{9,8},{10,11... | collective-permute-start | bytes 786440 | tf_op jit(solution)/shard_map/ppermute | solution.py:443
